TPU v7x, 32 devices: a whole 2x2x4 slice. The times are simulated.
32 devices in a mesh: blk: 8 (over y, x, core), group: 4 (over z).
Axes of the slice: x: 2, y: 2, z: 4, core: 2. Of those that a mesh axis runs over, the one named last changes fastest.
Arguments:
- codes: bfloat16 [16384, 1024], P(('blk', 'group')), may hold values from -6 to 6
- row_scale: bfloat16 [16384], P(('blk', 'group')), may hold values from 0.3 to 3
- row_group: int32 [16384, 1], P(('blk', 'group')), may hold values from 0 to 3; in each aligned block of 512 rows (0 to 511, 512 to 1023, ...) at most 192 rows name the same one
- row_sub: int32 [16384], P(('blk', 'group')), may hold values from 0 to 1
- centroids: bfloat16 [8, 1024], P('group'), may hold values from -6 to 6
Outputs:
- best_sim: float32 [16384], P(('blk', 'group'))
Inputs may be any that keep to these rules, and one draw needn't show every extreme that they name: `row_group`: among the rows of one device no cluster group is named by more than 192 rows, and in every draw some device has a group named by exactly 192 of its rows.
All inputs are finite; a program needn't handle non-finite values.
Results may differ from a plain program's by a relative error of at most 0.0003.
Values may be sent and summed in bfloat16 or wider, within the bound.
No kernel may reach another device: no remote copies, remote signals or barrier semaphores. Data moves between devices by JAX's collectives and lax.ppermute only.
A program may use at most 128 MiB of HBM per device.

v0:
```python
import jax
import jax.numpy as jnp
from jax import lax
from jax.sharding import PartitionSpec as P


def for_sending(shard):
    return jax.tree.map(lambda a: a.astype(jnp.bfloat16) if a.dtype == jnp.float32 else a, shard)


def compare(best_sim, own_rows, own_order, own_sub, key_rows, key_order, key_sub):
    scores = jnp.einsum("qd,kd->qk", own_rows, key_rows, preferred_element_type=jnp.float32)
    allowed = (
        (key_sub[None, :] == own_sub[:, None])
        & (key_order[None, :] < own_order[:, None])
        & (key_order[None, :] > 0)
    )
    return jnp.maximum(best_sim, jnp.max(jnp.where(allowed, scores, -1.0), axis=1))


def shards(codes, row_scale, row_group, row_sub, centroids):
    row_count, width = codes.shape
    groups = lax.axis_size("group")
    capacity = 3 * row_count // (2 * groups)
    slot_count = groups * capacity
    cycle_pos = lax.axis_index("blk")
    group_pos = lax.axis_index("group")
    target = row_group[:, 0]
    member = (target[:, None] == jnp.arange(groups, dtype=jnp.int32)[None, :]).astype(jnp.int32)
    slot_rank = jnp.sum((jnp.cumsum(member, axis=0) - 1) * member, axis=1)
    placed = target * capacity + slot_rank
    row_order = (
        (cycle_pos * groups + group_pos) * row_count + jnp.arange(row_count, dtype=jnp.int32) + 1
    )
    send_codes = (
        jnp.zeros((slot_count, width), jnp.bfloat16)
        .at[placed]
        .set(codes)
        .reshape(groups, capacity, width)
    )
    send_scale = (
        jnp.zeros((slot_count,), jnp.bfloat16).at[placed].set(row_scale).reshape(groups, capacity)
    )
    send_sub = jnp.zeros((slot_count,), jnp.int32).at[placed].set(row_sub).reshape(groups, capacity)
    send_order = (
        jnp.zeros((slot_count,), jnp.int32).at[placed].set(row_order).reshape(groups, capacity)
    )
    centroid_count = centroids.shape[0]
    part_codes = lax.all_to_all(send_codes, "group", split_axis=0, concat_axis=0, tiled=True)
    part_scale = lax.all_to_all(send_scale, "group", split_axis=0, concat_axis=0, tiled=True)
    part_sub = lax.all_to_all(send_sub, "group", split_axis=0, concat_axis=0, tiled=True)
    part_order = lax.all_to_all(send_order, "group", split_axis=0, concat_axis=0, tiled=True)
    picks = (part_sub[..., None] == jnp.arange(centroid_count, dtype=jnp.int32)).astype(
        jnp.bfloat16
    )
    centre = jnp.einsum("gnc,cd->gnd", picks, centroids, preferred_element_type=jnp.float32)
    vectors = centre + part_scale.astype(jnp.float32)[..., None] * part_codes.astype(jnp.float32)
    unit_part = (
        vectors / jnp.sqrt(jnp.sum(vectors * vectors, axis=-1, keepdims=True) + 1e-06)
    ).astype(jnp.bfloat16)
    own_rows = unit_part.reshape(slot_count, width)
    own_order = part_order.reshape(slot_count)
    own_sub = part_sub.reshape(slot_count)
    start_sim = jnp.full((slot_count,), -1.0, jnp.float32)
    piece_rows = lax.all_gather(own_rows, "blk", axis=0, tiled=True)
    piece_order = lax.all_gather(for_sending(own_order), "blk", axis=0, tiled=True)
    piece_sub = lax.all_gather(for_sending(own_sub), "blk", axis=0, tiled=True)
    shard_count = piece_rows.shape[0] // slot_count
    stacked = (
        piece_rows.reshape(shard_count, slot_count, width),
        piece_order.reshape(shard_count, slot_count),
        piece_sub.reshape(shard_count, slot_count),
        jnp.arange(shard_count, dtype=jnp.int32),
    )

    def per_shard(carry, item):
        shard_rows, shard_order, shard_sub, source = item
        carry = compare(carry, own_rows, own_order, own_sub, shard_rows, shard_order, shard_sub)
        return (carry, None)

    best_sim = lax.scan(per_shard, start_sim, stacked)[0]
    returned = lax.all_to_all(
        best_sim.reshape(groups, capacity), "group", split_axis=0, concat_axis=0, tiled=True
    )
    return returned.reshape(-1)[placed]


def solution(mesh):
    return jax.shard_map(
        shards,
        mesh=mesh,
        in_specs=(
            P(("blk", "group"), None),
            P(("blk", "group")),
            P(("blk", "group"), None),
            P(("blk", "group")),
            P("group", None),
        ),
        out_specs=P(("blk", "group")),
        check_vma=False,
    )
```

profile of v0, /device:TPU:0, one launch (start us, length us, event | category | flops | bytes accessed | tf_op | source)
XLA Modules:
  0.0 199.2 jit_solution(477196664060088286)
XLA Ops:
  6.5 0.7 fusion.11
  7.2 1.2 reduce-window.6
  8.9 0.7 fusion.9
  9.6 0.7 compare_select_fusion
  10.3 3.9 %scatter_custom_fusion.2 = bf16[768]{0:T(1024)(128)(2,1)S(1)} fusion(s32[512]{0:T(512)S(1)} %bitcast.72, bf16[512]{0:T(512)(128)(2,1)} %param.8, bf16[]{:T(256)} %constant.15.clone.1), kind=kCustom, calls=%fused_computation.45 | custom fusion | bytes 2048 | tf_op jit(solution)/shard_map/scatter | solution.py:42
  14.9 6.3 %all-to-all-start.2 = ((bf16[4,1,192]{2,1,0:T(2,128)(2,1)}), bf16[4,1,192]{2,1,0:T(2,128)(2,1)S(1)}, u32[]{:S(2)}, u32[]{:S(2)}) async-start(bf16[4,1,192]{2,1,0:T(2,128)(2,1)} %all_to_all.39), calls=%async_computation.2 | async-start | bytes 8192 | tf_op jit(solution)/shard_map/all_to_all | solution.py:50
  21.2 2.6 %scatter_custom_fusion = s32[768]{0:T(1024)S(1)} fusion(s32[512]{0:T(512)S(1)} %bitcast.73, s32[512]{0:T(512)} %param.10, s32[]{:T(128)} %constant.11.clone.1), kind=kCustom, calls=%fused_computation.43 | custom fusion | bytes 3584 | tf_op jit(solution)/shard_map/scatter | solution.py:44
  24.5 2.3 %all-to-all-done.2 = bf16[4,1,192]{2,1,0:T(2,128)(2,1)S(1)} async-done(((bf16[4,1,192]{2,1,0:T(2,128)(2,1)}), bf16[4,1,192]{2,1,0:T(2,128)(2,1)S(1)}, u32[]{:S(2)}, u32[]{:S(2)}) %all-to-all-start.2) | async-done | bytes 1568 | tf_op jit(solution)/shard_map/all_to_all | solution.py:50
  26.8 3.2 %all-to-all-start = ((s32[4,1,192]{2,1,0:T(1,128)}), s32[4,1,192]{2,1,0:T(1,128)S(1)}, u32[]{:S(2)}, u32[]{:S(2)}) async-start(s32[4,1,192]{2,1,0:T(1,128)} %all_to_all.29), calls=%async_computation | async-start | bytes 8192 | tf_op jit(solution)/shard_map/all_to_all | solution.py:51
  30.1 4.5 %scatter_custom_fusion.3 = bf16[768,1024]{1,0:T(8,128)(2,1)} fusion(s32[512]{0:T(512)S(1)} %bitcast.74, bf16[512,1024]{1,0:T(8,128)(2,1)} %param.7, bf16[]{:T(256)} %constant.15.clone.1), kind=kCustom, calls=%fused_computation.17 | custom fusion | bytes 1573376 | tf_op jit(solution)/shard_map/scatter | solution.py:38
  34.6 0.9 all-to-all-done
  35.4 4.2 %all-to-all-start.3 = ((bf16[4,192,1024]{2,1,0:T(8,128)(2,1)}), bf16[4,192,1024]{2,1,0:T(8,128)(2,1)S(1)}, u32[]{:S(2)}, u32[]{:S(2)}) async-start(bf16[4,192,1024]{2,1,0:T(8,128)(2,1)} %bitcast.6), calls=%async_computation.3 | async-start | bytes 3145728 | tf_op jit(solution)/shard_map/all_to_all | solution.py:49
  39.7 35.4 %all-to-all-done.3 = bf16[4,192,1024]{2,1,0:T(8,128)(2,1)S(1)} async-done(((bf16[4,192,1024]{2,1,0:T(8,128)(2,1)}), bf16[4,192,1024]{2,1,0:T(8,128)(2,1)S(1)}, u32[]{:S(2)}, u32[]{:S(2)}) %all-to-all-start.3) | async-done | bytes 1572896 | tf_op jit(solution)/shard_map/all_to_all | solution.py:49
  75.1 1.2 multiply_reduce_fusion
  76.2 1.8 divide_convert_fusion
  78.0 2.4 %scatter_custom_fusion.1 = s32[768]{0:T(1024)S(1)} fusion(s32[512]{0:T(512)S(1)} %bitcast.75, s32[512]{0:T(512)S(1)} %add_add_fusion, s32[]{:T(128)} %constant.11.clone.1), kind=kCustom, calls=%fused_computation.41 | custom fusion | bytes 3076 | tf_op jit(solution)/shard_map/scatter | solution.py:46
  81.2 3.2 %all-to-all-start.1 = ((s32[4,1,192]{2,1,0:T(1,128)}), s32[4,1,192]{2,1,0:T(1,128)S(1)}, u32[]{:S(2)}, u32[]{:S(2)}) async-start(s32[4,1,192]{2,1,0:T(1,128)} %all_to_all.31), calls=%async_computation.1 | async-start | bytes 8192 | tf_op jit(solution)/shard_map/all_to_all | solution.py:52
  84.6 9.0 %all-gather = s32[8,1,768]{2,1,0:T(1,128)S(1)} all-gather(s32[1,1,768]{2,1,0:T(1,128)S(1)} %reshape.129), channel_id=1, replica_groups=mesh['blk'=8,'group'=4] {'blk'}, dimensions={0}, use_global_device_ids=true | all-gather | bytes 27648 | tf_op jit(solution)/shard_map/all_gather | solution.py:67
  93.8 9.1 %all-gather.1 = s32[8,1,768]{2,1,0:T(1,128)S(1)} all-gather(s32[1,1,768]{2,1,0:T(1,128)S(1)} %reshape.131), channel_id=1, replica_groups=mesh['blk'=8,'group'=4] {'blk'}, dimensions={0}, use_global_device_ids=true | all-gather | bytes 27648 | tf_op jit(solution)/shard_map/all_gather | solution.py:66
  102.9 46.6 %all-gather.4.cloned.1.call-done = bf16[6144,1024]{1,0:T(8,128)(2,1)} async-done(((bf16[768,1024]{1,0:T(8,128)(2,1)}), bf16[6144,1024]{1,0:T(8,128)(2,1)}) %all-gather.4.cloned.1.call-update) | async-done | bytes 12582928 | tf_op jit(solution)/shard_map/all_gather | solution.py:65
  149.5 28.4 %while.12 = (s32[]{:T(128)}, f32[768]{0:T(1024)S(1)}, s32[8,768]{1,0:T(8,128)S(1)}, s32[4,192]{1,0:T(4,128)}, s32[8,768]{1,0:T(8,128)S(1)}, /*index=5*/s32[4,192...) while((s32[]{:T(128)}, f32[768]{0:T(1024)S(1)}, ...), condition=%wide.wide.region_10.11_spmd.clone, body=%wide.wide.region_8.10_spmd.clone.sunk | while | flops 1211500032 | bytes 3187347 | solution.py:81
  149.6 3.5 %fusion.29 = f32[768]{0:T(1024)S(1)} fusion(bf16[768,1024]{1,0:T(8,128)(2,1)} %get-tuple-element.224, bf16[8,768,1024]{2,1,0:T(8,128)(2,1)} %get-tuple-element.223, s32[]{:T(128)S(6)} %copy.30, s32[768]{0:T(1024)S(1)} %get-tuple-element.225, s32[768]{0:T(1024)S(1)} %get-tuple-element.226, s32[768]{0:T(1024)S(1)} %get-tuple-element.191, ...), kind=kOutput, calls=%fused_computation.6.clone.clone.1 | convolution fusion | flops 1211497728 | bytes 3161860 | tf_op jit(solution)/shard_map/while/body/eval_jaxpr/qd,kd->qk/dot_general | solution.py:12
  153.2 3.5 %fusion.29 = f32[768]{0:T(1024)S(1)} fusion(bf16[768,1024]{1,0:T(8,128)(2,1)} %get-tuple-element.224, bf16[8,768,1024]{2,1,0:T(8,128)(2,1)} %get-tuple-element.223, s32[]{:T(128)S(6)} %copy.30, s32[768]{0:T(1024)S(1)} %get-tuple-element.225, s32[768]{0:T(1024)S(1)} %get-tuple-element.226, s32[768]{0:T(1024)S(1)} %get-tuple-element.191, ...), kind=kOutput, calls=%fused_computation.6.clone.clone.1 | convolution fusion | flops 1211497728 | bytes 3161860 | tf_op jit(solution)/shard_map/while/body/eval_jaxpr/qd,kd->qk/dot_general | solution.py:12
  156.7 3.5 %fusion.29 = f32[768]{0:T(1024)S(1)} fusion(bf16[768,1024]{1,0:T(8,128)(2,1)} %get-tuple-element.224, bf16[8,768,1024]{2,1,0:T(8,128)(2,1)} %get-tuple-element.223, s32[]{:T(128)S(6)} %copy.30, s32[768]{0:T(1024)S(1)} %get-tuple-element.225, s32[768]{0:T(1024)S(1)} %get-tuple-element.226, s32[768]{0:T(1024)S(1)} %get-tuple-element.191, ...), kind=kOutput, calls=%fused_computation.6.clone.clone.1 | convolution fusion | flops 1211497728 | bytes 3161860 | tf_op jit(solution)/shard_map/while/body/eval_jaxpr/qd,kd->qk/dot_general | solution.py:12
  160.3 3.5 %fusion.29 = f32[768]{0:T(1024)S(1)} fusion(bf16[768,1024]{1,0:T(8,128)(2,1)} %get-tuple-element.224, bf16[8,768,1024]{2,1,0:T(8,128)(2,1)} %get-tuple-element.223, s32[]{:T(128)S(6)} %copy.30, s32[768]{0:T(1024)S(1)} %get-tuple-element.225, s32[768]{0:T(1024)S(1)} %get-tuple-element.226, s32[768]{0:T(1024)S(1)} %get-tuple-element.191, ...), kind=kOutput, calls=%fused_computation.6.clone.clone.1 | convolution fusion | flops 1211497728 | bytes 3161860 | tf_op jit(solution)/shard_map/while/body/eval_jaxpr/qd,kd->qk/dot_general | solution.py:12
  163.8 3.5 %fusion.29 = f32[768]{0:T(1024)S(1)} fusion(bf16[768,1024]{1,0:T(8,128)(2,1)} %get-tuple-element.224, bf16[8,768,1024]{2,1,0:T(8,128)(2,1)} %get-tuple-element.223, s32[]{:T(128)S(6)} %copy.30, s32[768]{0:T(1024)S(1)} %get-tuple-element.225, s32[768]{0:T(1024)S(1)} %get-tuple-element.226, s32[768]{0:T(1024)S(1)} %get-tuple-element.191, ...), kind=kOutput, calls=%fused_computation.6.clone.clone.1 | convolution fusion | flops 1211497728 | bytes 3161860 | tf_op jit(solution)/shard_map/while/body/eval_jaxpr/qd,kd->qk/dot_general | solution.py:12
  167.4 3.5 %fusion.29 = f32[768]{0:T(1024)S(1)} fusion(bf16[768,1024]{1,0:T(8,128)(2,1)} %get-tuple-element.224, bf16[8,768,1024]{2,1,0:T(8,128)(2,1)} %get-tuple-element.223, s32[]{:T(128)S(6)} %copy.30, s32[768]{0:T(1024)S(1)} %get-tuple-element.225, s32[768]{0:T(1024)S(1)} %get-tuple-element.226, s32[768]{0:T(1024)S(1)} %get-tuple-element.191, ...), kind=kOutput, calls=%fused_computation.6.clone.clone.1 | convolution fusion | flops 1211497728 | bytes 3161860 | tf_op jit(solution)/shard_map/while/body/eval_jaxpr/qd,kd->qk/dot_general | solution.py:12
  170.9 3.5 %fusion.29 = f32[768]{0:T(1024)S(1)} fusion(bf16[768,1024]{1,0:T(8,128)(2,1)} %get-tuple-element.224, bf16[8,768,1024]{2,1,0:T(8,128)(2,1)} %get-tuple-element.223, s32[]{:T(128)S(6)} %copy.30, s32[768]{0:T(1024)S(1)} %get-tuple-element.225, s32[768]{0:T(1024)S(1)} %get-tuple-element.226, s32[768]{0:T(1024)S(1)} %get-tuple-element.191, ...), kind=kOutput, calls=%fused_computation.6.clone.clone.1 | convolution fusion | flops 1211497728 | bytes 3161860 | tf_op jit(solution)/shard_map/while/body/eval_jaxpr/qd,kd->qk/dot_general | solution.py:12
  174.5 3.5 %fusion.29 = f32[768]{0:T(1024)S(1)} fusion(bf16[768,1024]{1,0:T(8,128)(2,1)} %get-tuple-element.224, bf16[8,768,1024]{2,1,0:T(8,128)(2,1)} %get-tuple-element.223, s32[]{:T(128)S(6)} %copy.30, s32[768]{0:T(1024)S(1)} %get-tuple-element.225, s32[768]{0:T(1024)S(1)} %get-tuple-element.226, s32[768]{0:T(1024)S(1)} %get-tuple-element.191, ...), kind=kOutput, calls=%fused_computation.6.clone.clone.1 | convolution fusion | flops 1211497728 | bytes 3161860 | tf_op jit(solution)/shard_map/while/body/eval_jaxpr/qd,kd->qk/dot_general | solution.py:12
  178.6 4.6 %all-to-all-start.4 = ((f32[4,1,192]{2,1,0:T(1,128)}), f32[4,1,192]{2,1,0:T(1,128)S(1)}, u32[]{:S(2)}, u32[]{:S(2)}) async-start(f32[4,1,192]{2,1,0:T(1,128)} %all_to_all.37), calls=%async_computation.4 | async-start | bytes 8192 | tf_op jit(solution)/shard_map/all_to_all | solution.py:82
  183.2 5.6 %all-to-all-done.4 = f32[4,1,192]{2,1,0:T(1,128)S(1)} async-done(((f32[4,1,192]{2,1,0:T(1,128)}), f32[4,1,192]{2,1,0:T(1,128)S(1)}, u32[]{:S(2)}, u32[]{:S(2)}) %all-to-all-start.4) | async-done | bytes 3104 | tf_op jit(solution)/shard_map/all_to_all | solution.py:82
  188.9 3.4 %gather_fusion = f32[512]{0:T(512)} fusion(f32[768]{0:T(1024)S(1)} %reshape.87, s32[1024]{0:T(1024)S(1)} %pad_clamp_fusion), kind=kCustom, calls=%fused_computation | custom fusion | bytes 6144 | tf_op jit(solution)/shard_map/gather | solution.py:85
  (57 shorter events, 4.2 us)
Async XLA Ops:
  6.5 68.5 %copy-start = (bf16[2,1024]{1,0:T(2,128)(2,1)S(1)}, bf16[2,1024]{1,0:T(2,128)(2,1)}, u32[]{:S(2)}) copy-start(bf16[2,1024]{1,0:T(2,128)(2,1)} %param.11) | copy-start | bytes 12292
  14.9 11.9 %all-to-all-start.2 = ((bf16[4,1,192]{2,1,0:T(2,128)(2,1)}), bf16[4,1,192]{2,1,0:T(2,128)(2,1)S(1)}, u32[]{:S(2)}, u32[]{:S(2)}) async-start(bf16[4,1,192]{2,1,0:T(2,128)(2,1)} %all_to_all.39), calls=%async_computation.2 | async-start | bytes 8192 | tf_op jit(solution)/shard_map/all_to_all | solution.py:50
  26.8 8.6 %all-to-all-start = ((s32[4,1,192]{2,1,0:T(1,128)}), s32[4,1,192]{2,1,0:T(1,128)S(1)}, u32[]{:S(2)}, u32[]{:S(2)}) async-start(s32[4,1,192]{2,1,0:T(1,128)} %all_to_all.29), calls=%async_computation | async-start | bytes 8192 | tf_op jit(solution)/shard_map/all_to_all | solution.py:51
  35.4 39.6 %all-to-all-start.3 = ((bf16[4,192,1024]{2,1,0:T(8,128)(2,1)}), bf16[4,192,1024]{2,1,0:T(8,128)(2,1)S(1)}, u32[]{:S(2)}, u32[]{:S(2)}) async-start(bf16[4,192,1024]{2,1,0:T(8,128)(2,1)} %bitcast.6), calls=%async_computation.3 | async-start | bytes 3145728 | tf_op jit(solution)/shard_map/all_to_all | solution.py:49
  39.6 109.9 %all-gather.4.cloned.1.call-start = ((), (), s32[]{:S(2)}) async-start(), calls=%async_computation.5 | async-start | bytes 14155776 | tf_op jit(solution)/shard_map/all_gather | solution.py:65
  39.6 44.8 %copy-start.1 = (s32[4,1,192]{2,0,1:T(4,128)}, s32[4,1,192]{2,0,1:T(4,128)S(1)}, u32[]{:S(2)}) copy-start(s32[4,1,192]{2,0,1:T(4,128)S(1)} %copy.27) | copy-start | bytes 9220
  81.2 12.5 %all-to-all-start.1 = ((s32[4,1,192]{2,1,0:T(1,128)}), s32[4,1,192]{2,1,0:T(1,128)S(1)}, u32[]{:S(2)}, u32[]{:S(2)}) async-start(s32[4,1,192]{2,1,0:T(1,128)} %all_to_all.31), calls=%async_computation.1 | async-start | bytes 8192 | tf_op jit(solution)/shard_map/all_to_all | solution.py:52
  102.8 46.7 %copy-start.2 = (s32[4,1,192]{2,0,1:T(4,128)}, s32[4,1,192]{2,0,1:T(4,128)S(1)}, u32[]{:S(2)}) copy-start(s32[4,1,192]{2,0,1:T(4,128)S(1)} %copy.26) | copy-start | bytes 9220
  178.6 10.2 %all-to-all-start.4 = ((f32[4,1,192]{2,1,0:T(1,128)}), f32[4,1,192]{2,1,0:T(1,128)S(1)}, u32[]{:S(2)}, u32[]{:S(2)}) async-start(f32[4,1,192]{2,1,0:T(1,128)} %all_to_all.37), calls=%async_computation.4 | async-start | bytes 8192 | tf_op jit(solution)/shard_map/all_to_all | solution.py:82
Sparse Core Ops, SparseCore 0:
  78.1 71.3 all-gather.3
where the time goes:
time: 200 us; the launch traced here: 199 us
  waiting for transfers between devices  90.8 us (45%)
  matrix products  28.8 us (14%)
  starting transfers between devices  21.6 us (11%)
  local copies, waits for them, and re-layouts  20.4 us (10%)
  blocking collectives  18.1 us (9%)
  between operations  13.5 us (7%)
  other arithmetic  5.7 us (3%)
    all_gather x1, waiting for transfers between devices, shards(): piece_rows = lax.all_gather(own_rows, 'blk', axis=0, tiled=True)  46.6 us
    all_to_all x1, waiting for transfers between devices, shards(): lax.all_to_all(send_codes, 'group', split_axis=0, concat_axis=0, tiled=True)  35.4 us
    dot_general x8, matrix products, compare(): jnp.einsum('qd,kd->qk', own_rows, key_rows, preferred_element_type=jnp.fl...  27.6 us
    all_gather x1, blocking collectives, shards(): lax.all_gather(for_sending(own_order), 'blk', axis=0, tiled=True)  9.07 us
    all_gather x1, blocking collectives, shards(): piece_sub = lax.all_gather(for_sending(own_sub), 'blk', axis=0, tiled=True)  9.03 us
    all_to_all x1, starting transfers between devices, shards(): lax.all_to_all(send_scale, 'group', split_axis=0, concat_axis=0, tiled=True)  6.32 us
    all_to_all x1, waiting for transfers between devices, shards(): lax.all_to_all(best_sim.reshape(groups, capacity), 'group', split_axis=0,...  5.57 us
    all_to_all x1, starting transfers between devices, shards(): lax.all_to_all(best_sim.reshape(groups, capacity), 'group', split_axis=0,...  4.6 us
  transfers between devices with their start and end apart: 6, of which 5 were waited for; matrix products, arithmetic and copies ran while one was open for 5% of the time, Pallas kernels for 0%

commit v1 on v0

v1 whole, which is shorter than its diff:
```python
import functools

import jax
import jax.numpy as jnp
from jax import lax
from jax.experimental import pallas as pl
from jax.experimental.pallas import tpu as pltpu
from jax.sharding import PartitionSpec as P

META = 16
OWN, SIB, XN, YN = 0, 1, 2, 3
VMEM_LIMIT = 48 * 1024 * 1024


def dot_last(a, b):
    return lax.dot_general(a, b, (((1,), (1,)), ((), ())), preferred_element_type=jnp.float32)


def as_column(row):
    n = row.shape[1]
    eye = lax.broadcasted_iota(jnp.int32, (n, n), 0) == lax.broadcasted_iota(jnp.int32, (n, n), 1)
    return jnp.sum(jnp.where(eye, row, 0.0), axis=1, keepdims=True)


def vmem_specs(count):
    return [pl.BlockSpec(memory_space=pltpu.VMEM)] * count


def pack_kernel(cap, groups, aux_ref, codes_ref, *out_refs):
    chunk_refs, place_ref = out_refs[:groups], out_refs[groups]
    rows = codes_ref.shape[0]
    group_pos = lax.axis_index("group")
    hop = aux_ref[2:3, :].astype(jnp.int32) ^ group_pos
    member = (lax.broadcasted_iota(jnp.int32, (16, rows), 0) == hop).astype(jnp.bfloat16)
    upto = (
        lax.broadcasted_iota(jnp.int32, (rows, rows), 0)
        <= lax.broadcasted_iota(jnp.int32, (rows, rows), 1)
    ).astype(jnp.bfloat16)
    counts = jnp.dot(member, upto, preferred_element_type=jnp.float32)
    rank = jnp.sum(counts * member.astype(jnp.float32), axis=0, keepdims=True).astype(jnp.int32) - 1
    place_ref[...] = jnp.concatenate([hop, rank] + [jnp.zeros_like(rank)] * 6, axis=0)
    meta_rows = jnp.concatenate(
        [aux_ref[0:2, :], jnp.zeros((META - 2, rows), jnp.float32)], axis=0
    ).astype(jnp.bfloat16)
    codes = codes_ref[...]
    slots = lax.broadcasted_iota(jnp.int32, (cap, rows), 0)
    for s in range(groups):
        pick = (slots == jnp.where(hop == s, rank, -1)).astype(jnp.bfloat16)
        chunk_refs[s][0:cap, :] = jnp.dot(pick, codes, preferred_element_type=jnp.float32).astype(
            jnp.bfloat16
        )
        chunk_refs[s][cap:, :] = jnp.zeros((META, codes.shape[1]), jnp.bfloat16)
        chunk_refs[s][cap:, 0:cap] = dot_last(meta_rows, pick).astype(jnp.bfloat16)


def unit_kernel(cap, chunk_ref, cent_ref, out_ref):
    meta = chunk_ref[cap:, 0:cap].astype(jnp.float32)
    scale = as_column(meta[0:1, :])
    code = as_column(meta[1:2, :])
    cent = cent_ref[...].astype(jnp.float32)
    centre = jnp.where(code == 2.0, cent[1:2, :], cent[0:1, :])
    vectors = centre + scale * chunk_ref[0:cap, :].astype(jnp.float32)
    norm = jnp.sqrt(jnp.sum(vectors * vectors, axis=1, keepdims=True) + 1e-06)
    out_ref[0:cap, :] = (vectors * (1.0 / norm)).astype(jnp.bfloat16)
    out_ref[cap:, :] = chunk_ref[cap:, :]


def score_kernel(cap, old, new, *refs):
    chunks = old + new
    count = len(chunks)
    ins = refs[: 4 * count]
    before = refs[4 * count : 4 * count + 3] if old else ()
    own_ref, x_ref, y_ref, data, meta, acc, sem = refs[4 * count + len(before) :]
    blk = lax.axis_index("blk")
    group_pos = lax.axis_index("group")
    core, x, y = blk % 2, (blk // 2) % 2, blk // 4
    copies = []
    for block in range(4):
        for at in range(count):
            source = ins[block * count + at]
            copies.append(
                (
                    pltpu.make_async_copy(
                        source.at[0:cap, :],
                        data.at[block, at * cap : (at + 1) * cap, :],
                        sem.at[0, block, at],
                    ),
                    pltpu.make_async_copy(
                        source.at[cap:, 0:256], meta.at[block, at], sem.at[1, block, at]
                    ),
                )
            )
    for pair in copies:
        pair[0].start()
        pair[1].start()
    acc[...] = jnp.full(acc.shape, -1.0, jnp.float32)
    if old:
        for block, ref in zip((OWN, XN, YN), before):
            acc[block, 0:4, :] = ref[...]
    for pair in copies:
        pair[0].wait()
        pair[1].wait()

    def codes_of(block, at):
        return meta[block, at][1:2, 0:cap].astype(jnp.float32)

    def score(early, late, late_at, early_from, early_to, own_pair=False):
        e_rows = data[early, early_from * cap : early_to * cap, :]
        l_rows = data[late, late_at * cap : (late_at + 1) * cap, :]
        scores = dot_last(e_rows, l_rows)
        l_code = codes_of(late, late_at)
        best = acc[late, chunks[late_at] : chunks[late_at] + 1, :]
        for at in range(early_from, early_to):
            part = scores[(at - early_from) * cap : (at - early_from + 1) * cap, :]
            allowed = as_column(codes_of(early, at)) == l_code
            if own_pair:
                if at == late_at:
                    allowed &= lax.broadcasted_iota(
                        jnp.int32, (cap, cap), 0
                    ) < lax.broadcasted_iota(jnp.int32, (cap, cap), 1)
                else:
                    limit = jnp.where(
                        (group_pos ^ chunks[at]) < (group_pos ^ chunks[late_at]), cap, 0
                    )
                    allowed &= lax.broadcasted_iota(jnp.int32, (cap, cap), 0) < limit
            best = jnp.maximum(
                best, jnp.max(jnp.where(allowed, part, -1.0), axis=0, keepdims=True)
            )
        acc[late, chunks[late_at] : chunks[late_at] + 1, :] = best

    def all_of(early, late, own_pair=False):
        for late_at in range(count):
            if late_at < len(old):
                score(early, late, late_at, len(old), count, own_pair)
            else:
                score(early, late, late_at, 0, count, own_pair)

    def one_pair(number, carry):
        late = jnp.where(
            number == 0,
            jnp.where(x == 0, XN, OWN),
            jnp.where(
                number == 1,
                jnp.where(y == 0, YN, OWN),
                jnp.where(number == 2, jnp.where(y == 0, YN, XN), OWN),
            ),
        )
        both = jnp.where(
            number == 0,
            OWN + XN,
            jnp.where(number == 1, OWN + YN, jnp.where(number == 2, XN + YN, OWN + SIB)),
        )
        all_of(both - late, late)
        return carry

    all_of(OWN, OWN, own_pair=True)
    lax.fori_loop(0, 3 + core, one_pair, 0)
    own_ref[...] = acc[OWN, 0:4, :]
    x_ref[...] = acc[XN, 0:4, :]
    y_ref[...] = acc[YN, 0:4, :]


def restore_kernel(cap, groups, place_ref, *refs):
    parts, out_ref = refs[:groups], refs[groups]
    rows = place_ref.shape[1]
    hop, rank = place_ref[0:1, :], place_ref[1:2, :]
    slots = lax.broadcasted_iota(jnp.int32, (cap, rows), 0)
    total = jnp.zeros((16, rows), jnp.float32)
    for s in range(groups):
        value = parts[s][...]
        high = value.astype(jnp.bfloat16)
        rest = value - high.astype(jnp.float32)
        middle = rest.astype(jnp.bfloat16)
        low = (rest - middle.astype(jnp.float32)).astype(jnp.bfloat16)
        stacked = jnp.concatenate(
            [high.astype(jnp.float32), middle.astype(jnp.float32), low.astype(jnp.float32)]
            + [jnp.zeros((13, cap), jnp.float32)],
            axis=0,
        ).astype(jnp.bfloat16)
        pick = (slots == jnp.where(hop == s, rank, -1)).astype(jnp.bfloat16)
        total = total + jnp.dot(stacked, pick, preferred_element_type=jnp.float32)
    out_ref[...] = total[0:1, :] + (total[1:2, :] + total[2:3, :])


def blk_of(y, x, core):
    return (y * 2 + x) * 2 + core


def plane_pairs():
    to_x, to_y, to_sib = [], [], []
    for y in range(2):
        for x in range(2):
            for core in range(2):
                me = blk_of(y, x, core)
                to_x.append((blk_of(y, 1 - x, core ^ x ^ y), me))
                to_y.append((blk_of(1 - y, x, core ^ y), me))

            to_sib.append((blk_of(y, x, 0), blk_of(y, x, 1)))
    return to_x, to_y, to_sib


def reverse(pairs):
    return [(b, a) for a, b in pairs]


def score_call(cap, old, new, blocks, before, width):
    count = len(old) + len(new)
    arrays = [block[at] for block in blocks for at in old + new]
    shape = jax.ShapeDtypeStruct((4, cap), jnp.float32)
    pairs = 5 * (count * count - len(old) ** 2)
    return pl.pallas_call(
        functools.partial(score_kernel, cap, tuple(old), tuple(new)),
        out_shape=[shape] * 3,
        in_specs=[pl.BlockSpec(memory_space=pl.ANY)] * (4 * count) + vmem_specs(len(before)),
        out_specs=vmem_specs(3),
        scratch_shapes=[
            pltpu.VMEM((4, count * cap, width), jnp.bfloat16),
            pltpu.VMEM((4, count, META, 256), jnp.bfloat16),
            pltpu.VMEM((4, 8, cap), jnp.float32),
            pltpu.SemaphoreType.DMA((2, 4, count)),
        ],
        compiler_params=pltpu.CompilerParams(vmem_limit_bytes=VMEM_LIMIT),
        cost_estimate=pl.CostEstimate(
            flops=2 * pairs * cap * cap * width,
            bytes_accessed=8 * count * cap * width,
            transcendentals=0,
        ),
    )(*arrays, *before)


def paired_shards(codes, row_scale, row_group, row_sub, centroids):
    row_count, width = codes.shape
    groups = lax.axis_size("group")
    cap = 3 * row_count // (2 * groups)
    params = pltpu.CompilerParams(vmem_limit_bytes=VMEM_LIMIT)
    aux = jnp.stack(
        [
            row_scale.astype(jnp.float32),
            row_sub.astype(jnp.float32) + 1.0,
            row_group[:, 0].astype(jnp.float32),
            jnp.zeros((row_count,), jnp.float32),
        ]
    )
    chunk_shape = jax.ShapeDtypeStruct((cap + META, width), jnp.bfloat16)
    *packed, place = pl.pallas_call(
        functools.partial(pack_kernel, cap, groups),
        out_shape=[chunk_shape] * groups + [jax.ShapeDtypeStruct((8, row_count), jnp.int32)],
        in_specs=vmem_specs(2),
        out_specs=vmem_specs(groups + 1),
        compiler_params=params,
    )(aux, codes)
    hops = [[(g, g ^ s) for g in range(groups)] for s in range(groups)]
    arrived = [None] * groups
    for s in (2, 3, 1):
        arrived[s] = lax.ppermute(packed[s], "group", hops[s])
    arrived[0] = packed[0]
    unit_call = pl.pallas_call(
        functools.partial(unit_kernel, cap),
        out_shape=chunk_shape,
        in_specs=vmem_specs(2),
        out_specs=pl.BlockSpec(memory_space=pltpu.VMEM),
        compiler_params=params,
        cost_estimate=pl.CostEstimate(
            flops=8 * cap * width, bytes_accessed=4 * cap * width, transcendentals=0
        ),
    )
    to_x, to_y, to_sib = plane_pairs()
    blocks = [[None] * groups for _ in range(4)]
    for s in (0, 1, 2, 3):
        unit = unit_call(arrived[s], centroids)
        blocks[OWN][s] = unit
        blocks[XN][s] = lax.ppermute(unit, "blk", to_x)
        blocks[YN][s] = lax.ppermute(unit, "blk", to_y)
        blocks[SIB][s] = lax.ppermute(unit, "blk", to_sib)
    before = score_call(cap, [], [0, 1, 2], blocks, [], width)
    best, for_x, for_y = score_call(cap, [0, 1, 2], [3], blocks, before, width)
    best = jnp.maximum(
        best,
        jnp.maximum(
            lax.ppermute(for_x, "blk", reverse(to_x)), lax.ppermute(for_y, "blk", reverse(to_y))
        ),
    )
    returned = [best[0:1]] + [
        lax.ppermute(best[s : s + 1], "group", hops[s]) for s in range(1, groups)
    ]
    out = pl.pallas_call(
        functools.partial(restore_kernel, cap, groups),
        out_shape=jax.ShapeDtypeStruct((1, row_count), jnp.float32),
        in_specs=vmem_specs(groups + 1),
        out_specs=pl.BlockSpec(memory_space=pltpu.VMEM),
        compiler_params=params,
    )(place, *returned)
    return out.reshape(row_count)


def compare(best_sim, own_rows, own_order, own_sub, key_rows, key_order, key_sub):
    scores = jnp.einsum("qd,kd->qk", own_rows, key_rows, preferred_element_type=jnp.float32)
    allowed = (
        (key_sub[None, :] == own_sub[:, None])
        & (key_order[None, :] < own_order[:, None])
        & (key_order[None, :] > 0)
    )
    return jnp.maximum(best_sim, jnp.max(jnp.where(allowed, scores, -1.0), axis=1))


def gathered_shards(codes, row_scale, row_group, row_sub, centroids):
    row_count, width = codes.shape
    groups = lax.axis_size("group")
    capacity = 3 * row_count // (2 * groups)
    slot_count = groups * capacity
    cycle_pos = lax.axis_index("blk")
    group_pos = lax.axis_index("group")
    target = row_group[:, 0]
    member = (target[:, None] == jnp.arange(groups, dtype=jnp.int32)[None, :]).astype(jnp.int32)
    slot_rank = jnp.sum((jnp.cumsum(member, axis=0) - 1) * member, axis=1)
    placed = target * capacity + slot_rank
    row_order = (
        (cycle_pos * groups + group_pos) * row_count + jnp.arange(row_count, dtype=jnp.int32) + 1
    )

    def send(values):
        slots = jnp.zeros((slot_count,) + values.shape[1:], values.dtype).at[placed].set(values)
        return lax.all_to_all(
            slots.reshape((groups, capacity) + values.shape[1:]), "group", 0, 0, tiled=True
        )

    part_codes, part_scale = send(codes), send(row_scale)
    part_sub, part_order = send(row_sub), send(row_order)
    picks = (part_sub[..., None] == jnp.arange(centroids.shape[0], dtype=jnp.int32)).astype(
        jnp.bfloat16
    )
    centre = jnp.einsum("gnc,cd->gnd", picks, centroids, preferred_element_type=jnp.float32)
    vectors = centre + part_scale.astype(jnp.float32)[..., None] * part_codes.astype(jnp.float32)
    unit_part = (
        vectors / jnp.sqrt(jnp.sum(vectors * vectors, axis=-1, keepdims=True) + 1e-06)
    ).astype(jnp.bfloat16)
    own_rows = unit_part.reshape(slot_count, width)
    own_order = part_order.reshape(slot_count)
    own_sub = part_sub.reshape(slot_count)
    stacked = tuple(lax.all_gather(a, "blk", axis=0) for a in (own_rows, own_order, own_sub))

    def per_shard(carry, item):
        return compare(carry, own_rows, own_order, own_sub, *item), None

    start_sim = jnp.full((slot_count,), -1.0, jnp.float32)
    best_sim = lax.scan(per_shard, start_sim, stacked)[0]
    returned = lax.all_to_all(best_sim.reshape(groups, capacity), "group", 0, 0, tiled=True)
    return returned.reshape(-1)[placed]


def solution(mesh):
    paired = mesh.shape["blk"] == 8 and mesh.shape["group"] == 4
    return jax.shard_map(
        paired_shards if paired else gathered_shards,
        mesh=mesh,
        in_specs=(
            P(("blk", "group"), None),
            P(("blk", "group")),
            P(("blk", "group"), None),
            P(("blk", "group")),
            P("group", None),
        ),
        out_specs=P(("blk", "group")),
        check_vma=False,
    )
```

time: 200 us -> 91.2 us (0.46)
  waiting for transfers between devices: 90.8 us -> 32.4 us
  matrix products: 28.8 us -> 0 us
  Pallas kernels: 0 us -> 18.8 us
  local copies, waits for them, and re-layouts: 20.4 us -> 2 us
  blocking collectives: 18.1 us -> 0 us
  starting transfers between devices: 21.6 us -> 36.7 us
  between operations: 13.5 us -> 0.22 us
  other arithmetic: 5.7 us -> 0.78 us
    all_gather x1 -> x0, waiting for transfers between devices: 46.6 us -> none  [shards(): piece_rows = lax.all_gather(own_rows, 'blk', axis=0, tiled=True)]
    all_to_all x5 -> x0, waiting for transfers between devices: 44.2 us -> none  [the longest x1 35.4 us: shards(): lax.all_to_all(send_codes, 'group', split_axis=0, concat_axis=0, tiled=True)]
    ppermute x0 -> x20, starting transfers between devices: none -> 36.7 us  [the longest x3 13.3 us: paired_shards(): lax.ppermute(best[s:s + 1], 'group', hops[s])]
    ppermute x0 -> x20, waiting for transfers between devices: none -> 32.4 us  [the longest x3 17.1 us: paired_shards(): arrived[s] = lax.ppermute(packed[s], 'group', hops[s])]
    dot_general x9 -> x0, matrix products: 28.8 us -> none  [the longest x8 27.6 us: compare(): jnp.einsum('qd,kd->qk', own_rows, key_rows, preferred_element_type=jnp.fl...]
    all_to_all x5 -> x0, starting transfers between devices: 21.6 us -> none  [the longest x1 6.32 us: shards(): lax.all_to_all(send_scale, 'group', split_axis=0, concat_axis=0, tiled=True)]
    pallas_call x0 -> x8, Pallas kernels: none -> 18.8 us  [the longest x2 15.3 us: score_call(): pl.pallas_call(functools.partial(score_kernel, cap, tuple(old), tuple(new...]
    all_gather x2 -> x0, blocking collectives: 18.1 us -> none  [the longest x1 9.07 us: shards(): lax.all_gather(for_sending(own_order), 'blk', axis=0, tiled=True)]
  transfers between devices with their start and end apart: 6 -> 20, of which waited for: 5 -> 9; matrix products, arithmetic and copies ran while one was open for 5% -> 0% of each run, Pallas kernels for 0% -> 9%
where the time goes in v1:
time: 91.2 us; the launch traced here: 90.9 us
  starting transfers between devices  36.7 us (40%)
  waiting for transfers between devices  32.4 us (36%)
  Pallas kernels  18.8 us (21%)
  local copies, waits for them, and re-layouts  2 us (2%)
    ppermute x3, waiting for transfers between devices, paired_shards(): arrived[s] = lax.ppermute(packed[s], 'group', hops[s])  17.1 us
    pallas_call x2, Pallas kernels, score_call(): pl.pallas_call(functools.partial(score_kernel, cap, tuple(old), tuple(new...  15.3 us
    ppermute x3, starting transfers between devices, paired_shards(): lax.ppermute(best[s:s + 1], 'group', hops[s])  13.3 us
    ppermute x3, starting transfers between devices, paired_shards(): arrived[s] = lax.ppermute(packed[s], 'group', hops[s])  8.31 us
    ppermute x4, waiting for transfers between devices, paired_shards(): blocks[YN][s] = lax.ppermute(unit, 'blk', to_y)  8.21 us
    ppermute x4, starting transfers between devices, paired_shards(): blocks[XN][s] = lax.ppermute(unit, 'blk', to_x)  7.17 us
    ppermute x4, starting transfers between devices, paired_shards(): blocks[SIB][s] = lax.ppermute(unit, 'blk', to_sib)  5.22 us
    ppermute x3, waiting for transfers between devices, paired_shards(): lax.ppermute(best[s:s + 1], 'group', hops[s])  3.83 us
  transfers between devices with their start and end apart: 20, of which 9 were waited for; matrix products, arithmetic and copies ran while one was open for 0% of the time, Pallas kernels for 9%

profile of v1, /device:TPU:0, one launch (start us, length us, event | category | flops | bytes accessed | tf_op | source)
XLA Modules:
  0.0 90.9 jit_solution(1572415782681023985)
XLA Ops:
  0.0 0.7 stack.17
  0.7 0.7 copy-done.4
  1.5 1.2 %copy-done = bf16[512,1024]{1,0:T(8,128)(2,1)S(1)} copy-done((bf16[512,1024]{1,0:T(8,128)(2,1)S(1)}, bf16[512,1024]{1,0:T(8,128)(2,1)}, u32[]{:S(2)}) %copy-start) | copy-done | bytes 1048600
  2.8 1.4 %shard_map.55 = (bf16[208,1024]{1,0:T(8,128)(2,1)S(1)}, bf16[208,1024]{1,0:T(8,128)(2,1)S(1)}, bf16[208,1024]{1,0:T(8,128)(2,1)S(1)}, bf16[208,1024]{1,0:T(8,128)(2,1)S(1)}, s32[8,512]{1,0:T(8,128)S(1)}) custom-call(f32[4,512]{1,0:T(4,128)S(1)} %maximum_maximum_fusion.aux_ref, bf16[512,1024]{1,0:T(8,128)(2,1)S(1)} %copy-done), custom_call_target="tpu_custom_call" | custom-call | tf_op jit(solution)/shard_map/pallas_call | solution.py:245
  4.1 3.1 %collective-permute-start = (bf16[208,1024]{1,0:T(8,128)(2,1)S(1)}, bf16[208,1024]{1,0:T(8,128)(2,1)S(1)}, u32[]{:S(2)}, u32[]{:S(2)}) collective-permute-start(bf16[208,1024]{1,0:T(8,128)(2,1)S(1)} %get-tuple-element.18), channel_id=1, source_target_pairs={{0,1},{1,0},{2,3},{3,2},{4,5},{5,4},{6,7},{7,6},{8,9},{9,8},{10,11... | collective-permute-start | bytes 1277960 | tf_op jit(solution)/shard_map/ppermute | solution.py:255
  7.2 2.6 %collective-permute-start.1 = (bf16[208,1024]{1,0:T(8,128)(2,1)S(1)}, bf16[208,1024]{1,0:T(8,128)(2,1)S(1)}, u32[]{:S(2)}, u32[]{:S(2)}) collective-permute-start(bf16[208,1024]{1,0:T(8,128)(2,1)S(1)} %get-tuple-element.19), channel_id=1, source_target_pairs={{0,2},{1,3},{2,0},{3,1},{4,6},{5,7},{6,4},{7,5},{8,10},{9,11},{10,... | collective-permute-start | bytes 1277960 | tf_op jit(solution)/shard_map/ppermute | solution.py:255
  10.2 0.5 collective-permute-start.11
  10.6 2.3 %collective-permute-start.7 = (bf16[208,1024]{1,0:T(8,128)(2,1)S(1)}, bf16[208,1024]{1,0:T(8,128)(2,1)S(1)}, u32[]{:S(2)}, u32[]{:S(2)}) collective-permute-start(bf16[208,1024]{1,0:T(8,128)(2,1)S(1)} %shard_map.56.refs_0_), channel_id=1, source_target_pairs={{8,0},{12,4},{4,8},{0,12},{28,16},{24,20},{16,24},{20,28},{9,1},{1... | collective-permute-start | bytes 1277960 | tf_op jit(solution)/shard_map/ppermute | solution.py:272
  12.9 1.3 %collective-permute-start.3 = (bf16[208,1024]{1,0:T(8,128)(2,1)S(1)}, bf16[208,1024]{1,0:T(8,128)(2,1)S(1)}, u32[]{:S(2)}, u32[]{:S(2)}) collective-permute-start(bf16[208,1024]{1,0:T(8,128)(2,1)S(1)} %shard_map.56.refs_0_), channel_id=1, source_target_pairs={{0,4},{8,12},{16,20},{24,28},{1,5},{9,13},{17,21},{25,29},{2,6},{1... | collective-permute-start | bytes 1277960 | tf_op jit(solution)/shard_map/ppermute | solution.py:274
  14.3 11.8 %collective-permute-done.chunk_ref = bf16[208,1024]{1,0:T(8,128)(2,1)S(1)} collective-permute-done((bf16[208,1024]{1,0:T(8,128)(2,1)S(1)}, bf16[208,1024]{1,0:T(8,128)(2,1)S(1)}, u32[]{:S(2)}, u32[]{:S(2)}) %collective-permute-start) | collective-permute-done | bytes 426016 | tf_op jit(solution)/shard_map/ppermute | solution.py:255
  26.0 2.6 %collective-permute-start.2 = (bf16[208,1024]{1,0:T(8,128)(2,1)S(1)}, bf16[208,1024]{1,0:T(8,128)(2,1)S(1)}, u32[]{:S(2)}, u32[]{:S(2)}) collective-permute-start(bf16[208,1024]{1,0:T(8,128)(2,1)S(1)} %get-tuple-element.20), channel_id=1, source_target_pairs={{0,3},{1,2},{2,1},{3,0},{4,7},{5,6},{6,5},{7,4},{8,11},{9,10},{10,... | collective-permute-start | bytes 1277960 | tf_op jit(solution)/shard_map/ppermute | solution.py:255
  29.5 2.8 %collective-permute-start.8 = (bf16[208,1024]{1,0:T(8,128)(2,1)S(1)}, bf16[208,1024]{1,0:T(8,128)(2,1)S(1)}, u32[]{:S(2)}, u32[]{:S(2)}) collective-permute-start(bf16[208,1024]{1,0:T(8,128)(2,1)S(1)} %shard_map.57.refs_1_), channel_id=1, source_target_pairs={{8,0},{12,4},{4,8},{0,12},{28,16},{24,20},{16,24},{20,28},{9,1},{1... | collective-permute-start | bytes 1277960 | tf_op jit(solution)/shard_map/ppermute | solution.py:272
  32.2 1.3 %collective-permute-start.4 = (bf16[208,1024]{1,0:T(8,128)(2,1)S(1)}, bf16[208,1024]{1,0:T(8,128)(2,1)S(1)}, u32[]{:S(2)}, u32[]{:S(2)}) collective-permute-start(bf16[208,1024]{1,0:T(8,128)(2,1)S(1)} %shard_map.57.refs_1_), channel_id=1, source_target_pairs={{0,4},{8,12},{16,20},{24,28},{1,5},{9,13},{17,21},{25,29},{2,6},{1... | collective-permute-start | bytes 1277960 | tf_op jit(solution)/shard_map/ppermute | solution.py:274
  33.6 5.3 %collective-permute-done.2.chunk_ref = bf16[208,1024]{1,0:T(8,128)(2,1)S(1)} collective-permute-done((bf16[208,1024]{1,0:T(8,128)(2,1)S(1)}, bf16[208,1024]{1,0:T(8,128)(2,1)S(1)}, u32[]{:S(2)}, u32[]{:S(2)}) %collective-permute-start.2) | collective-permute-done | bytes 426016 | tf_op jit(solution)/shard_map/ppermute | solution.py:255
  39.0 2.9 %collective-permute-done.12.refs_10_.refs_13_ = bf16[208,1024]{1,0:T(8,128)(2,1)S(1)} collective-permute-done((bf16[208,1024]{1,0:T(8,128)(2,1)S(1)}, bf16[208,1024]{1,0:T(8,128)(2,1)S(1)}, u32[]{:S(2)}, u32[]{:S(2)}) %collective-permute-start.12) | collective-permute-done | bytes 426016 | tf_op jit(solution)/shard_map/ppermute | solution.py:273
  41.8 1.3 %collective-permute-start.5 = (bf16[208,1024]{1,0:T(8,128)(2,1)S(1)}, bf16[208,1024]{1,0:T(8,128)(2,1)S(1)}, u32[]{:S(2)}, u32[]{:S(2)}) collective-permute-start(bf16[208,1024]{1,0:T(8,128)(2,1)S(1)} %shard_map.58.refs_2_), channel_id=1, source_target_pairs={{0,4},{8,12},{16,20},{24,28},{1,5},{9,13},{17,21},{25,29},{2,6},{1... | collective-permute-start | bytes 1277960 | tf_op jit(solution)/shard_map/ppermute | solution.py:274
  43.2 0.3 shard_map.59.refs_3_
  43.6 2.1 %collective-permute-start.10 = (bf16[208,1024]{1,0:T(8,128)(2,1)S(1)}, bf16[208,1024]{1,0:T(8,128)(2,1)S(1)}, u32[]{:S(2)}, u32[]{:S(2)}) collective-permute-start(bf16[208,1024]{1,0:T(8,128)(2,1)S(1)} %shard_map.59.refs_3_), channel_id=1, source_target_pairs={{8,0},{12,4},{4,8},{0,12},{28,16},{24,20},{16,24},{20,28},{9,1},{1... | collective-permute-start | bytes 1277960 | tf_op jit(solution)/shard_map/ppermute | solution.py:272
  45.7 5.3 %collective-permute-done.13.refs_11_.refs_14_ = bf16[208,1024]{1,0:T(8,128)(2,1)S(1)} collective-permute-done((bf16[208,1024]{1,0:T(8,128)(2,1)S(1)}, bf16[208,1024]{1,0:T(8,128)(2,1)S(1)}, u32[]{:S(2)}, u32[]{:S(2)}) %collective-permute-start.13) | collective-permute-done | bytes 426016 | tf_op jit(solution)/shard_map/ppermute | solution.py:273
  51.0 1.3 %collective-permute-start.6 = (bf16[208,1024]{1,0:T(8,128)(2,1)S(1)}, bf16[208,1024]{1,0:T(8,128)(2,1)S(1)}, u32[]{:S(2)}, u32[]{:S(2)}) collective-permute-start(bf16[208,1024]{1,0:T(8,128)(2,1)S(1)} %shard_map.59.refs_3_), channel_id=1, source_target_pairs={{0,4},{8,12},{16,20},{24,28},{1,5},{9,13},{17,21},{25,29},{2,6},{1... | collective-permute-start | bytes 1277960 | tf_op jit(solution)/shard_map/ppermute | solution.py:274
  52.3 7.1 %shard_map.60 = (f32[4,192]{1,0:T(4,128)S(1)}, f32[4,192]{1,0:T(4,128)S(1)}, f32[4,192]{1,0:T(4,128)S(1)}) custom-call(bf16[208,1024]{1,0:T(8,128)(2,1)S(1)} %shard_map.56.refs_0_, bf16[208,1024]{1,0:T(8,128)(2,1)S(1)} %shard_map.57.refs_1_, bf16[208,1024]{1,0:T(8,128)(2,1)S(1)} %shard_map.58.refs_2_, ...), custom_call_target="tpu_custom_call" | custom-call | flops 3397386240 | bytes 4718592 | tf_op jit(solution)/shard_map/pallas_call | solution.py:211
  59.5 1.0 %collective-permute-done.10.refs_11_ = bf16[208,1024]{1,0:T(8,128)(2,1)S(1)} collective-permute-done((bf16[208,1024]{1,0:T(8,128)(2,1)S(1)}, bf16[208,1024]{1,0:T(8,128)(2,1)S(1)}, u32[]{:S(2)}, u32[]{:S(2)}) %collective-permute-start.10) | collective-permute-done | bytes 426016 | tf_op jit(solution)/shard_map/ppermute | solution.py:272
  60.5 8.1 %shard_map.61 = (f32[4,192]{1,0:T(4,128)S(1)}, f32[4,192]{1,0:T(4,128)S(1)}, f32[4,192]{1,0:T(4,128)S(1)}) custom-call(bf16[208,1024]{1,0:T(8,128)(2,1)S(1)} %shard_map.56.refs_0_, bf16[208,1024]{1,0:T(8,128)(2,1)S(1)} %shard_map.57.refs_1_, bf16[208,1024]{1,0:T(8,128)(2,1)S(1)} %shard_map.58.refs_2_, bf16[208,1024]{1,0:T(8,128)(2,1)S(1)} %shard_map.59.refs_3_, ...), custom_call_target="tpu_custom_call" | custom-call | flops 2642411520 | bytes 6291456 | tf_op jit(solution)/shard_map/pallas_call | solution.py:211
  68.6 1.3 %collective-permute-start.15 = (f32[4,192]{1,0:T(4,128)S(1)}, f32[4,192]{1,0:T(4,128)S(1)}, u32[]{:S(2)}, u32[]{:S(2)}) collective-permute-start(f32[4,192]{1,0:T(4,128)S(1)} %get-tuple-element.25), channel_id=1, source_target_pairs={{0,8},{4,12},{8,4},{12,0},{16,28},{20,24},{24,16},{28,20},{1,9},{5... | collective-permute-start | bytes 9224 | tf_op jit(solution)/shard_map/ppermute | solution.py:280
  69.9 0.8 collective-permute-start.16
  70.7 1.0 %collective-permute-done.15 = f32[4,192]{1,0:T(4,128)S(1)} collective-permute-done((f32[4,192]{1,0:T(4,128)S(1)}, f32[4,192]{1,0:T(4,128)S(1)}, u32[]{:S(2)}, u32[]{:S(2)}) %collective-permute-start.15) | collective-permute-done | bytes 3104 | tf_op jit(solution)/shard_map/ppermute | solution.py:280
  71.7 1.3 %collective-permute-done.16 = f32[4,192]{1,0:T(4,128)S(1)} collective-permute-done((f32[4,192]{1,0:T(4,128)S(1)}, f32[4,192]{1,0:T(4,128)S(1)}, u32[]{:S(2)}, u32[]{:S(2)}) %collective-permute-start.16) | collective-permute-done | bytes 3104 | tf_op jit(solution)/shard_map/ppermute | solution.py:280
  73.0 12.6 %collective-permute-start.19 = (f32[1,192]{1,0:T(1,128)S(1)}, f32[1,192]{1,0:T(1,128)S(1)}, u32[]{:S(2)}, u32[]{:S(2)}) collective-permute-start(f32[1,192]{1,0:T(1,128)S(1)} %get-tuple-element.27), channel_id=1, source_target_pairs={{0,3},{1,2},{2,1},{3,0},{4,7},{5,6},{6,5},{7,4},{8,11},{9,10},{10,... | collective-permute-start | bytes 2312 | tf_op jit(solution)/shard_map/ppermute | solution.py:284
  85.6 0.6 collective-permute-start.17
  86.2 0.9 collective-permute-done.19.refs_3_
  87.1 2.9 %collective-permute-done.18.refs_2_ = f32[1,192]{1,0:T(1,128)S(1)} collective-permute-done((f32[1,192]{1,0:T(1,128)S(1)}, f32[1,192]{1,0:T(1,128)S(1)}, u32[]{:S(2)}, u32[]{:S(2)}) %collective-permute-start.18) | collective-permute-done | bytes 800 | tf_op jit(solution)/shard_map/ppermute | solution.py:284
  90.1 0.8 shard_map.62
  (35 shorter events, 1.4 us)
Async XLA Ops:
  0.0 0.7 copy-start.3
  0.7 0.7 copy-start.4
  1.5 1.2 %copy-start = (bf16[512,1024]{1,0:T(8,128)(2,1)S(1)}, bf16[512,1024]{1,0:T(8,128)(2,1)}, u32[]{:S(2)}) copy-start(bf16[512,1024]{1,0:T(8,128)(2,1)} %codes_ref.1) | copy-start | bytes 3145732
  4.1 5.7 %copy-start.1 = (bf16[2,1024]{1,0:T(2,128)(2,1)S(1)}, bf16[2,1024]{1,0:T(2,128)(2,1)}, u32[]{:S(2)}) copy-start(bf16[2,1024]{1,0:T(2,128)(2,1)} %cent_ref.7) | copy-start | bytes 12292
  4.1 21.9 %collective-permute-start = (bf16[208,1024]{1,0:T(8,128)(2,1)S(1)}, bf16[208,1024]{1,0:T(8,128)(2,1)S(1)}, u32[]{:S(2)}, u32[]{:S(2)}) collective-permute-start(bf16[208,1024]{1,0:T(8,128)(2,1)S(1)} %get-tuple-element.18), channel_id=1, source_target_pairs={{0,1},{1,0},{2,3},{3,2},{4,5},{5,4},{6,7},{7,6},{8,9},{9,8},{10,11... | collective-permute-start | bytes 1277960 | tf_op jit(solution)/shard_map/ppermute | solution.py:255
  7.2 21.8 %collective-permute-start.1 = (bf16[208,1024]{1,0:T(8,128)(2,1)S(1)}, bf16[208,1024]{1,0:T(8,128)(2,1)S(1)}, u32[]{:S(2)}, u32[]{:S(2)}) collective-permute-start(bf16[208,1024]{1,0:T(8,128)(2,1)S(1)} %get-tuple-element.19), channel_id=1, source_target_pairs={{0,2},{1,3},{2,0},{3,1},{4,6},{5,7},{6,4},{7,5},{8,10},{9,11},{10,... | collective-permute-start | bytes 1277960 | tf_op jit(solution)/shard_map/ppermute | solution.py:255
  10.2 19.3 %collective-permute-start.11 = (bf16[208,1024]{1,0:T(8,128)(2,1)S(1)}, bf16[208,1024]{1,0:T(8,128)(2,1)S(1)}, u32[]{:S(2)}, u32[]{:S(2)}) collective-permute-start(bf16[208,1024]{1,0:T(8,128)(2,1)S(1)} %shard_map.56.refs_0_), channel_id=1, source_target_pairs={{16,0},{20,4},{24,8},{28,12},{4,16},{0,20},{12,24},{8,28},{17,1},{... | collective-permute-start | bytes 1277960 | tf_op jit(solution)/shard_map/ppermute | solution.py:273
  10.6 21.6 %collective-permute-start.7 = (bf16[208,1024]{1,0:T(8,128)(2,1)S(1)}, bf16[208,1024]{1,0:T(8,128)(2,1)S(1)}, u32[]{:S(2)}, u32[]{:S(2)}) collective-permute-start(bf16[208,1024]{1,0:T(8,128)(2,1)S(1)} %shard_map.56.refs_0_), channel_id=1, source_target_pairs={{8,0},{12,4},{4,8},{0,12},{28,16},{24,20},{16,24},{20,28},{9,1},{1... | collective-permute-start | bytes 1277960 | tf_op jit(solution)/shard_map/ppermute | solution.py:272
  12.9 20.6 %collective-permute-start.3 = (bf16[208,1024]{1,0:T(8,128)(2,1)S(1)}, bf16[208,1024]{1,0:T(8,128)(2,1)S(1)}, u32[]{:S(2)}, u32[]{:S(2)}) collective-permute-start(bf16[208,1024]{1,0:T(8,128)(2,1)S(1)} %shard_map.56.refs_0_), channel_id=1, source_target_pairs={{0,4},{8,12},{16,20},{24,28},{1,5},{9,13},{17,21},{25,29},{2,6},{1... | collective-permute-start | bytes 1277960 | tf_op jit(solution)/shard_map/ppermute | solution.py:274
  26.0 12.9 %collective-permute-start.2 = (bf16[208,1024]{1,0:T(8,128)(2,1)S(1)}, bf16[208,1024]{1,0:T(8,128)(2,1)S(1)}, u32[]{:S(2)}, u32[]{:S(2)}) collective-permute-start(bf16[208,1024]{1,0:T(8,128)(2,1)S(1)} %get-tuple-element.20), channel_id=1, source_target_pairs={{0,3},{1,2},{2,1},{3,0},{4,7},{5,6},{6,5},{7,4},{8,11},{9,10},{10,... | collective-permute-start | bytes 1277960 | tf_op jit(solution)/shard_map/ppermute | solution.py:255
  29.0 12.8 %collective-permute-start.12 = (bf16[208,1024]{1,0:T(8,128)(2,1)S(1)}, bf16[208,1024]{1,0:T(8,128)(2,1)S(1)}, u32[]{:S(2)}, u32[]{:S(2)}) collective-permute-start(bf16[208,1024]{1,0:T(8,128)(2,1)S(1)} %shard_map.57.refs_1_), channel_id=1, source_target_pairs={{16,0},{20,4},{24,8},{28,12},{4,16},{0,20},{12,24},{8,28},{17,1},{... | collective-permute-start | bytes 1277960 | tf_op jit(solution)/shard_map/ppermute | solution.py:273
  29.5 14.0 %collective-permute-start.8 = (bf16[208,1024]{1,0:T(8,128)(2,1)S(1)}, bf16[208,1024]{1,0:T(8,128)(2,1)S(1)}, u32[]{:S(2)}, u32[]{:S(2)}) collective-permute-start(bf16[208,1024]{1,0:T(8,128)(2,1)S(1)} %shard_map.57.refs_1_), channel_id=1, source_target_pairs={{8,0},{12,4},{4,8},{0,12},{28,16},{24,20},{16,24},{20,28},{9,1},{1... | collective-permute-start | bytes 1277960 | tf_op jit(solution)/shard_map/ppermute | solution.py:272
  32.2 11.3 %collective-permute-start.4 = (bf16[208,1024]{1,0:T(8,128)(2,1)S(1)}, bf16[208,1024]{1,0:T(8,128)(2,1)S(1)}, u32[]{:S(2)}, u32[]{:S(2)}) collective-permute-start(bf16[208,1024]{1,0:T(8,128)(2,1)S(1)} %shard_map.57.refs_1_), channel_id=1, source_target_pairs={{0,4},{8,12},{16,20},{24,28},{1,5},{9,13},{17,21},{25,29},{2,6},{1... | collective-permute-start | bytes 1277960 | tf_op jit(solution)/shard_map/ppermute | solution.py:274
  33.6 17.4 %collective-permute-start.13 = (bf16[208,1024]{1,0:T(8,128)(2,1)S(1)}, bf16[208,1024]{1,0:T(8,128)(2,1)S(1)}, u32[]{:S(2)}, u32[]{:S(2)}) collective-permute-start(bf16[208,1024]{1,0:T(8,128)(2,1)S(1)} %shard_map.58.refs_2_), channel_id=1, source_target_pairs={{16,0},{20,4},{24,8},{28,12},{4,16},{0,20},{12,24},{8,28},{17,1},{... | collective-permute-start | bytes 1277960 | tf_op jit(solution)/shard_map/ppermute | solution.py:273
  39.0 13.3 %collective-permute-start.9 = (bf16[208,1024]{1,0:T(8,128)(2,1)S(1)}, bf16[208,1024]{1,0:T(8,128)(2,1)S(1)}, u32[]{:S(2)}, u32[]{:S(2)}) collective-permute-start(bf16[208,1024]{1,0:T(8,128)(2,1)S(1)} %shard_map.58.refs_2_), channel_id=1, source_target_pairs={{8,0},{12,4},{4,8},{0,12},{28,16},{24,20},{16,24},{20,28},{9,1},{1... | collective-permute-start | bytes 1277960 | tf_op jit(solution)/shard_map/ppermute | solution.py:272
  41.8 10.5 %collective-permute-start.5 = (bf16[208,1024]{1,0:T(8,128)(2,1)S(1)}, bf16[208,1024]{1,0:T(8,128)(2,1)S(1)}, u32[]{:S(2)}, u32[]{:S(2)}) collective-permute-start(bf16[208,1024]{1,0:T(8,128)(2,1)S(1)} %shard_map.58.refs_2_), channel_id=1, source_target_pairs={{0,4},{8,12},{16,20},{24,28},{1,5},{9,13},{17,21},{25,29},{2,6},{1... | collective-permute-start | bytes 1277960 | tf_op jit(solution)/shard_map/ppermute | solution.py:274
  43.5 15.9 %collective-permute-start.14 = (bf16[208,1024]{1,0:T(8,128)(2,1)S(1)}, bf16[208,1024]{1,0:T(8,128)(2,1)S(1)}, u32[]{:S(2)}, u32[]{:S(2)}) collective-permute-start(bf16[208,1024]{1,0:T(8,128)(2,1)S(1)} %shard_map.59.refs_3_), channel_id=1, source_target_pairs={{16,0},{20,4},{24,8},{28,12},{4,16},{0,20},{12,24},{8,28},{17,1},{... | collective-permute-start | bytes 1277960 | tf_op jit(solution)/shard_map/ppermute | solution.py:273
  43.6 16.9 %collective-permute-start.10 = (bf16[208,1024]{1,0:T(8,128)(2,1)S(1)}, bf16[208,1024]{1,0:T(8,128)(2,1)S(1)}, u32[]{:S(2)}, u32[]{:S(2)}) collective-permute-start(bf16[208,1024]{1,0:T(8,128)(2,1)S(1)} %shard_map.59.refs_3_), channel_id=1, source_target_pairs={{8,0},{12,4},{4,8},{0,12},{28,16},{24,20},{16,24},{20,28},{9,1},{1... | collective-permute-start | bytes 1277960 | tf_op jit(solution)/shard_map/ppermute | solution.py:272
  51.0 8.5 %copy-start.2 = (bf16[208,1024]{1,0:T(8,128)(2,1)}, bf16[208,1024]{1,0:T(8,128)(2,1)S(1)}, u32[]{:S(2)}) copy-start(bf16[208,1024]{1,0:T(8,128)(2,1)S(1)} %collective-permute-done.13.refs_11_.refs_14_) | copy-start | bytes 1277956
  51.0 9.5 %collective-permute-start.6 = (bf16[208,1024]{1,0:T(8,128)(2,1)S(1)}, bf16[208,1024]{1,0:T(8,128)(2,1)S(1)}, u32[]{:S(2)}, u32[]{:S(2)}) collective-permute-start(bf16[208,1024]{1,0:T(8,128)(2,1)S(1)} %shard_map.59.refs_3_), channel_id=1, source_target_pairs={{0,4},{8,12},{16,20},{24,28},{1,5},{9,13},{17,21},{25,29},{2,6},{1... | collective-permute-start | bytes 1277960 | tf_op jit(solution)/shard_map/ppermute | solution.py:274
  59.5 1.0 %copy-start.5 = (bf16[208,1024]{1,0:T(8,128)(2,1)}, bf16[208,1024]{1,0:T(8,128)(2,1)S(1)}, u32[]{:S(2)}) copy-start(bf16[208,1024]{1,0:T(8,128)(2,1)S(1)} %collective-permute-done.14.refs_15_) | copy-start | bytes 1277956
  68.6 3.1 %collective-permute-start.15 = (f32[4,192]{1,0:T(4,128)S(1)}, f32[4,192]{1,0:T(4,128)S(1)}, u32[]{:S(2)}, u32[]{:S(2)}) collective-permute-start(f32[4,192]{1,0:T(4,128)S(1)} %get-tuple-element.25), channel_id=1, source_target_pairs={{0,8},{4,12},{8,4},{12,0},{16,28},{20,24},{24,16},{28,20},{1,9},{5... | collective-permute-start | bytes 9224 | tf_op jit(solution)/shard_map/ppermute | solution.py:280
  69.9 3.0 %collective-permute-start.16 = (f32[4,192]{1,0:T(4,128)S(1)}, f32[4,192]{1,0:T(4,128)S(1)}, u32[]{:S(2)}, u32[]{:S(2)}) collective-permute-start(f32[4,192]{1,0:T(4,128)S(1)} %get-tuple-element.26), channel_id=1, source_target_pairs={{0,16},{4,20},{8,24},{12,28},{16,4},{20,0},{24,12},{28,8},{1,17},{... | collective-permute-start | bytes 9224 | tf_op jit(solution)/shard_map/ppermute | solution.py:280
  73.0 14.2 %collective-permute-start.19 = (f32[1,192]{1,0:T(1,128)S(1)}, f32[1,192]{1,0:T(1,128)S(1)}, u32[]{:S(2)}, u32[]{:S(2)}) collective-permute-start(f32[1,192]{1,0:T(1,128)S(1)} %get-tuple-element.27), channel_id=1, source_target_pairs={{0,3},{1,2},{2,1},{3,0},{4,7},{5,6},{6,5},{7,4},{8,11},{9,10},{10,... | collective-permute-start | bytes 2312 | tf_op jit(solution)/shard_map/ppermute | solution.py:284
  85.6 4.5 %collective-permute-start.18 = (f32[1,192]{1,0:T(1,128)S(1)}, f32[1,192]{1,0:T(1,128)S(1)}, u32[]{:S(2)}, u32[]{:S(2)}) collective-permute-start(f32[1,192]{1,0:T(1,128)S(1)} %get-tuple-element.28), channel_id=1, source_target_pairs={{0,2},{1,3},{2,0},{3,1},{4,6},{5,7},{6,4},{7,5},{8,10},{9,11},{10,... | collective-permute-start | bytes 2312 | tf_op jit(solution)/shard_map/ppermute | solution.py:284
  85.6 4.5 %collective-permute-start.17 = (f32[1,192]{1,0:T(1,128)S(1)}, f32[1,192]{1,0:T(1,128)S(1)}, u32[]{:S(2)}, u32[]{:S(2)}) collective-permute-start(f32[1,192]{1,0:T(1,128)S(1)} %get-tuple-element.29), channel_id=1, source_target_pairs={{0,1},{1,0},{2,3},{3,2},{4,5},{5,4},{6,7},{7,6},{8,9},{9,8},{10,11... | collective-permute-start | bytes 2312 | tf_op jit(solution)/shard_map/ppermute | solution.py:284

commit v2 on v1

v2 whole, which is shorter than its diff:
```python
import functools

import jax
import jax.numpy as jnp
from jax import lax
from jax.experimental import pallas as pl
from jax.experimental.pallas import tpu as pltpu
from jax.sharding import PartitionSpec as P

META = 8
OWN, SIB, XN, YN = 0, 1, 2, 3
VMEM_LIMIT = 20 * 1024 * 1024


def dot_last(a, b):
    return lax.dot_general(a, b, (((1,), (1,)), ((), ())), preferred_element_type=jnp.float32)


def iota(shape, dim):
    return lax.broadcasted_iota(jnp.int32, shape, dim)


def as_column(row):
    n = row.shape[1]
    return jnp.sum(jnp.where(iota((n, n), 0) == iota((n, n), 1), row, 0.0), axis=1, keepdims=True)


def vmem_specs(count):
    return [pl.BlockSpec(memory_space=pltpu.VMEM)] * count


def pack_kernel(cap, groups, group_ref, sub_ref, scale_ref, codes_ref, *out_refs):
    chunk_refs, place_ref = out_refs[:groups], out_refs[groups]
    rows, width = codes_ref.shape
    hop = group_ref[...] ^ lax.axis_index("group")
    keys = iota((16, rows), 0)
    member = keys == hop * 2 + sub_ref[...]
    upto = (iota((rows, rows), 0) <= iota((rows, rows), 1)).astype(jnp.bfloat16)
    counts = jnp.dot(member.astype(jnp.bfloat16), upto, preferred_element_type=jnp.float32)
    totals = counts[:, rows - 1 : rows]
    before = jnp.concatenate([jnp.zeros((1, 1), jnp.float32), totals[:-1]], axis=0)
    base = jnp.where(keys % 2 == 1, before, 0.0) - 1.0
    rank = jnp.sum(jnp.where(member, counts + base, 0.0), axis=0, keepdims=True).astype(jnp.int32)
    place_ref[...] = jnp.concatenate([hop, rank] + [jnp.zeros_like(rank)] * 6, axis=0)
    scales = jnp.concatenate(
        [scale_ref[...], jnp.zeros((15, rows), jnp.float32)], axis=0
    ).astype(jnp.bfloat16)
    codes = codes_ref[...]
    for s in range(groups):
        pick = (iota((cap, rows), 0) == jnp.where(hop == s, rank, -1)).astype(jnp.bfloat16)
        chunk_refs[s][0:cap, :] = jnp.dot(pick, codes, preferred_element_type=jnp.float32).astype(
            jnp.bfloat16
        )
        first = jnp.broadcast_to(totals[2 * s : 2 * s + 1, :], (1, cap))
        both = first + totals[2 * s + 1 : 2 * s + 2, :]
        meta = jnp.concatenate(
            [dot_last(scales, pick)[0:1, :], first, both, jnp.zeros((META - 3, cap), jnp.float32)],
            axis=0,
        )
        chunk_refs[s][cap:, :] = jnp.concatenate(
            [meta, jnp.zeros((META, width - cap), jnp.float32)], axis=1
        ).astype(jnp.bfloat16)


def unit_kernel(cap, chunk_ref, cent_ref, out_ref):
    meta = chunk_ref[cap:, 0:cap].astype(jnp.float32)
    scale = as_column(meta[0:1, :])
    first = meta[1:2, 0:1].astype(jnp.int32)
    cent = cent_ref[...].astype(jnp.float32)
    centre = jnp.where(iota((cap, 1), 0) < first, cent[0:1, :], cent[1:2, :])
    vectors = centre + scale * chunk_ref[0:cap, :].astype(jnp.float32)
    norm = jnp.sqrt(jnp.sum(vectors * vectors, axis=1, keepdims=True) + 1e-06)
    out_ref[0:cap, :] = (vectors * (1.0 / norm)).astype(jnp.bfloat16)
    out_ref[cap:, :] = chunk_ref[cap:, :]


def score_kernel(cap, old, new, *refs):
    chunks = old + new
    count = len(chunks)
    data = [dict(zip(chunks, refs[block * count : (block + 1) * count])) for block in range(4)]
    rest = refs[4 * count :]
    best_refs = dict(zip((OWN, XN, YN), rest[-3:]))
    blk = lax.axis_index("blk")
    group_pos = lax.axis_index("group")
    core, x, y = blk % 2, (blk // 2) % 2, blk // 4
    row = iota((cap, cap), 0)
    lane = iota((1, cap), 1)
    if old:
        for block, ref in zip((OWN, XN, YN), rest[:3]):
            best_refs[block][...] = ref[...]
    else:
        for block in (OWN, XN, YN):
            best_refs[block][...] = jnp.full((4, cap), -1.0, jnp.float32)

    def sizes(block, at):
        meta = data[block][at][cap:, 0:cap].astype(jnp.float32).astype(jnp.int32)
        return meta[1:2, :], meta[2:3, :]

    def score(early, late):
        for late_at in chunks:
            late_first = lane < sizes(late, late_at)[0]
            best = best_refs[late][late_at : late_at + 1, :]
            for at in chunks if late_at in new else new:
                scores = dot_last(data[early][at][0:cap, :], data[late][late_at][0:cap, :])
                first, both = sizes(early, at)
                low = jnp.where(late_first, 0, first)
                high = jnp.where(late_first, first, both)
                if early == late:
                    if at == late_at:
                        high = jnp.minimum(high, lane)
                    else:
                        high = jnp.where((group_pos ^ at) < (group_pos ^ late_at), high, 0)
                kept = jnp.where((row >= low) & (row < high), scores, -1.0)
                best = jnp.maximum(best, jnp.max(kept, axis=0, keepdims=True))
            best_refs[late][late_at : late_at + 1, :] = best

    score(OWN, OWN)
    pl.when(x == 0)(lambda: score(OWN, XN))
    pl.when(x == 1)(lambda: score(XN, OWN))

    @pl.when(y == 0)
    def _():
        score(OWN, YN)
        score(XN, YN)

    @pl.when(y == 1)
    def _():
        score(YN, OWN)
        score(YN, XN)

    pl.when(core == 1)(lambda: score(SIB, OWN))


def split_kernel(own_ref, x_ref, y_ref, *out_refs):
    best = jnp.maximum(own_ref[...], jnp.maximum(x_ref[...], y_ref[...]))
    for s, ref in enumerate(out_refs):
        ref[...] = best[s : s + 1, :]


def restore_kernel(cap, groups, place_ref, *refs):
    parts, out_ref = refs[:groups], refs[groups]
    rows = place_ref.shape[1]
    hop, rank = place_ref[0:1, :], place_ref[1:2, :]
    total = jnp.zeros((16, rows), jnp.float32)
    for s in range(groups):
        value = parts[s][...]
        high = value.astype(jnp.bfloat16)
        rest = value - high.astype(jnp.float32)
        middle = rest.astype(jnp.bfloat16)
        low = rest - middle.astype(jnp.float32)
        stacked = jnp.concatenate(
            [high.astype(jnp.float32), middle.astype(jnp.float32), low]
            + [jnp.zeros((13, cap), jnp.float32)],
            axis=0,
        ).astype(jnp.bfloat16)
        pick = (iota((cap, rows), 0) == jnp.where(hop == s, rank, -1)).astype(jnp.bfloat16)
        total = total + jnp.dot(stacked, pick, preferred_element_type=jnp.float32)
    out_ref[...] = total[0:1, :] + (total[1:2, :] + total[2:3, :])


def blk_of(y, x, core):
    return (y * 2 + x) * 2 + core


def plane_pairs():
    to_x, to_y, to_sib = [], [], []
    for y in range(2):
        for x in range(2):
            for core in range(2):
                me = blk_of(y, x, core)
                to_x.append((blk_of(y, 1 - x, core ^ x ^ y), me))
                to_y.append((blk_of(1 - y, x, core ^ y), me))
            to_sib.append((blk_of(y, x, 0), blk_of(y, x, 1)))
    return to_x, to_y, to_sib


def reverse(pairs):
    return [(b, a) for a, b in pairs]


def after(value, *others):
    return lax.optimization_barrier((value,) + others)[0]


def score_call(cap, old, new, blocks, before, width):
    count = len(old) + len(new)
    arrays = [block[at] for block in blocks for at in old + new]
    pairs = 5 * (count * count - len(old) ** 2)
    return pl.pallas_call(
        functools.partial(score_kernel, cap, tuple(old), tuple(new)),
        out_shape=[jax.ShapeDtypeStruct((4, cap), jnp.float32)] * 3,
        in_specs=vmem_specs(4 * count + len(before)),
        out_specs=vmem_specs(3),
        compiler_params=pltpu.CompilerParams(vmem_limit_bytes=VMEM_LIMIT),
        cost_estimate=pl.CostEstimate(
            flops=2 * pairs * cap * cap * width,
            bytes_accessed=8 * count * cap * width,
            transcendentals=0,
        ),
    )(*arrays, *before)


def paired_shards(codes, row_scale, row_group, row_sub, centroids):
    row_count, width = codes.shape
    groups = lax.axis_size("group")
    cap = 3 * row_count // (2 * groups)
    params = pltpu.CompilerParams(vmem_limit_bytes=VMEM_LIMIT)
    chunk_shape = jax.ShapeDtypeStruct((cap + META, width), jnp.bfloat16)
    *packed, place = pl.pallas_call(
        functools.partial(pack_kernel, cap, groups),
        out_shape=[chunk_shape] * groups + [jax.ShapeDtypeStruct((8, row_count), jnp.int32)],
        in_specs=vmem_specs(4),
        out_specs=vmem_specs(groups + 1),
        compiler_params=params,
    )(
        row_group.reshape(1, row_count),
        row_sub.reshape(1, row_count),
        row_scale.astype(jnp.float32).reshape(1, row_count),
        codes,
    )
    hops = [[(g, g ^ s) for g in range(groups)] for s in range(groups)]
    unit_call = pl.pallas_call(
        functools.partial(unit_kernel, cap),
        out_shape=chunk_shape,
        in_specs=vmem_specs(2),
        out_specs=pl.BlockSpec(memory_space=pltpu.VMEM),
        compiler_params=params,
        cost_estimate=pl.CostEstimate(
            flops=8 * cap * width, bytes_accessed=4 * cap * width, transcendentals=0
        ),
    )
    to_x, to_y, to_sib = plane_pairs()
    blocks = [[None] * groups for _ in range(4)]

    def spread(s, chunk, sib_after=(), x_after=(), y_after=()):
        unit = unit_call(chunk, centroids)
        blocks[OWN][s] = unit
        blocks[SIB][s] = lax.ppermute(after(unit, *sib_after), "blk", to_sib)
        blocks[XN][s] = lax.ppermute(after(unit, *x_after), "blk", to_x)
        blocks[YN][s] = lax.ppermute(after(unit, *y_after), "blk", to_y)

    one = lax.ppermute(packed[1], "group", hops[1])
    two = lax.ppermute(packed[2], "group", hops[2])
    three = lax.ppermute(after(packed[3], one), "group", hops[3])
    spread(0, packed[0])
    _, sib0, x0, y0 = (block[0] for block in blocks)
    spread(1, one, [sib0], [x0], [y0])
    best0 = score_call(cap, [], [0], blocks, [], width)
    _, sib1, x1, y1 = (block[1] for block in blocks)
    spread(2, after(two, sib1, *best0), [x1, y1])
    best1 = score_call(cap, [0], [1], blocks, best0, width)
    spread(3, after(three, blocks[SIB][2], *best1))
    best2 = score_call(cap, [0, 1], [2], blocks, best1, width)
    best, for_x, for_y = score_call(cap, [0, 1, 2], [3], blocks, best2, width)
    returned = pl.pallas_call(
        split_kernel,
        out_shape=[jax.ShapeDtypeStruct((1, cap), jnp.float32)] * groups,
        in_specs=vmem_specs(3),
        out_specs=vmem_specs(groups),
        compiler_params=params,
    )(best, lax.ppermute(for_x, "blk", reverse(to_x)), lax.ppermute(for_y, "blk", reverse(to_y)))
    returned = [returned[0]] + [
        lax.ppermute(returned[s], "group", hops[s]) for s in range(1, groups)
    ]
    out = pl.pallas_call(
        functools.partial(restore_kernel, cap, groups),
        out_shape=jax.ShapeDtypeStruct((1, row_count), jnp.float32),
        in_specs=vmem_specs(groups + 1),
        out_specs=pl.BlockSpec(memory_space=pltpu.VMEM),
        compiler_params=params,
    )(place, *returned)
    return out.reshape(row_count)


def compare(best_sim, own_rows, own_order, own_sub, key_rows, key_order, key_sub):
    scores = jnp.einsum("qd,kd->qk", own_rows, key_rows, preferred_element_type=jnp.float32)
    allowed = (
        (key_sub[None, :] == own_sub[:, None])
        & (key_order[None, :] < own_order[:, None])
        & (key_order[None, :] > 0)
    )
    return jnp.maximum(best_sim, jnp.max(jnp.where(allowed, scores, -1.0), axis=1))


def gathered_shards(codes, row_scale, row_group, row_sub, centroids):
    row_count, width = codes.shape
    groups = lax.axis_size("group")
    capacity = 3 * row_count // (2 * groups)
    slot_count = groups * capacity
    cycle_pos = lax.axis_index("blk")
    group_pos = lax.axis_index("group")
    target = row_group[:, 0]
    member = (target[:, None] == jnp.arange(groups, dtype=jnp.int32)[None, :]).astype(jnp.int32)
    slot_rank = jnp.sum((jnp.cumsum(member, axis=0) - 1) * member, axis=1)
    placed = target * capacity + slot_rank
    row_order = (
        (cycle_pos * groups + group_pos) * row_count + jnp.arange(row_count, dtype=jnp.int32) + 1
    )

    def send(values):
        slots = jnp.zeros((slot_count,) + values.shape[1:], values.dtype).at[placed].set(values)
        return lax.all_to_all(
            slots.reshape((groups, capacity) + values.shape[1:]), "group", 0, 0, tiled=True
        )

    part_codes, part_scale = send(codes), send(row_scale)
    part_sub, part_order = send(row_sub), send(row_order)
    picks = (part_sub[..., None] == jnp.arange(centroids.shape[0], dtype=jnp.int32)).astype(
        jnp.bfloat16
    )
    centre = jnp.einsum("gnc,cd->gnd", picks, centroids, preferred_element_type=jnp.float32)
    vectors = centre + part_scale.astype(jnp.float32)[..., None] * part_codes.astype(jnp.float32)
    unit_part = (
        vectors / jnp.sqrt(jnp.sum(vectors * vectors, axis=-1, keepdims=True) + 1e-06)
    ).astype(jnp.bfloat16)
    own_rows = unit_part.reshape(slot_count, width)
    own_order = part_order.reshape(slot_count)
    own_sub = part_sub.reshape(slot_count)
    stacked = tuple(lax.all_gather(a, "blk", axis=0) for a in (own_rows, own_order, own_sub))

    def per_shard(carry, item):
        return compare(carry, own_rows, own_order, own_sub, *item), None

    start_sim = jnp.full((slot_count,), -1.0, jnp.float32)
    best_sim = lax.scan(per_shard, start_sim, stacked)[0]
    returned = lax.all_to_all(best_sim.reshape(groups, capacity), "group", 0, 0, tiled=True)
    return returned.reshape(-1)[placed]


def solution(mesh):
    paired = mesh.shape["blk"] == 8 and mesh.shape["group"] == 4
    return jax.shard_map(
        paired_shards if paired else gathered_shards,
        mesh=mesh,
        in_specs=(
            P(("blk", "group"), None),
            P(("blk", "group")),
            P(("blk", "group"), None),
            P(("blk", "group")),
            P("group", None),
        ),
        out_specs=P(("blk", "group")),
        check_vma=False,
    )
```

time: 91.2 us -> 82.8 us (0.908)
  starting transfers between devices: 36.7 us -> 29.7 us
  Pallas kernels: 18.8 us -> 15.1 us
  waiting for transfers between devices: 32.4 us -> 35 us
    ppermute x18, starting transfers between devices: 34.6 us -> 28.4 us  [the longest x4 7.62 us: spread(): blocks[SIB][s] = lax.ppermute(after(unit, *sib_after), 'blk', to_sib)]
    pallas_call x2 -> x4, Pallas kernels: 15.3 us -> 11.4 us  [score_call(): pl.pallas_call(functools.partial(score_kernel, cap, tuple(old), tuple(new...]
    ppermute x18, waiting for transfers between devices: 30.2 us -> 33.1 us  [the longest x1 14.1 us: paired_shards(): two = lax.ppermute(packed[2], 'group', hops[2])]
    ppermute x1, starting transfers between devices: 1.33 us -> 0.06 us  [paired_shards(): lax.ppermute(for_x, 'blk', reverse(to_x))]
    ppermute x1, waiting for transfers between devices: 1.27 us -> 0.07 us  [paired_shards(): lax.ppermute(for_y, 'blk', reverse(to_y))]
    unnamed x12 -> x8, local copies, waits for them, and re-layouts: 1.92 us -> 1.92 us
  transfers between devices with their start and end apart: 20 -> 20, of which waited for: 9 -> 10; matrix products, arithmetic and copies ran while one was open for 0% -> 0% of each run, Pallas kernels for 9% -> 10%
where the time goes in v2:
time: 82.8 us; the launch traced here: 82.6 us
  waiting for transfers between devices  35 us (42%)
  starting transfers between devices  29.7 us (36%)
  Pallas kernels  15.1 us (18%)
  local copies, waits for them, and re-layouts  1.92 us (2%)
    ppermute x1, waiting for transfers between devices, paired_shards(): two = lax.ppermute(packed[2], 'group', hops[2])  14.1 us
    pallas_call x4, Pallas kernels, score_call(): pl.pallas_call(functools.partial(score_kernel, cap, tuple(old), tuple(new...  11.4 us
    ppermute x4, starting transfers between devices, spread(): blocks[SIB][s] = lax.ppermute(after(unit, *sib_after), 'blk', to_sib)  7.62 us
    ppermute x1, waiting for transfers between devices, paired_shards(): one = lax.ppermute(packed[1], 'group', hops[1])  6.47 us
    ppermute x4, waiting for transfers between devices, spread(): blocks[XN][s] = lax.ppermute(after(unit, *x_after), 'blk', to_x)  5.33 us
    ppermute x4, starting transfers between devices, spread(): blocks[XN][s] = lax.ppermute(after(unit, *x_after), 'blk', to_x)  4.76 us
    ppermute x3, starting transfers between devices, paired_shards(): lax.ppermute(returned[s], 'group', hops[s])  4.44 us
    ppermute x3, waiting for transfers between devices, paired_shards(): lax.ppermute(returned[s], 'group', hops[s])  4 us
  transfers between devices with their start and end apart: 20, of which 10 were waited for; matrix products, arithmetic and copies ran while one was open for 0% of the time, Pallas kernels for 10%

profile of v2, /device:TPU:0, one launch (start us, length us, event | category | flops | bytes accessed | tf_op | source)
XLA Modules:
  0.0 82.6 jit_solution(13337352010158253135)
XLA Ops:
  0.0 0.7 reshape.19
  0.7 0.7 copy-done.3
  1.4 1.2 %copy-done = bf16[512,1024]{1,0:T(8,128)(2,1)S(1)} copy-done((bf16[512,1024]{1,0:T(8,128)(2,1)S(1)}, bf16[512,1024]{1,0:T(8,128)(2,1)}, u32[]{:S(2)}) %copy-start) | copy-done | bytes 1048600
  2.6 1.5 %shard_map.55 = (bf16[200,1024]{1,0:T(8,128)(2,1)S(1)}, bf16[200,1024]{1,0:T(8,128)(2,1)S(1)}, bf16[200,1024]{1,0:T(8,128)(2,1)S(1)}, bf16[200,1024]{1,0:T(8,128)(2,1)S(1)}, s32[8,512]{1,0:T(8,128)S(1)}) custom-call(s32[1,512]{1,0:T(1,128)S(1)} %bitcast.5, s32[1,512]{1,0:T(1,128)S(1)} %bitcast.6, f32[1,512]{1,0:T(1,128)S(1)} %bitcast.4, ...), custom_call_target="tpu_custom_call" | custom-call | tf_op jit(solution)/shard_map/pallas_call | solution.py:209
  4.1 3.1 %collective-permute-start = (bf16[200,1024]{1,0:T(8,128)(2,1)S(1)}, bf16[200,1024]{1,0:T(8,128)(2,1)S(1)}, u32[]{:S(2)}, u32[]{:S(2)}) collective-permute-start(bf16[200,1024]{1,0:T(8,128)(2,1)S(1)} %get-tuple-element.35), channel_id=1, source_target_pairs={{0,1},{1,0},{2,3},{3,2},{4,5},{5,4},{6,7},{7,6},{8,9},{9,8},{10,11... | collective-permute-start | bytes 1228808 | tf_op jit(solution)/shard_map/ppermute | solution.py:242
  7.5 1.5 %collective-permute-start.2 = (bf16[200,1024]{1,0:T(8,128)(2,1)S(1)}, bf16[200,1024]{1,0:T(8,128)(2,1)S(1)}, u32[]{:S(2)}, u32[]{:S(2)}) collective-permute-start(bf16[200,1024]{1,0:T(8,128)(2,1)S(1)} %shard_map.56.refs_0_), channel_id=1, source_target_pairs={{0,4},{8,12},{16,20},{24,28},{1,5},{9,13},{17,21},{25,29},{2,6},{1... | collective-permute-start | bytes 1228808 | tf_op jit(solution)/shard_map/ppermute | solution.py:238
  9.6 2.2 %collective-permute-start.4 = (bf16[200,1024]{1,0:T(8,128)(2,1)S(1)}, bf16[200,1024]{1,0:T(8,128)(2,1)S(1)}, u32[]{:S(2)}, u32[]{:S(2)}) collective-permute-start(bf16[200,1024]{1,0:T(8,128)(2,1)S(1)} %shard_map.56.refs_0_), channel_id=1, source_target_pairs={{8,0},{12,4},{4,8},{0,12},{28,16},{24,20},{16,24},{20,28},{9,1},{1... | collective-permute-start | bytes 1228808 | tf_op jit(solution)/shard_map/ppermute | solution.py:239
  11.8 2.6 %collective-permute-start.1 = (bf16[200,1024]{1,0:T(8,128)(2,1)S(1)}, bf16[200,1024]{1,0:T(8,128)(2,1)S(1)}, u32[]{:S(2)}, u32[]{:S(2)}) collective-permute-start(bf16[200,1024]{1,0:T(8,128)(2,1)S(1)} %get-tuple-element.36), channel_id=1, source_target_pairs={{0,2},{1,3},{2,0},{3,1},{4,6},{5,7},{6,4},{7,5},{8,10},{9,11},{10,... | collective-permute-start | bytes 1228808 | tf_op jit(solution)/shard_map/ppermute | solution.py:243
  14.4 6.5 %collective-permute-done.chunk_ref = bf16[200,1024]{1,0:T(8,128)(2,1)S(1)} collective-permute-done((bf16[200,1024]{1,0:T(8,128)(2,1)S(1)}, bf16[200,1024]{1,0:T(8,128)(2,1)S(1)}, u32[]{:S(2)}, u32[]{:S(2)}) %collective-permute-start) | collective-permute-done | bytes 409632 | tf_op jit(solution)/shard_map/ppermute | solution.py:242
  21.2 1.3 %collective-permute-start.3 = (bf16[200,1024]{1,0:T(8,128)(2,1)S(1)}, bf16[200,1024]{1,0:T(8,128)(2,1)S(1)}, u32[]{:S(2)}, u32[]{:S(2)}) collective-permute-start(bf16[200,1024]{1,0:T(8,128)(2,1)S(1)} %shard_map.57.refs_1_), channel_id=1, source_target_pairs={{0,4},{8,12},{16,20},{24,28},{1,5},{9,13},{17,21},{25,29},{2,6},{1... | collective-permute-start | bytes 1228808 | tf_op jit(solution)/shard_map/ppermute | solution.py:238
  22.9 2.1 %collective-permute-start.8 = (bf16[200,1024]{1,0:T(8,128)(2,1)S(1)}, bf16[200,1024]{1,0:T(8,128)(2,1)S(1)}, u32[]{:S(2)}, u32[]{:S(2)}) collective-permute-start(bf16[200,1024]{1,0:T(8,128)(2,1)S(1)} %shard_map.57.refs_1_), channel_id=1, source_target_pairs={{16,0},{20,4},{24,8},{28,12},{4,16},{0,20},{12,24},{8,28},{17,1},{... | collective-permute-start | bytes 1228808 | tf_op jit(solution)/shard_map/ppermute | solution.py:240
  25.0 2.5 %collective-permute-start.6 = (bf16[200,1024]{1,0:T(8,128)(2,1)S(1)}, bf16[200,1024]{1,0:T(8,128)(2,1)S(1)}, u32[]{:S(2)}, u32[]{:S(2)}) collective-permute-start(bf16[200,1024]{1,0:T(8,128)(2,1)S(1)} %get-tuple-element.43), channel_id=1, source_target_pairs={{0,3},{1,2},{2,1},{3,0},{4,7},{5,6},{6,5},{7,4},{8,11},{9,10},{10,... | collective-permute-start | bytes 1228808 | tf_op jit(solution)/shard_map/ppermute | solution.py:244
  27.5 1.0 %shard_map.58 = (f32[4,192]{1,0:T(4,128)S(1)}, f32[4,192]{1,0:T(4,128)S(1)}, f32[4,192]{1,0:T(4,128)S(1)}) custom-call(bf16[200,1024]{1,0:T(8,128)(2,1)S(1)} %shard_map.56.refs_0_, bf16[200,1024]{1,0:T(8,128)(2,1)S(1)} %collective-permute-done.2.refs_1_.refs_2_.refs_3_.refs_4_, bf16[200,1024]{1,0:T(8,128)(2,1)S(1)} %collective-permute-done.4.refs_2_.refs_4_.refs_6_.refs_8_, ...), custom_call_target="tpu_custom_call" | custom-call | flops 377487360 | bytes 1572864 | tf_op jit(solution)/shard_map/pallas_call | solution.py:189
  28.5 14.1 %collective-permute-done.1.chunk_ref = bf16[200,1024]{1,0:T(8,128)(2,1)S(1)} collective-permute-done((bf16[200,1024]{1,0:T(8,128)(2,1)S(1)}, bf16[200,1024]{1,0:T(8,128)(2,1)S(1)}, u32[]{:S(2)}, u32[]{:S(2)}) %collective-permute-start.1) | collective-permute-done | bytes 409632 | tf_op jit(solution)/shard_map/ppermute | solution.py:243
  43.1 1.3 %collective-permute-start.9 = (bf16[200,1024]{1,0:T(8,128)(2,1)S(1)}, bf16[200,1024]{1,0:T(8,128)(2,1)S(1)}, u32[]{:S(2)}, u32[]{:S(2)}) collective-permute-start(bf16[200,1024]{1,0:T(8,128)(2,1)S(1)} %shard_map.59.refs_2_), channel_id=1, source_target_pairs={{0,4},{8,12},{16,20},{24,28},{1,5},{9,13},{17,21},{25,29},{2,6},{1... | collective-permute-start | bytes 1228808 | tf_op jit(solution)/shard_map/ppermute | solution.py:238
  44.5 0.6 collective-permute-start.11
  45.0 2.2 %shard_map.60 = (f32[4,192]{1,0:T(4,128)S(1)}, f32[4,192]{1,0:T(4,128)S(1)}, f32[4,192]{1,0:T(4,128)S(1)}) custom-call(bf16[200,1024]{1,0:T(8,128)(2,1)S(1)} %shard_map.56.refs_0_, bf16[200,1024]{1,0:T(8,128)(2,1)S(1)} %shard_map.57.refs_1_, bf16[200,1024]{1,0:T(8,128)(2,1)S(1)} %collective-permute-done.2.refs_1_.refs_2_.refs_3_.refs_4_, ...), custom_call_target="tpu_custom_call" | custom-call | flops 1132462080 | bytes 3145728 | tf_op jit(solution)/shard_map/pallas_call | solution.py:189
  47.6 0.8 collective-permute-start.14
  48.4 1.6 %collective-permute-start.12 = (bf16[200,1024]{1,0:T(8,128)(2,1)S(1)}, bf16[200,1024]{1,0:T(8,128)(2,1)S(1)}, u32[]{:S(2)}, u32[]{:S(2)}) collective-permute-start(bf16[200,1024]{1,0:T(8,128)(2,1)S(1)} %shard_map.61.refs_3_), channel_id=1, source_target_pairs={{8,0},{12,4},{4,8},{0,12},{28,16},{24,20},{16,24},{20,28},{9,1},{1... | collective-permute-start | bytes 1228808 | tf_op jit(solution)/shard_map/ppermute | solution.py:239
  50.0 3.5 %collective-permute-start.10 = (bf16[200,1024]{1,0:T(8,128)(2,1)S(1)}, bf16[200,1024]{1,0:T(8,128)(2,1)S(1)}, u32[]{:S(2)}, u32[]{:S(2)}) collective-permute-start(bf16[200,1024]{1,0:T(8,128)(2,1)S(1)} %shard_map.61.refs_3_), channel_id=1, source_target_pairs={{0,4},{8,12},{16,20},{24,28},{1,5},{9,13},{17,21},{25,29},{2,6},{1... | collective-permute-start | bytes 1228808 | tf_op jit(solution)/shard_map/ppermute | solution.py:238
  53.5 0.7 collective-permute-done.13.refs_11_.refs_14_
  54.1 2.7 %collective-permute-done.11.refs_8_.refs_10_ = bf16[200,1024]{1,0:T(8,128)(2,1)S(1)} collective-permute-done((bf16[200,1024]{1,0:T(8,128)(2,1)S(1)}, bf16[200,1024]{1,0:T(8,128)(2,1)S(1)}, u32[]{:S(2)}, u32[]{:S(2)}) %collective-permute-start.11) | collective-permute-done | bytes 409632 | tf_op jit(solution)/shard_map/ppermute | solution.py:239
  56.8 3.6 %shard_map.62 = (f32[4,192]{1,0:T(4,128)S(1)}, f32[4,192]{1,0:T(4,128)S(1)}, f32[4,192]{1,0:T(4,128)S(1)}) custom-call(bf16[200,1024]{1,0:T(8,128)(2,1)S(1)} %shard_map.56.refs_0_, bf16[200,1024]{1,0:T(8,128)(2,1)S(1)} %shard_map.57.refs_1_, bf16[200,1024]{1,0:T(8,128)(2,1)S(1)} %shard_map.59.refs_2_, ...), custom_call_target="tpu_custom_call" | custom-call | flops 1887436800 | bytes 4718592 | tf_op jit(solution)/shard_map/pallas_call | solution.py:189
  60.4 2.5 %collective-permute-done.14.refs_15_ = bf16[200,1024]{1,0:T(8,128)(2,1)S(1)} collective-permute-done((bf16[200,1024]{1,0:T(8,128)(2,1)S(1)}, bf16[200,1024]{1,0:T(8,128)(2,1)S(1)}, u32[]{:S(2)}, u32[]{:S(2)}) %collective-permute-start.14) | collective-permute-done | bytes 409632 | tf_op jit(solution)/shard_map/ppermute | solution.py:240
  62.9 2.6 %collective-permute-done.12.refs_11_ = bf16[200,1024]{1,0:T(8,128)(2,1)S(1)} collective-permute-done((bf16[200,1024]{1,0:T(8,128)(2,1)S(1)}, bf16[200,1024]{1,0:T(8,128)(2,1)S(1)}, u32[]{:S(2)}, u32[]{:S(2)}) %collective-permute-start.12) | collective-permute-done | bytes 409632 | tf_op jit(solution)/shard_map/ppermute | solution.py:239
  65.5 4.6 %shard_map.63 = (f32[4,192]{1,0:T(4,128)S(1)}, f32[4,192]{1,0:T(4,128)S(1)}, f32[4,192]{1,0:T(4,128)S(1)}) custom-call(bf16[200,1024]{1,0:T(8,128)(2,1)S(1)} %shard_map.56.refs_0_, bf16[200,1024]{1,0:T(8,128)(2,1)S(1)} %shard_map.57.refs_1_, bf16[200,1024]{1,0:T(8,128)(2,1)S(1)} %shard_map.59.refs_2_, bf16[200,1024]{1,0:T(8,128)(2,1)S(1)} %shard_map.61.refs_3_, ...), custom_call_target="tpu_custom_call" | custom-call | flops 2642411520 | bytes 6291456 | tf_op jit(solution)/shard_map/pallas_call | solution.py:189
  70.2 1.2 %collective-permute-start.16 = (f32[4,192]{1,0:T(4,128)S(1)}, f32[4,192]{1,0:T(4,128)S(1)}, u32[]{:S(2)}, u32[]{:S(2)}) collective-permute-start(f32[4,192]{1,0:T(4,128)S(1)} %get-tuple-element.56), channel_id=1, source_target_pairs={{0,16},{4,20},{8,24},{12,28},{16,4},{20,0},{24,12},{28,8},{1,17},{... | collective-permute-start | bytes 9224 | tf_op jit(solution)/shard_map/ppermute | solution.py:261
  71.4 1.8 %collective-permute-done.15.x_ref = f32[4,192]{1,0:T(4,128)S(1)} collective-permute-done((f32[4,192]{1,0:T(4,128)S(1)}, f32[4,192]{1,0:T(4,128)S(1)}, u32[]{:S(2)}, u32[]{:S(2)}) %collective-permute-start.15) | collective-permute-done | bytes 3104 | tf_op jit(solution)/shard_map/ppermute | solution.py:261
  73.3 3.0 %collective-permute-start.18 = (f32[1,192]{1,0:T(1,128)S(1)}, f32[1,192]{1,0:T(1,128)S(1)}, u32[]{:S(2)}, u32[]{:S(2)}) collective-permute-start(f32[1,192]{1,0:T(1,128)S(1)} %get-tuple-element.59), channel_id=1, source_target_pairs={{0,2},{1,3},{2,0},{3,1},{4,6},{5,7},{6,4},{7,5},{8,10},{9,11},{10,... | collective-permute-start | bytes 2312 | tf_op jit(solution)/shard_map/ppermute | solution.py:263
  76.3 1.4 %collective-permute-start.19 = (f32[1,192]{1,0:T(1,128)S(1)}, f32[1,192]{1,0:T(1,128)S(1)}, u32[]{:S(2)}, u32[]{:S(2)}) collective-permute-start(f32[1,192]{1,0:T(1,128)S(1)} %get-tuple-element.60), channel_id=1, source_target_pairs={{0,3},{1,2},{2,1},{3,0},{4,7},{5,6},{6,5},{7,4},{8,11},{9,10},{10,... | collective-permute-start | bytes 2312 | tf_op jit(solution)/shard_map/ppermute | solution.py:263
  77.9 3.8 %collective-permute-done.19.refs_3_ = f32[1,192]{1,0:T(1,128)S(1)} collective-permute-done((f32[1,192]{1,0:T(1,128)S(1)}, f32[1,192]{1,0:T(1,128)S(1)}, u32[]{:S(2)}, u32[]{:S(2)}) %collective-permute-start.19) | collective-permute-done | bytes 800 | tf_op jit(solution)/shard_map/ppermute | solution.py:263
  81.7 0.8 %shard_map.65 = f32[1,512]{1,0:T(1,128)} custom-call(s32[8,512]{1,0:T(8,128)S(1)} %get-tuple-element.33.place_ref, f32[1,192]{1,0:T(1,128)S(1)} %get-tuple-element.57.refs_0_, f32[1,192]{1,0:T(1,128)S(1)} %collective-permute-done.17.refs_1_, f32[1,192]{1,0:T(1,128)S(1)} %collective-permute-done.18.refs_2_, f32[1,192]{1,0:T(1,128)S(1)} %collective-permute-done.19.refs_3_), custom_call_target="tpu_custom_call" | custom-call | tf_op jit(solution)/shard_map/pallas_call | solution.py:265
  (28 shorter events, 2.8 us)
Async XLA Ops:
  0.7 0.7 copy-start.3
  0.7 0.7 copy-start.2
  1.4 1.2 %copy-start = (bf16[512,1024]{1,0:T(8,128)(2,1)S(1)}, bf16[512,1024]{1,0:T(8,128)(2,1)}, u32[]{:S(2)}) copy-start(bf16[512,1024]{1,0:T(8,128)(2,1)} %codes_ref.1) | copy-start | bytes 3145732
  2.6 4.6 %copy-start.1 = (bf16[2,1024]{1,0:T(2,128)(2,1)S(1)}, bf16[2,1024]{1,0:T(2,128)(2,1)}, u32[]{:S(2)}) copy-start(bf16[2,1024]{1,0:T(2,128)(2,1)} %cent_ref.7) | copy-start | bytes 12292
  4.1 16.8 %collective-permute-start = (bf16[200,1024]{1,0:T(8,128)(2,1)S(1)}, bf16[200,1024]{1,0:T(8,128)(2,1)S(1)}, u32[]{:S(2)}, u32[]{:S(2)}) collective-permute-start(bf16[200,1024]{1,0:T(8,128)(2,1)S(1)} %get-tuple-element.35), channel_id=1, source_target_pairs={{0,1},{1,0},{2,3},{3,2},{4,5},{5,4},{6,7},{7,6},{8,9},{9,8},{10,11... | collective-permute-start | bytes 1228808 | tf_op jit(solution)/shard_map/ppermute | solution.py:242
  7.5 13.7 %collective-permute-start.2 = (bf16[200,1024]{1,0:T(8,128)(2,1)S(1)}, bf16[200,1024]{1,0:T(8,128)(2,1)S(1)}, u32[]{:S(2)}, u32[]{:S(2)}) collective-permute-start(bf16[200,1024]{1,0:T(8,128)(2,1)S(1)} %shard_map.56.refs_0_), channel_id=1, source_target_pairs={{0,4},{8,12},{16,20},{24,28},{1,5},{9,13},{17,21},{25,29},{2,6},{1... | collective-permute-start | bytes 1228808 | tf_op jit(solution)/shard_map/ppermute | solution.py:238
  9.0 13.5 %collective-permute-start.5 = (bf16[200,1024]{1,0:T(8,128)(2,1)S(1)}, bf16[200,1024]{1,0:T(8,128)(2,1)S(1)}, u32[]{:S(2)}, u32[]{:S(2)}) collective-permute-start(bf16[200,1024]{1,0:T(8,128)(2,1)S(1)} %shard_map.56.refs_0_), channel_id=1, source_target_pairs={{16,0},{20,4},{24,8},{28,12},{4,16},{0,20},{12,24},{8,28},{17,1},{... | collective-permute-start | bytes 1228808 | tf_op jit(solution)/shard_map/ppermute | solution.py:240
  9.6 13.0 %collective-permute-start.4 = (bf16[200,1024]{1,0:T(8,128)(2,1)S(1)}, bf16[200,1024]{1,0:T(8,128)(2,1)S(1)}, u32[]{:S(2)}, u32[]{:S(2)}) collective-permute-start(bf16[200,1024]{1,0:T(8,128)(2,1)S(1)} %shard_map.56.refs_0_), channel_id=1, source_target_pairs={{8,0},{12,4},{4,8},{0,12},{28,16},{24,20},{16,24},{20,28},{9,1},{1... | collective-permute-start | bytes 1228808 | tf_op jit(solution)/shard_map/ppermute | solution.py:239
  11.8 30.9 %collective-permute-start.1 = (bf16[200,1024]{1,0:T(8,128)(2,1)S(1)}, bf16[200,1024]{1,0:T(8,128)(2,1)S(1)}, u32[]{:S(2)}, u32[]{:S(2)}) collective-permute-start(bf16[200,1024]{1,0:T(8,128)(2,1)S(1)} %get-tuple-element.36), channel_id=1, source_target_pairs={{0,2},{1,3},{2,0},{3,1},{4,6},{5,7},{6,4},{7,5},{8,10},{9,11},{10,... | collective-permute-start | bytes 1228808 | tf_op jit(solution)/shard_map/ppermute | solution.py:243
  21.2 21.4 %collective-permute-start.3 = (bf16[200,1024]{1,0:T(8,128)(2,1)S(1)}, bf16[200,1024]{1,0:T(8,128)(2,1)S(1)}, u32[]{:S(2)}, u32[]{:S(2)}) collective-permute-start(bf16[200,1024]{1,0:T(8,128)(2,1)S(1)} %shard_map.57.refs_1_), channel_id=1, source_target_pairs={{0,4},{8,12},{16,20},{24,28},{1,5},{9,13},{17,21},{25,29},{2,6},{1... | collective-permute-start | bytes 1228808 | tf_op jit(solution)/shard_map/ppermute | solution.py:238
  22.6 20.5 %collective-permute-start.7 = (bf16[200,1024]{1,0:T(8,128)(2,1)S(1)}, bf16[200,1024]{1,0:T(8,128)(2,1)S(1)}, u32[]{:S(2)}, u32[]{:S(2)}) collective-permute-start(bf16[200,1024]{1,0:T(8,128)(2,1)S(1)} %shard_map.57.refs_1_), channel_id=1, source_target_pairs={{8,0},{12,4},{4,8},{0,12},{28,16},{24,20},{16,24},{20,28},{9,1},{1... | collective-permute-start | bytes 1228808 | tf_op jit(solution)/shard_map/ppermute | solution.py:239
  22.9 20.1 %collective-permute-start.8 = (bf16[200,1024]{1,0:T(8,128)(2,1)S(1)}, bf16[200,1024]{1,0:T(8,128)(2,1)S(1)}, u32[]{:S(2)}, u32[]{:S(2)}) collective-permute-start(bf16[200,1024]{1,0:T(8,128)(2,1)S(1)} %shard_map.57.refs_1_), channel_id=1, source_target_pairs={{16,0},{20,4},{24,8},{28,12},{4,16},{0,20},{12,24},{8,28},{17,1},{... | collective-permute-start | bytes 1228808 | tf_op jit(solution)/shard_map/ppermute | solution.py:240
  25.0 22.2 %collective-permute-start.6 = (bf16[200,1024]{1,0:T(8,128)(2,1)S(1)}, bf16[200,1024]{1,0:T(8,128)(2,1)S(1)}, u32[]{:S(2)}, u32[]{:S(2)}) collective-permute-start(bf16[200,1024]{1,0:T(8,128)(2,1)S(1)} %get-tuple-element.43), channel_id=1, source_target_pairs={{0,3},{1,2},{2,1},{3,0},{4,7},{5,6},{6,5},{7,4},{8,11},{9,10},{10,... | collective-permute-start | bytes 1228808 | tf_op jit(solution)/shard_map/ppermute | solution.py:244
  43.1 4.2 %collective-permute-start.9 = (bf16[200,1024]{1,0:T(8,128)(2,1)S(1)}, bf16[200,1024]{1,0:T(8,128)(2,1)S(1)}, u32[]{:S(2)}, u32[]{:S(2)}) collective-permute-start(bf16[200,1024]{1,0:T(8,128)(2,1)S(1)} %shard_map.59.refs_2_), channel_id=1, source_target_pairs={{0,4},{8,12},{16,20},{24,28},{1,5},{9,13},{17,21},{25,29},{2,6},{1... | collective-permute-start | bytes 1228808 | tf_op jit(solution)/shard_map/ppermute | solution.py:238
  44.4 9.7 %collective-permute-start.13 = (bf16[200,1024]{1,0:T(8,128)(2,1)S(1)}, bf16[200,1024]{1,0:T(8,128)(2,1)S(1)}, u32[]{:S(2)}, u32[]{:S(2)}) collective-permute-start(bf16[200,1024]{1,0:T(8,128)(2,1)S(1)} %shard_map.59.refs_2_), channel_id=1, source_target_pairs={{16,0},{20,4},{24,8},{28,12},{4,16},{0,20},{12,24},{8,28},{17,1},{... | collective-permute-start | bytes 1228808 | tf_op jit(solution)/shard_map/ppermute | solution.py:240
  44.5 12.4 %collective-permute-start.11 = (bf16[200,1024]{1,0:T(8,128)(2,1)S(1)}, bf16[200,1024]{1,0:T(8,128)(2,1)S(1)}, u32[]{:S(2)}, u32[]{:S(2)}) collective-permute-start(bf16[200,1024]{1,0:T(8,128)(2,1)S(1)} %shard_map.59.refs_2_), channel_id=1, source_target_pairs={{8,0},{12,4},{4,8},{0,12},{28,16},{24,20},{16,24},{20,28},{9,1},{1... | collective-permute-start | bytes 1228808 | tf_op jit(solution)/shard_map/ppermute | solution.py:239
  47.6 15.3 %collective-permute-start.14 = (bf16[200,1024]{1,0:T(8,128)(2,1)S(1)}, bf16[200,1024]{1,0:T(8,128)(2,1)S(1)}, u32[]{:S(2)}, u32[]{:S(2)}) collective-permute-start(bf16[200,1024]{1,0:T(8,128)(2,1)S(1)} %shard_map.61.refs_3_), channel_id=1, source_target_pairs={{16,0},{20,4},{24,8},{28,12},{4,16},{0,20},{12,24},{8,28},{17,1},{... | collective-permute-start | bytes 1228808 | tf_op jit(solution)/shard_map/ppermute | solution.py:240
  48.4 17.1 %collective-permute-start.12 = (bf16[200,1024]{1,0:T(8,128)(2,1)S(1)}, bf16[200,1024]{1,0:T(8,128)(2,1)S(1)}, u32[]{:S(2)}, u32[]{:S(2)}) collective-permute-start(bf16[200,1024]{1,0:T(8,128)(2,1)S(1)} %shard_map.61.refs_3_), channel_id=1, source_target_pairs={{8,0},{12,4},{4,8},{0,12},{28,16},{24,20},{16,24},{20,28},{9,1},{1... | collective-permute-start | bytes 1228808 | tf_op jit(solution)/shard_map/ppermute | solution.py:239
  50.0 15.5 %collective-permute-start.10 = (bf16[200,1024]{1,0:T(8,128)(2,1)S(1)}, bf16[200,1024]{1,0:T(8,128)(2,1)S(1)}, u32[]{:S(2)}, u32[]{:S(2)}) collective-permute-start(bf16[200,1024]{1,0:T(8,128)(2,1)S(1)} %shard_map.61.refs_3_), channel_id=1, source_target_pairs={{0,4},{8,12},{16,20},{24,28},{1,5},{9,13},{17,21},{25,29},{2,6},{1... | collective-permute-start | bytes 1228808 | tf_op jit(solution)/shard_map/ppermute | solution.py:238
  70.1 3.1 %collective-permute-start.15 = (f32[4,192]{1,0:T(4,128)S(1)}, f32[4,192]{1,0:T(4,128)S(1)}, u32[]{:S(2)}, u32[]{:S(2)}) collective-permute-start(f32[4,192]{1,0:T(4,128)S(1)} %get-tuple-element.55), channel_id=1, source_target_pairs={{0,8},{4,12},{8,4},{12,0},{16,28},{20,24},{24,16},{28,20},{1,9},{5... | collective-permute-start | bytes 9224 | tf_op jit(solution)/shard_map/ppermute | solution.py:261
  70.2 3.1 %collective-permute-start.16 = (f32[4,192]{1,0:T(4,128)S(1)}, f32[4,192]{1,0:T(4,128)S(1)}, u32[]{:S(2)}, u32[]{:S(2)}) collective-permute-start(f32[4,192]{1,0:T(4,128)S(1)} %get-tuple-element.56), channel_id=1, source_target_pairs={{0,16},{4,20},{8,24},{12,28},{16,4},{20,0},{24,12},{28,8},{1,17},{... | collective-permute-start | bytes 9224 | tf_op jit(solution)/shard_map/ppermute | solution.py:261
  73.3 4.4 %collective-permute-start.17 = (f32[1,192]{1,0:T(1,128)S(1)}, f32[1,192]{1,0:T(1,128)S(1)}, u32[]{:S(2)}, u32[]{:S(2)}) collective-permute-start(f32[1,192]{1,0:T(1,128)S(1)} %get-tuple-element.58), channel_id=1, source_target_pairs={{0,1},{1,0},{2,3},{3,2},{4,5},{5,4},{6,7},{7,6},{8,9},{9,8},{10,11... | collective-permute-start | bytes 2312 | tf_op jit(solution)/shard_map/ppermute | solution.py:263
  73.3 4.6 %collective-permute-start.18 = (f32[1,192]{1,0:T(1,128)S(1)}, f32[1,192]{1,0:T(1,128)S(1)}, u32[]{:S(2)}, u32[]{:S(2)}) collective-permute-start(f32[1,192]{1,0:T(1,128)S(1)} %get-tuple-element.59), channel_id=1, source_target_pairs={{0,2},{1,3},{2,0},{3,1},{4,6},{5,7},{6,4},{7,5},{8,10},{9,11},{10,... | collective-permute-start | bytes 2312 | tf_op jit(solution)/shard_map/ppermute | solution.py:263
  76.3 5.4 %collective-permute-start.19 = (f32[1,192]{1,0:T(1,128)S(1)}, f32[1,192]{1,0:T(1,128)S(1)}, u32[]{:S(2)}, u32[]{:S(2)}) collective-permute-start(f32[1,192]{1,0:T(1,128)S(1)} %get-tuple-element.60), channel_id=1, source_target_pairs={{0,3},{1,2},{2,1},{3,0},{4,7},{5,6},{6,5},{7,4},{8,11},{9,10},{10,... | collective-permute-start | bytes 2312 | tf_op jit(solution)/shard_map/ppermute | solution.py:263

commit v3 on v2

--- a/solution.py
+++ b/solution.py
@@ -10,6 +10,7 @@
 META = 8
 OWN, SIB, XN, YN = 0, 1, 2, 3
 VMEM_LIMIT = 20 * 1024 * 1024
+COST = pl.CostEstimate(flops=1, bytes_accessed=1, transcendentals=0)
 
 
 def dot_last(a, b):
@@ -29,8 +30,8 @@
     return [pl.BlockSpec(memory_space=pltpu.VMEM)] * count
 
 
-def pack_kernel(cap, groups, group_ref, sub_ref, scale_ref, codes_ref, *out_refs):
-    chunk_refs, place_ref = out_refs[:groups], out_refs[groups]
+def pack_kernel(cap, group_ref, sub_ref, scale_ref, codes_ref, *out_refs):
+    chunk_refs, place_ref = out_refs[:-1], out_refs[-1]
     rows, width = codes_ref.shape
     hop = group_ref[...] ^ lax.axis_index("group")
     keys = iota((16, rows), 0)
@@ -46,9 +47,9 @@
         [scale_ref[...], jnp.zeros((15, rows), jnp.float32)], axis=0
     ).astype(jnp.bfloat16)
     codes = codes_ref[...]
-    for s in range(groups):
+    for s, ref in enumerate(chunk_refs):
         pick = (iota((cap, rows), 0) == jnp.where(hop == s, rank, -1)).astype(jnp.bfloat16)
-        chunk_refs[s][0:cap, :] = jnp.dot(pick, codes, preferred_element_type=jnp.float32).astype(
+        ref[0:cap, :] = jnp.dot(pick, codes, preferred_element_type=jnp.float32).astype(
             jnp.bfloat16
         )
         first = jnp.broadcast_to(totals[2 * s : 2 * s + 1, :], (1, cap))
@@ -57,64 +58,89 @@
             [dot_last(scales, pick)[0:1, :], first, both, jnp.zeros((META - 3, cap), jnp.float32)],
             axis=0,
         )
-        chunk_refs[s][cap:, :] = jnp.concatenate(
+        ref[cap:, :] = jnp.concatenate(
             [meta, jnp.zeros((META, width - cap), jnp.float32)], axis=1
         ).astype(jnp.bfloat16)
 
 
-def unit_kernel(cap, chunk_ref, cent_ref, out_ref):
-    meta = chunk_ref[cap:, 0:cap].astype(jnp.float32)
-    scale = as_column(meta[0:1, :])
-    first = meta[1:2, 0:1].astype(jnp.int32)
+def unit_kernel(cap, *refs):
+    chunk_refs, cent_ref, out_ref = refs[:-2], refs[-2], refs[-1]
+    count = len(chunk_refs)
     cent = cent_ref[...].astype(jnp.float32)
-    centre = jnp.where(iota((cap, 1), 0) < first, cent[0:1, :], cent[1:2, :])
-    vectors = centre + scale * chunk_ref[0:cap, :].astype(jnp.float32)
-    norm = jnp.sqrt(jnp.sum(vectors * vectors, axis=1, keepdims=True) + 1e-06)
-    out_ref[0:cap, :] = (vectors * (1.0 / norm)).astype(jnp.bfloat16)
-    out_ref[cap:, :] = chunk_ref[cap:, :]
-
-
-def score_kernel(cap, old, new, *refs):
-    chunks = old + new
-    count = len(chunks)
-    data = [dict(zip(chunks, refs[block * count : (block + 1) * count])) for block in range(4)]
-    rest = refs[4 * count :]
+    for at, ref in enumerate(chunk_refs):
+        meta = ref[cap:, 0:cap].astype(jnp.float32)
+        scale = as_column(meta[0:1, :])
+        first = meta[1:2, 0:1].astype(jnp.int32)
+        centre = jnp.where(iota((cap, 1), 0) < first, cent[0:1, :], cent[1:2, :])
+        vectors = centre + scale * ref[0:cap, :].astype(jnp.float32)
+        norm = jnp.sqrt(jnp.sum(vectors * vectors, axis=1, keepdims=True) + 1e-06)
+        out_ref[at * cap : (at + 1) * cap, :] = (vectors * (1.0 / norm)).astype(jnp.bfloat16)
+        start = count * cap + at * META
+        out_ref[start : start + META, :] = ref[cap:, :]
+
+
+def blocks_used(inner, outer):
+    return (OWN,) + (SIB,) * inner + (XN, YN) * outer
+
+
+def score_kernel(cap, old, new, inner, outer, *refs):
+    parts = old + new
+    chunks = sum(parts, ())
+    fresh = sum(new, ())
+    used = blocks_used(inner, outer)
+    arrays = {
+        (block, part): refs[at * len(parts) + which]
+        for at, block in enumerate(used)
+        for which, part in enumerate(parts)
+    }
+    part_of = {chunk: part for part in parts for chunk in part}
+    rest = refs[len(arrays) :]
     best_refs = dict(zip((OWN, XN, YN), rest[-3:]))
     blk = lax.axis_index("blk")
     group_pos = lax.axis_index("group")
     core, x, y = blk % 2, (blk // 2) % 2, blk // 4
-    row = iota((cap, cap), 0)
-    lane = iota((1, cap), 1)
-    if old:
+    row, lane = iota((cap, cap), 0), iota((1, cap), 1)
+    if len(rest) > 3:
         for block, ref in zip((OWN, XN, YN), rest[:3]):
             best_refs[block][...] = ref[...]
     else:
         for block in (OWN, XN, YN):
             best_refs[block][...] = jnp.full((4, cap), -1.0, jnp.float32)
 
-    def sizes(block, at):
-        meta = data[block][at][cap:, 0:cap].astype(jnp.float32).astype(jnp.int32)
+    def rows_of(block, chunk):
+        part = part_of[chunk]
+        at = part.index(chunk)
+        return arrays[block, part][at * cap : (at + 1) * cap, :]
+
+    def sizes(block, chunk):
+        part = part_of[chunk]
+        start = len(part) * cap + part.index(chunk) * META
+        meta = arrays[block, part][start : start + META, 0:1].astype(jnp.float32).astype(jnp.int32)
         return meta[1:2, :], meta[2:3, :]
 
     def score(early, late):
-        for late_at in chunks:
-            late_first = lane < sizes(late, late_at)[0]
-            best = best_refs[late][late_at : late_at + 1, :]
-            for at in chunks if late_at in new else new:
-                scores = dot_last(data[early][at][0:cap, :], data[late][late_at][0:cap, :])
-                first, both = sizes(early, at)
+        for late_chunk in chunks:
+            late_first = lane < sizes(late, late_chunk)[0]
+            best = best_refs[late][late_chunk : late_chunk + 1, :]
+            for chunk in chunks if late_chunk in fresh else fresh:
+                scores = dot_last(rows_of(early, chunk), rows_of(late, late_chunk))
+                first, both = sizes(early, chunk)
                 low = jnp.where(late_first, 0, first)
                 high = jnp.where(late_first, first, both)
                 if early == late:
-                    if at == late_at:
+                    if chunk == late_chunk:
                         high = jnp.minimum(high, lane)
                     else:
-                        high = jnp.where((group_pos ^ at) < (group_pos ^ late_at), high, 0)
+                        high = jnp.where((group_pos ^ chunk) < (group_pos ^ late_chunk), high, 0)
                 kept = jnp.where((row >= low) & (row < high), scores, -1.0)
                 best = jnp.maximum(best, jnp.max(kept, axis=0, keepdims=True))
-            best_refs[late][late_at : late_at + 1, :] = best
-
-    score(OWN, OWN)
+            best_refs[late][late_chunk : late_chunk + 1, :] = best
+
+    if inner:
+        score(OWN, OWN)
+        pl.when(core == 1)(lambda: score(SIB, OWN))
+    if not outer:
+        return
     pl.when(x == 0)(lambda: score(OWN, XN))
     pl.when(x == 1)(lambda: score(XN, OWN))
 
@@ -127,8 +153,6 @@
     def _():
         score(YN, OWN)
         score(YN, XN)
-
-    pl.when(core == 1)(lambda: score(SIB, OWN))
 
 
 def split_kernel(own_ref, x_ref, y_ref, *out_refs):
@@ -182,21 +206,15 @@
     return lax.optimization_barrier((value,) + others)[0]
 
 
-def score_call(cap, old, new, blocks, before, width):
-    count = len(old) + len(new)
-    arrays = [block[at] for block in blocks for at in old + new]
-    pairs = 5 * (count * count - len(old) ** 2)
+def score_call(cap, old, new, blocks, before, inner=True, outer=True):
+    arrays = [blocks[block][part] for block in blocks_used(inner, outer) for part in old + new]
     return pl.pallas_call(
-        functools.partial(score_kernel, cap, tuple(old), tuple(new)),
+        functools.partial(score_kernel, cap, old, new, inner, outer),
         out_shape=[jax.ShapeDtypeStruct((4, cap), jnp.float32)] * 3,
-        in_specs=vmem_specs(4 * count + len(before)),
+        in_specs=vmem_specs(len(arrays) + len(before)),
         out_specs=vmem_specs(3),
         compiler_params=pltpu.CompilerParams(vmem_limit_bytes=VMEM_LIMIT),
-        cost_estimate=pl.CostEstimate(
-            flops=2 * pairs * cap * cap * width,
-            bytes_accessed=8 * count * cap * width,
-            transcendentals=0,
-        ),
+        cost_estimate=COST,
     )(*arrays, *before)
 
 
@@ -205,10 +223,13 @@
     groups = lax.axis_size("group")
     cap = 3 * row_count // (2 * groups)
     params = pltpu.CompilerParams(vmem_limit_bytes=VMEM_LIMIT)
-    chunk_shape = jax.ShapeDtypeStruct((cap + META, width), jnp.bfloat16)
+
+    def chunks_shape(count):
+        return jax.ShapeDtypeStruct((count * (cap + META), width), jnp.bfloat16)
+
     *packed, place = pl.pallas_call(
-        functools.partial(pack_kernel, cap, groups),
-        out_shape=[chunk_shape] * groups + [jax.ShapeDtypeStruct((8, row_count), jnp.int32)],
+        functools.partial(pack_kernel, cap),
+        out_shape=[chunks_shape(1)] * groups + [jax.ShapeDtypeStruct((8, row_count), jnp.int32)],
         in_specs=vmem_specs(4),
         out_specs=vmem_specs(groups + 1),
         compiler_params=params,
@@ -219,39 +240,34 @@
         codes,
     )
     hops = [[(g, g ^ s) for g in range(groups)] for s in range(groups)]
-    unit_call = pl.pallas_call(
-        functools.partial(unit_kernel, cap),
-        out_shape=chunk_shape,
-        in_specs=vmem_specs(2),
-        out_specs=pl.BlockSpec(memory_space=pltpu.VMEM),
-        compiler_params=params,
-        cost_estimate=pl.CostEstimate(
-            flops=8 * cap * width, bytes_accessed=4 * cap * width, transcendentals=0
-        ),
-    )
     to_x, to_y, to_sib = plane_pairs()
-    blocks = [[None] * groups for _ in range(4)]
-
-    def spread(s, chunk, sib_after=(), x_after=(), y_after=()):
-        unit = unit_call(chunk, centroids)
-        blocks[OWN][s] = unit
-        blocks[SIB][s] = lax.ppermute(after(unit, *sib_after), "blk", to_sib)
-        blocks[XN][s] = lax.ppermute(after(unit, *x_after), "blk", to_x)
-        blocks[YN][s] = lax.ppermute(after(unit, *y_after), "blk", to_y)
-
-    one = lax.ppermute(packed[1], "group", hops[1])
-    two = lax.ppermute(packed[2], "group", hops[2])
-    three = lax.ppermute(after(packed[3], one), "group", hops[3])
-    spread(0, packed[0])
-    _, sib0, x0, y0 = (block[0] for block in blocks)
-    spread(1, one, [sib0], [x0], [y0])
-    best0 = score_call(cap, [], [0], blocks, [], width)
-    _, sib1, x1, y1 = (block[1] for block in blocks)
-    spread(2, after(two, sib1, *best0), [x1, y1])
-    best1 = score_call(cap, [0], [1], blocks, best0, width)
-    spread(3, after(three, blocks[SIB][2], *best1))
-    best2 = score_call(cap, [0, 1], [2], blocks, best1, width)
-    best, for_x, for_y = score_call(cap, [0, 1, 2], [3], blocks, best2, width)
+    own, sib, x_block, y_block = blocks = [{} for _ in range(4)]
+
+    def spread(part, arrived, sib_after=(), x_after=(), y_after=()):
+        unit = pl.pallas_call(
+            functools.partial(unit_kernel, cap),
+            out_shape=chunks_shape(len(part)),
+            in_specs=vmem_specs(len(part) + 1),
+            out_specs=pl.BlockSpec(memory_space=pltpu.VMEM),
+            compiler_params=params,
+            cost_estimate=COST,
+        )(*arrived, centroids)
+        own[part] = unit
+        sib[part] = lax.ppermute(after(unit, *sib_after), "blk", to_sib)
+        x_block[part] = lax.ppermute(after(unit, *x_after), "blk", to_x)
+        y_block[part] = lax.ppermute(after(unit, *y_after), "blk", to_y)
+
+    near, middle, far = (0,), (2, 1), (3,)
+    at_two = lax.ppermute(packed[2], "group", hops[2])
+    at_one = lax.ppermute(packed[1], "group", hops[1])
+    at_three = lax.ppermute(after(packed[3], at_two), "group", hops[3])
+    spread(near, [packed[0]])
+    best = score_call(cap, (), (near,), blocks, [])
+    spread(middle, [at_two, at_one], [sib[near]], [x_block[near]], [y_block[near]])
+    spread(far, [after(at_three, *best)])
+    best = score_call(cap, (near,), (middle,), blocks, best)
+    best = score_call(cap, (near, middle), (far,), blocks, best, outer=False)
+    best, for_x, for_y = score_call(cap, (near, middle), (far,), blocks, best, inner=False)
     returned = pl.pallas_call(
         split_kernel,
         out_shape=[jax.ShapeDtypeStruct((1, cap), jnp.float32)] * groups,

time: 82.8 us -> 77.4 us (0.935)
  starting transfers between devices: 29.7 us -> 26.4 us
  waiting for transfers between devices: 35 us -> 33.4 us
    ppermute x15 -> x12, starting transfers between devices: 24 us -> 20.2 us  [the longest x3 4.96 us: spread(): x_block[part] = lax.ppermute(after(unit, *x_after), 'blk', to_x)]
    ppermute x3, waiting for transfers between devices: 4 us -> 1.68 us  [paired_shards(): lax.ppermute(returned[s], 'group', hops[s])]
    ppermute x1, waiting for transfers between devices: 1.79 us -> 2.66 us  [paired_shards(): lax.ppermute(for_x, 'blk', reverse(to_x))]
    pallas_call x9 -> x8, Pallas kernels: 14.3 us -> 13.8 us  [the longest x4 11 us: score_call(): pl.pallas_call(functools.partial(score_kernel, cap, old, new, inner, oute...]
    ppermute x15 -> x12, waiting for transfers between devices: 29.1 us -> 29.1 us  [the longest x1 12.3 us: paired_shards(): at_two = lax.ppermute(packed[2], 'group', hops[2])]
  transfers between devices with their start and end apart: 20 -> 17, of which waited for: 10 -> 9; matrix products, arithmetic and copies ran while one was open for 0% -> 0% of each run, Pallas kernels for 10% -> 11%
where the time goes in v3:
time: 77.4 us; the launch traced here: 77.2 us
  waiting for transfers between devices  33.4 us (43%)
  starting transfers between devices  26.4 us (34%)
  Pallas kernels  14.6 us (19%)
  local copies, waits for them, and re-layouts  1.93 us (2%)
    ppermute x1, waiting for transfers between devices, paired_shards(): at_two = lax.ppermute(packed[2], 'group', hops[2])  12.3 us
    pallas_call x4, Pallas kernels, score_call(): pl.pallas_call(functools.partial(score_kernel, cap, old, new, inner, oute...  11 us
    ppermute x3, waiting for transfers between devices, spread(): y_block[part] = lax.ppermute(after(unit, *y_after), 'blk', to_y)  9.36 us
    ppermute x1, waiting for transfers between devices, paired_shards(): at_three = lax.ppermute(after(packed[3], at_two), 'group', hops[3])  5.28 us
    ppermute x3, starting transfers between devices, spread(): x_block[part] = lax.ppermute(after(unit, *x_after), 'blk', to_x)  4.96 us
    ppermute x3, starting transfers between devices, paired_shards(): lax.ppermute(returned[s], 'group', hops[s])  4.45 us
    ppermute x1, starting transfers between devices, paired_shards(): at_two = lax.ppermute(packed[2], 'group', hops[2])  4.11 us
    ppermute x3, starting transfers between devices, spread(): sib[part] = lax.ppermute(after(unit, *sib_after), 'blk', to_sib)  3.97 us
  transfers between devices with their start and end apart: 17, of which 9 were waited for; matrix products, arithmetic and copies ran while one was open for 0% of the time, Pallas kernels for 11%

profile of v3, /device:TPU:0, one launch (start us, length us, event | category | flops | bytes accessed | tf_op | source)
XLA Modules:
  0.0 77.2 jit_solution(43935141499581145)
XLA Ops:
  0.0 0.7 reshape.19
  0.7 0.7 copy-done.3
  1.4 1.2 %copy-done = bf16[512,1024]{1,0:T(8,128)(2,1)S(1)} copy-done((bf16[512,1024]{1,0:T(8,128)(2,1)S(1)}, bf16[512,1024]{1,0:T(8,128)(2,1)}, u32[]{:S(2)}) %copy-start) | copy-done | bytes 1048600
  2.6 1.5 %shard_map.55 = (bf16[200,1024]{1,0:T(8,128)(2,1)S(1)}, bf16[200,1024]{1,0:T(8,128)(2,1)S(1)}, bf16[200,1024]{1,0:T(8,128)(2,1)S(1)}, bf16[200,1024]{1,0:T(8,128)(2,1)S(1)}, s32[8,512]{1,0:T(8,128)S(1)}) custom-call(s32[1,512]{1,0:T(1,128)S(1)} %bitcast.5, s32[1,512]{1,0:T(1,128)S(1)} %bitcast.6, f32[1,512]{1,0:T(1,128)S(1)} %bitcast.4, ...), custom_call_target="tpu_custom_call" | custom-call | tf_op jit(solution)/shard_map/pallas_call | solution.py:230
  4.1 4.1 %collective-permute-start = (bf16[200,1024]{1,0:T(8,128)(2,1)S(1)}, bf16[200,1024]{1,0:T(8,128)(2,1)S(1)}, u32[]{:S(2)}, u32[]{:S(2)}) collective-permute-start(bf16[200,1024]{1,0:T(8,128)(2,1)S(1)} %get-tuple-element.33), channel_id=1, source_target_pairs={{0,2},{1,3},{2,0},{3,1},{4,6},{5,7},{6,4},{7,5},{8,10},{9,11},{10,... | collective-permute-start | bytes 1228808 | tf_op jit(solution)/shard_map/ppermute | solution.py:261
  8.2 1.6 %collective-permute-start.1 = (bf16[200,1024]{1,0:T(8,128)(2,1)S(1)}, bf16[200,1024]{1,0:T(8,128)(2,1)S(1)}, u32[]{:S(2)}, u32[]{:S(2)}) collective-permute-start(bf16[200,1024]{1,0:T(8,128)(2,1)S(1)} %get-tuple-element.34), channel_id=1, source_target_pairs={{0,1},{1,0},{2,3},{3,2},{4,5},{5,4},{6,7},{7,6},{8,9},{9,8},{10,11... | collective-permute-start | bytes 1228808 | tf_op jit(solution)/shard_map/ppermute | solution.py:262
  9.8 0.3 shard_map.56.refs_0_
  10.2 1.3 %collective-permute-start.3 = (bf16[200,1024]{1,0:T(8,128)(2,1)S(1)}, bf16[200,1024]{1,0:T(8,128)(2,1)S(1)}, u32[]{:S(2)}, u32[]{:S(2)}) collective-permute-start(bf16[200,1024]{1,0:T(8,128)(2,1)S(1)} %shard_map.56.refs_0_), channel_id=1, source_target_pairs={{0,4},{8,12},{16,20},{24,28},{1,5},{9,13},{17,21},{25,29},{2,6},{1... | collective-permute-start | bytes 1228808 | tf_op jit(solution)/shard_map/ppermute | solution.py:256
  11.5 0.4 collective-permute-start.5
  11.9 2.4 %collective-permute-start.4 = (bf16[200,1024]{1,0:T(8,128)(2,1)S(1)}, bf16[200,1024]{1,0:T(8,128)(2,1)S(1)}, u32[]{:S(2)}, u32[]{:S(2)}) collective-permute-start(bf16[200,1024]{1,0:T(8,128)(2,1)S(1)} %shard_map.56.refs_0_), channel_id=1, source_target_pairs={{8,0},{12,4},{4,8},{0,12},{28,16},{24,20},{16,24},{20,28},{9,1},{1... | collective-permute-start | bytes 1228808 | tf_op jit(solution)/shard_map/ppermute | solution.py:257
  14.3 12.3 %collective-permute-done.refs_0_ = bf16[200,1024]{1,0:T(8,128)(2,1)S(1)} collective-permute-done((bf16[200,1024]{1,0:T(8,128)(2,1)S(1)}, bf16[200,1024]{1,0:T(8,128)(2,1)S(1)}, u32[]{:S(2)}, u32[]{:S(2)}) %collective-permute-start) | collective-permute-done | bytes 409632 | tf_op jit(solution)/shard_map/ppermute | solution.py:261
  26.7 0.6 shard_map.57.refs_1_
  27.4 1.3 %collective-permute-start.10 = (bf16[400,1024]{1,0:T(8,128)(2,1)S(1)}, bf16[400,1024]{1,0:T(8,128)(2,1)S(1)}, u32[]{:S(2)}, u32[]{:S(2)}) collective-permute-start(bf16[400,1024]{1,0:T(8,128)(2,1)S(1)} %shard_map.57.refs_1_), channel_id=1, source_target_pairs={{0,4},{8,12},{16,20},{24,28},{1,5},{9,13},{17,21},{25,29},{2,6},{1... | collective-permute-start | bytes 2457608 | tf_op jit(solution)/shard_map/ppermute | solution.py:256
  28.7 4.0 %collective-permute-start.2 = (bf16[200,1024]{1,0:T(8,128)(2,1)S(1)}, bf16[200,1024]{1,0:T(8,128)(2,1)S(1)}, u32[]{:S(2)}, u32[]{:S(2)}) collective-permute-start(bf16[200,1024]{1,0:T(8,128)(2,1)S(1)} %get-tuple-element.36), channel_id=1, source_target_pairs={{0,3},{1,2},{2,1},{3,0},{4,7},{5,6},{6,5},{7,4},{8,11},{9,10},{10,... | collective-permute-start | bytes 1228808 | tf_op jit(solution)/shard_map/ppermute | solution.py:263
  32.9 2.5 %collective-permute-start.6 = (bf16[400,1024]{1,0:T(8,128)(2,1)S(1)}, bf16[400,1024]{1,0:T(8,128)(2,1)S(1)}, u32[]{:S(2)}, u32[]{:S(2)}) collective-permute-start(bf16[400,1024]{1,0:T(8,128)(2,1)S(1)} %shard_map.57.refs_1_), channel_id=1, source_target_pairs={{8,0},{12,4},{4,8},{0,12},{28,16},{24,20},{16,24},{20,28},{9,1},{1... | collective-permute-start | bytes 2457608 | tf_op jit(solution)/shard_map/ppermute | solution.py:257
  35.4 1.0 %shard_map.58 = (f32[4,192]{1,0:T(4,128)S(1)}, f32[4,192]{1,0:T(4,128)S(1)}, f32[4,192]{1,0:T(4,128)S(1)}) custom-call(bf16[200,1024]{1,0:T(8,128)(2,1)S(1)} %shard_map.56.refs_0_, bf16[200,1024]{1,0:T(8,128)(2,1)S(1)} %collective-permute-done.3.refs_1_.refs_2_.refs_3_, bf16[200,1024]{1,0:T(8,128)(2,1)S(1)} %collective-permute-done.4.refs_2_.refs_4_.refs_3_, ...), custom_call_target="tpu_custom_call" | custom-call | flops 1 | bytes 1 | tf_op jit(solution)/shard_map/pallas_call | solution.py:211
  36.5 5.3 %collective-permute-done.2.refs_0_ = bf16[200,1024]{1,0:T(8,128)(2,1)S(1)} collective-permute-done((bf16[200,1024]{1,0:T(8,128)(2,1)S(1)}, bf16[200,1024]{1,0:T(8,128)(2,1)S(1)}, u32[]{:S(2)}, u32[]{:S(2)}) %collective-permute-start.2) | collective-permute-done | bytes 409632 | tf_op jit(solution)/shard_map/ppermute | solution.py:263
  41.7 0.3 shard_map.59.refs_2_
  42.1 1.3 %collective-permute-start.11 = (bf16[200,1024]{1,0:T(8,128)(2,1)S(1)}, bf16[200,1024]{1,0:T(8,128)(2,1)S(1)}, u32[]{:S(2)}, u32[]{:S(2)}) collective-permute-start(bf16[200,1024]{1,0:T(8,128)(2,1)S(1)} %shard_map.59.refs_2_), channel_id=1, source_target_pairs={{0,4},{8,12},{16,20},{24,28},{1,5},{9,13},{17,21},{25,29},{2,6},{1... | collective-permute-start | bytes 1228808 | tf_op jit(solution)/shard_map/ppermute | solution.py:256
  43.5 1.0 %collective-permute-start.9 = (bf16[200,1024]{1,0:T(8,128)(2,1)S(1)}, bf16[200,1024]{1,0:T(8,128)(2,1)S(1)}, u32[]{:S(2)}, u32[]{:S(2)}) collective-permute-start(bf16[200,1024]{1,0:T(8,128)(2,1)S(1)} %shard_map.59.refs_2_), channel_id=1, source_target_pairs={{16,0},{20,4},{24,8},{28,12},{4,16},{0,20},{12,24},{8,28},{17,1},{... | collective-permute-start | bytes 1228808 | tf_op jit(solution)/shard_map/ppermute | solution.py:258
  44.5 9.4 %collective-permute-done.8.refs_7_ = bf16[400,1024]{1,0:T(8,128)(2,1)S(1)} collective-permute-done((bf16[400,1024]{1,0:T(8,128)(2,1)S(1)}, bf16[400,1024]{1,0:T(8,128)(2,1)S(1)}, u32[]{:S(2)}, u32[]{:S(2)}) %collective-permute-start.8) | collective-permute-done | bytes 819232 | tf_op jit(solution)/shard_map/ppermute | solution.py:258
  54.1 5.4 %shard_map.60 = (f32[4,192]{1,0:T(4,128)S(1)}, f32[4,192]{1,0:T(4,128)S(1)}, f32[4,192]{1,0:T(4,128)S(1)}) custom-call(bf16[200,1024]{1,0:T(8,128)(2,1)S(1)} %shard_map.56.refs_0_, bf16[400,1024]{1,0:T(8,128)(2,1)S(1)} %shard_map.57.refs_1_, bf16[200,1024]{1,0:T(8,128)(2,1)S(1)} %collective-permute-done.3.refs_1_.refs_2_.refs_3_, ...), custom_call_target="tpu_custom_call" | custom-call | flops 1 | bytes 1 | tf_op jit(solution)/shard_map/pallas_call | solution.py:211
  59.5 1.2 %shard_map.61 = (f32[4,192]{1,0:T(4,128)S(1)}, f32[4,192]{1,0:T(4,128)S(1)}, f32[4,192]{1,0:T(4,128)S(1)}) custom-call(bf16[200,1024]{1,0:T(8,128)(2,1)S(1)} %shard_map.56.refs_0_, bf16[400,1024]{1,0:T(8,128)(2,1)S(1)} %shard_map.57.refs_1_, bf16[200,1024]{1,0:T(8,128)(2,1)S(1)} %shard_map.59.refs_2_, ...), custom_call_target="tpu_custom_call" | custom-call | flops 1 | bytes 1 | tf_op jit(solution)/shard_map/pallas_call | solution.py:211
  60.7 1.7 %collective-permute-done.7.refs_5_ = bf16[200,1024]{1,0:T(8,128)(2,1)S(1)} collective-permute-done((bf16[200,1024]{1,0:T(8,128)(2,1)S(1)}, bf16[200,1024]{1,0:T(8,128)(2,1)S(1)}, u32[]{:S(2)}, u32[]{:S(2)}) %collective-permute-start.7) | collective-permute-done | bytes 409632 | tf_op jit(solution)/shard_map/ppermute | solution.py:257
  62.4 3.4 %shard_map.62 = (f32[4,192]{1,0:T(4,128)S(1)}, f32[4,192]{1,0:T(4,128)S(1)}, f32[4,192]{1,0:T(4,128)S(1)}) custom-call(bf16[200,1024]{1,0:T(8,128)(2,1)S(1)} %shard_map.56.refs_0_, bf16[400,1024]{1,0:T(8,128)(2,1)S(1)} %shard_map.57.refs_1_, bf16[200,1024]{1,0:T(8,128)(2,1)S(1)} %shard_map.59.refs_2_, ...), custom_call_target="tpu_custom_call" | custom-call | flops 1 | bytes 1 | tf_op jit(solution)/shard_map/pallas_call | solution.py:211
  65.8 1.7 %collective-permute-start.13 = (f32[4,192]{1,0:T(4,128)S(1)}, f32[4,192]{1,0:T(4,128)S(1)}, u32[]{:S(2)}, u32[]{:S(2)}) collective-permute-start(f32[4,192]{1,0:T(4,128)S(1)} %get-tuple-element.52), channel_id=1, source_target_pairs={{0,16},{4,20},{8,24},{12,28},{16,4},{20,0},{24,12},{28,8},{1,17},{... | collective-permute-start | bytes 9224 | tf_op jit(solution)/shard_map/ppermute | solution.py:277
  67.5 2.7 %collective-permute-done.12.x_ref = f32[4,192]{1,0:T(4,128)S(1)} collective-permute-done((f32[4,192]{1,0:T(4,128)S(1)}, f32[4,192]{1,0:T(4,128)S(1)}, u32[]{:S(2)}, u32[]{:S(2)}) %collective-permute-start.12) | collective-permute-done | bytes 3104 | tf_op jit(solution)/shard_map/ppermute | solution.py:277
  70.2 0.8 collective-permute-start.14
  71.0 3.7 %collective-permute-start.16 = (f32[1,192]{1,0:T(1,128)S(1)}, f32[1,192]{1,0:T(1,128)S(1)}, u32[]{:S(2)}, u32[]{:S(2)}) collective-permute-start(f32[1,192]{1,0:T(1,128)S(1)} %get-tuple-element.56), channel_id=1, source_target_pairs={{0,3},{1,2},{2,1},{3,0},{4,7},{5,6},{6,5},{7,4},{8,11},{9,10},{10,... | collective-permute-start | bytes 2312 | tf_op jit(solution)/shard_map/ppermute | solution.py:279
  74.6 0.8 %collective-permute-done.15.refs_2_ = f32[1,192]{1,0:T(1,128)S(1)} collective-permute-done((f32[1,192]{1,0:T(1,128)S(1)}, f32[1,192]{1,0:T(1,128)S(1)}, u32[]{:S(2)}, u32[]{:S(2)}) %collective-permute-start.15) | collective-permute-done | bytes 800 | tf_op jit(solution)/shard_map/ppermute | solution.py:279
  75.4 0.9 %collective-permute-done.16.refs_3_ = f32[1,192]{1,0:T(1,128)S(1)} collective-permute-done((f32[1,192]{1,0:T(1,128)S(1)}, f32[1,192]{1,0:T(1,128)S(1)}, u32[]{:S(2)}, u32[]{:S(2)}) %collective-permute-start.16) | collective-permute-done | bytes 800 | tf_op jit(solution)/shard_map/ppermute | solution.py:279
  76.3 0.8 %shard_map.64 = f32[1,512]{1,0:T(1,128)} custom-call(s32[8,512]{1,0:T(8,128)S(1)} %get-tuple-element.31.place_ref, f32[1,192]{1,0:T(1,128)S(1)} %get-tuple-element.53.refs_0_, f32[1,192]{1,0:T(1,128)S(1)} %collective-permute-done.14.refs_1_, f32[1,192]{1,0:T(1,128)S(1)} %collective-permute-done.15.refs_2_, f32[1,192]{1,0:T(1,128)S(1)} %collective-permute-done.16.refs_3_), custom_call_target="tpu_custom_call" | custom-call | tf_op jit(solution)/shard_map/pallas_call | solution.py:281
  (21 shorter events, 0.8 us)
Async XLA Ops:
  0.7 0.7 copy-start.3
  0.7 0.7 copy-start.2
  1.4 1.2 %copy-start = (bf16[512,1024]{1,0:T(8,128)(2,1)S(1)}, bf16[512,1024]{1,0:T(8,128)(2,1)}, u32[]{:S(2)}) copy-start(bf16[512,1024]{1,0:T(8,128)(2,1)} %codes_ref.1) | copy-start | bytes 3145732
  4.1 5.7 %copy-start.1 = (bf16[2,1024]{1,0:T(2,128)(2,1)S(1)}, bf16[2,1024]{1,0:T(2,128)(2,1)}, u32[]{:S(2)}) copy-start(bf16[2,1024]{1,0:T(2,128)(2,1)} %refs_1_.3) | copy-start | bytes 12292
  4.1 22.5 %collective-permute-start = (bf16[200,1024]{1,0:T(8,128)(2,1)S(1)}, bf16[200,1024]{1,0:T(8,128)(2,1)S(1)}, u32[]{:S(2)}, u32[]{:S(2)}) collective-permute-start(bf16[200,1024]{1,0:T(8,128)(2,1)S(1)} %get-tuple-element.33), channel_id=1, source_target_pairs={{0,2},{1,3},{2,0},{3,1},{4,6},{5,7},{6,4},{7,5},{8,10},{9,11},{10,... | collective-permute-start | bytes 1228808 | tf_op jit(solution)/shard_map/ppermute | solution.py:261
  8.2 18.5 %collective-permute-start.1 = (bf16[200,1024]{1,0:T(8,128)(2,1)S(1)}, bf16[200,1024]{1,0:T(8,128)(2,1)S(1)}, u32[]{:S(2)}, u32[]{:S(2)}) collective-permute-start(bf16[200,1024]{1,0:T(8,128)(2,1)S(1)} %get-tuple-element.34), channel_id=1, source_target_pairs={{0,1},{1,0},{2,3},{3,2},{4,5},{5,4},{6,7},{7,6},{8,9},{9,8},{10,11... | collective-permute-start | bytes 1228808 | tf_op jit(solution)/shard_map/ppermute | solution.py:262
  10.2 17.2 %collective-permute-start.3 = (bf16[200,1024]{1,0:T(8,128)(2,1)S(1)}, bf16[200,1024]{1,0:T(8,128)(2,1)S(1)}, u32[]{:S(2)}, u32[]{:S(2)}) collective-permute-start(bf16[200,1024]{1,0:T(8,128)(2,1)S(1)} %shard_map.56.refs_0_), channel_id=1, source_target_pairs={{0,4},{8,12},{16,20},{24,28},{1,5},{9,13},{17,21},{25,29},{2,6},{1... | collective-permute-start | bytes 1228808 | tf_op jit(solution)/shard_map/ppermute | solution.py:256
  11.5 17.2 %collective-permute-start.5 = (bf16[200,1024]{1,0:T(8,128)(2,1)S(1)}, bf16[200,1024]{1,0:T(8,128)(2,1)S(1)}, u32[]{:S(2)}, u32[]{:S(2)}) collective-permute-start(bf16[200,1024]{1,0:T(8,128)(2,1)S(1)} %shard_map.56.refs_0_), channel_id=1, source_target_pairs={{16,0},{20,4},{24,8},{28,12},{4,16},{0,20},{12,24},{8,28},{17,1},{... | collective-permute-start | bytes 1228808 | tf_op jit(solution)/shard_map/ppermute | solution.py:258
  11.9 21.0 %collective-permute-start.4 = (bf16[200,1024]{1,0:T(8,128)(2,1)S(1)}, bf16[200,1024]{1,0:T(8,128)(2,1)S(1)}, u32[]{:S(2)}, u32[]{:S(2)}) collective-permute-start(bf16[200,1024]{1,0:T(8,128)(2,1)S(1)} %shard_map.56.refs_0_), channel_id=1, source_target_pairs={{8,0},{12,4},{4,8},{0,12},{28,16},{24,20},{16,24},{20,28},{9,1},{1... | collective-permute-start | bytes 1228808 | tf_op jit(solution)/shard_map/ppermute | solution.py:257
  27.4 16.1 %collective-permute-start.10 = (bf16[400,1024]{1,0:T(8,128)(2,1)S(1)}, bf16[400,1024]{1,0:T(8,128)(2,1)S(1)}, u32[]{:S(2)}, u32[]{:S(2)}) collective-permute-start(bf16[400,1024]{1,0:T(8,128)(2,1)S(1)} %shard_map.57.refs_1_), channel_id=1, source_target_pairs={{0,4},{8,12},{16,20},{24,28},{1,5},{9,13},{17,21},{25,29},{2,6},{1... | collective-permute-start | bytes 2457608 | tf_op jit(solution)/shard_map/ppermute | solution.py:256
  28.7 13.0 %collective-permute-start.2 = (bf16[200,1024]{1,0:T(8,128)(2,1)S(1)}, bf16[200,1024]{1,0:T(8,128)(2,1)S(1)}, u32[]{:S(2)}, u32[]{:S(2)}) collective-permute-start(bf16[200,1024]{1,0:T(8,128)(2,1)S(1)} %get-tuple-element.36), channel_id=1, source_target_pairs={{0,3},{1,2},{2,1},{3,0},{4,7},{5,6},{6,5},{7,4},{8,11},{9,10},{10,... | collective-permute-start | bytes 1228808 | tf_op jit(solution)/shard_map/ppermute | solution.py:263
  32.7 21.2 %collective-permute-start.8 = (bf16[400,1024]{1,0:T(8,128)(2,1)S(1)}, bf16[400,1024]{1,0:T(8,128)(2,1)S(1)}, u32[]{:S(2)}, u32[]{:S(2)}) collective-permute-start(bf16[400,1024]{1,0:T(8,128)(2,1)S(1)} %shard_map.57.refs_1_), channel_id=1, source_target_pairs={{16,0},{20,4},{24,8},{28,12},{4,16},{0,20},{12,24},{8,28},{17,1},{... | collective-permute-start | bytes 2457608 | tf_op jit(solution)/shard_map/ppermute | solution.py:258
  32.9 21.2 %collective-permute-start.6 = (bf16[400,1024]{1,0:T(8,128)(2,1)S(1)}, bf16[400,1024]{1,0:T(8,128)(2,1)S(1)}, u32[]{:S(2)}, u32[]{:S(2)}) collective-permute-start(bf16[400,1024]{1,0:T(8,128)(2,1)S(1)} %shard_map.57.refs_1_), channel_id=1, source_target_pairs={{8,0},{12,4},{4,8},{0,12},{28,16},{24,20},{16,24},{20,28},{9,1},{1... | collective-permute-start | bytes 2457608 | tf_op jit(solution)/shard_map/ppermute | solution.py:257
  42.1 17.4 %collective-permute-start.11 = (bf16[200,1024]{1,0:T(8,128)(2,1)S(1)}, bf16[200,1024]{1,0:T(8,128)(2,1)S(1)}, u32[]{:S(2)}, u32[]{:S(2)}) collective-permute-start(bf16[200,1024]{1,0:T(8,128)(2,1)S(1)} %shard_map.59.refs_2_), channel_id=1, source_target_pairs={{0,4},{8,12},{16,20},{24,28},{1,5},{9,13},{17,21},{25,29},{2,6},{1... | collective-permute-start | bytes 1228808 | tf_op jit(solution)/shard_map/ppermute | solution.py:256
  43.4 18.9 %collective-permute-start.7 = (bf16[200,1024]{1,0:T(8,128)(2,1)S(1)}, bf16[200,1024]{1,0:T(8,128)(2,1)S(1)}, u32[]{:S(2)}, u32[]{:S(2)}) collective-permute-start(bf16[200,1024]{1,0:T(8,128)(2,1)S(1)} %shard_map.59.refs_2_), channel_id=1, source_target_pairs={{8,0},{12,4},{4,8},{0,12},{28,16},{24,20},{16,24},{20,28},{9,1},{1... | collective-permute-start | bytes 1228808 | tf_op jit(solution)/shard_map/ppermute | solution.py:257
  43.5 18.9 %collective-permute-start.9 = (bf16[200,1024]{1,0:T(8,128)(2,1)S(1)}, bf16[200,1024]{1,0:T(8,128)(2,1)S(1)}, u32[]{:S(2)}, u32[]{:S(2)}) collective-permute-start(bf16[200,1024]{1,0:T(8,128)(2,1)S(1)} %shard_map.59.refs_2_), channel_id=1, source_target_pairs={{16,0},{20,4},{24,8},{28,12},{4,16},{0,20},{12,24},{8,28},{17,1},{... | collective-permute-start | bytes 1228808 | tf_op jit(solution)/shard_map/ppermute | solution.py:258
  65.7 4.4 %collective-permute-start.12 = (f32[4,192]{1,0:T(4,128)S(1)}, f32[4,192]{1,0:T(4,128)S(1)}, u32[]{:S(2)}, u32[]{:S(2)}) collective-permute-start(f32[4,192]{1,0:T(4,128)S(1)} %get-tuple-element.51), channel_id=1, source_target_pairs={{0,8},{4,12},{8,4},{12,0},{16,28},{20,24},{24,16},{28,20},{1,9},{5... | collective-permute-start | bytes 9224 | tf_op jit(solution)/shard_map/ppermute | solution.py:277
  65.8 4.4 %collective-permute-start.13 = (f32[4,192]{1,0:T(4,128)S(1)}, f32[4,192]{1,0:T(4,128)S(1)}, u32[]{:S(2)}, u32[]{:S(2)}) collective-permute-start(f32[4,192]{1,0:T(4,128)S(1)} %get-tuple-element.52), channel_id=1, source_target_pairs={{0,16},{4,20},{8,24},{12,28},{16,4},{20,0},{24,12},{28,8},{1,17},{... | collective-permute-start | bytes 9224 | tf_op jit(solution)/shard_map/ppermute | solution.py:277
  70.2 4.5 %collective-permute-start.14 = (f32[1,192]{1,0:T(1,128)S(1)}, f32[1,192]{1,0:T(1,128)S(1)}, u32[]{:S(2)}, u32[]{:S(2)}) collective-permute-start(f32[1,192]{1,0:T(1,128)S(1)} %get-tuple-element.54), channel_id=1, source_target_pairs={{0,1},{1,0},{2,3},{3,2},{4,5},{5,4},{6,7},{7,6},{8,9},{9,8},{10,11... | collective-permute-start | bytes 2312 | tf_op jit(solution)/shard_map/ppermute | solution.py:279
  71.0 4.5 %collective-permute-start.15 = (f32[1,192]{1,0:T(1,128)S(1)}, f32[1,192]{1,0:T(1,128)S(1)}, u32[]{:S(2)}, u32[]{:S(2)}) collective-permute-start(f32[1,192]{1,0:T(1,128)S(1)} %get-tuple-element.55), channel_id=1, source_target_pairs={{0,2},{1,3},{2,0},{3,1},{4,6},{5,7},{6,4},{7,5},{8,10},{9,11},{10,... | collective-permute-start | bytes 2312 | tf_op jit(solution)/shard_map/ppermute | solution.py:279
  71.0 5.4 %collective-permute-start.16 = (f32[1,192]{1,0:T(1,128)S(1)}, f32[1,192]{1,0:T(1,128)S(1)}, u32[]{:S(2)}, u32[]{:S(2)}) collective-permute-start(f32[1,192]{1,0:T(1,128)S(1)} %get-tuple-element.56), channel_id=1, source_target_pairs={{0,3},{1,2},{2,1},{3,0},{4,7},{5,6},{6,5},{7,4},{8,11},{9,10},{10,... | collective-permute-start | bytes 2312 | tf_op jit(solution)/shard_map/ppermute | solution.py:279

commit v4 on v3

--- a/solution.py
+++ b/solution.py
@@ -75,50 +75,42 @@
         vectors = centre + scale * ref[0:cap, :].astype(jnp.float32)
         norm = jnp.sqrt(jnp.sum(vectors * vectors, axis=1, keepdims=True) + 1e-06)
         out_ref[at * cap : (at + 1) * cap, :] = (vectors * (1.0 / norm)).astype(jnp.bfloat16)
-        start = count * cap + at * META
-        out_ref[start : start + META, :] = ref[cap:, :]
-
-
-def blocks_used(inner, outer):
-    return (OWN,) + (SIB,) * inner + (XN, YN) * outer
-
-
-def score_kernel(cap, old, new, inner, outer, *refs):
-    parts = old + new
-    chunks = sum(parts, ())
-    fresh = sum(new, ())
-    used = blocks_used(inner, outer)
-    arrays = {
-        (block, part): refs[at * len(parts) + which]
-        for at, block in enumerate(used)
-        for which, part in enumerate(parts)
-    }
-    part_of = {chunk: part for part in parts for chunk in part}
-    rest = refs[len(arrays) :]
+    out_ref[count * cap :, :] = jnp.concatenate(
+        [ref[cap:, :].astype(jnp.float32) for ref in chunk_refs], axis=0
+    ).astype(jnp.bfloat16)
+
+
+OWN_PAIRS, SIB_PAIRS, FAR_PAIRS = "own", "sib", "far"
+
+
+def score_kernel(cap, keys, jobs, *refs):
+    arrays = dict(zip(keys, refs))
+    part_of = {chunk: part for _, part in keys for chunk in part}
+    rest = refs[len(keys) :]
     best_refs = dict(zip((OWN, XN, YN), rest[-3:]))
     blk = lax.axis_index("blk")
     group_pos = lax.axis_index("group")
     core, x, y = blk % 2, (blk // 2) % 2, blk // 4
     row, lane = iota((cap, cap), 0), iota((1, cap), 1)
-    if len(rest) > 3:
-        for block, ref in zip((OWN, XN, YN), rest[:3]):
-            best_refs[block][...] = ref[...]
-    else:
-        for block in (OWN, XN, YN):
+    for at, block in enumerate((OWN, XN, YN)):
+        if len(rest) > 3:
+            best_refs[block][...] = rest[at][...]
+        else:
             best_refs[block][...] = jnp.full((4, cap), -1.0, jnp.float32)
 
     def rows_of(block, chunk):
         part = part_of[chunk]
-        at = part.index(chunk)
-        return arrays[block, part][at * cap : (at + 1) * cap, :]
+        start = part.index(chunk) * cap
+        return arrays[block, part][start : start + cap, :]
 
     def sizes(block, chunk):
         part = part_of[chunk]
-        start = len(part) * cap + part.index(chunk) * META
-        meta = arrays[block, part][start : start + META, 0:1].astype(jnp.float32).astype(jnp.int32)
-        return meta[1:2, :], meta[2:3, :]
-
-    def score(early, late):
+        meta = arrays[block, part][len(part) * cap :, 0:1].astype(jnp.float32).astype(jnp.int32)
+        at = part.index(chunk) * META
+        return meta[at + 1 : at + 2, :], meta[at + 2 : at + 3, :]
+
+    def score(early, late, old, new):
+        chunks, fresh = sum(old + new, ()), sum(new, ())
         for late_chunk in chunks:
             late_first = lane < sizes(late, late_chunk)[0]
             best = best_refs[late][late_chunk : late_chunk + 1, :]
@@ -136,23 +128,18 @@
                 best = jnp.maximum(best, jnp.max(kept, axis=0, keepdims=True))
             best_refs[late][late_chunk : late_chunk + 1, :] = best
 
-    if inner:
-        score(OWN, OWN)
-        pl.when(core == 1)(lambda: score(SIB, OWN))
-    if not outer:
-        return
-    pl.when(x == 0)(lambda: score(OWN, XN))
-    pl.when(x == 1)(lambda: score(XN, OWN))
-
-    @pl.when(y == 0)
-    def _():
-        score(OWN, YN)
-        score(XN, YN)
-
-    @pl.when(y == 1)
-    def _():
-        score(YN, OWN)
-        score(YN, XN)
+    for kind, *which in jobs:
+        if kind == OWN_PAIRS:
+            score(OWN, OWN, *which)
+        elif kind == SIB_PAIRS:
+            pl.when(core == 1)(functools.partial(score, SIB, OWN, *which))
+        else:
+            pl.when(x == 0)(functools.partial(score, OWN, XN, *which))
+            pl.when(x == 1)(functools.partial(score, XN, OWN, *which))
+            pl.when(y == 0)(functools.partial(score, OWN, YN, *which))
+            pl.when(y == 0)(functools.partial(score, XN, YN, *which))
+            pl.when(y == 1)(functools.partial(score, YN, OWN, *which))
+            pl.when(y == 1)(functools.partial(score, YN, XN, *which))
 
 
 def split_kernel(own_ref, x_ref, y_ref, *out_refs):
@@ -206,16 +193,20 @@
     return lax.optimization_barrier((value,) + others)[0]
 
 
-def score_call(cap, old, new, blocks, before, inner=True, outer=True):
-    arrays = [blocks[block][part] for block in blocks_used(inner, outer) for part in old + new]
+def score_call(cap, blocks, jobs, before):
+    used = {OWN_PAIRS: (OWN,), SIB_PAIRS: (OWN, SIB), FAR_PAIRS: (OWN, XN, YN)}
+    keys = [
+        (block, part) for kind, old, new in jobs for block in used[kind] for part in old + new
+    ]
+    keys = list(dict.fromkeys(keys))
     return pl.pallas_call(
-        functools.partial(score_kernel, cap, old, new, inner, outer),
+        functools.partial(score_kernel, cap, keys, jobs),
         out_shape=[jax.ShapeDtypeStruct((4, cap), jnp.float32)] * 3,
-        in_specs=vmem_specs(len(arrays) + len(before)),
+        in_specs=vmem_specs(len(keys) + len(before)),
         out_specs=vmem_specs(3),
         compiler_params=pltpu.CompilerParams(vmem_limit_bytes=VMEM_LIMIT),
         cost_estimate=COST,
-    )(*arrays, *before)
+    )(*[blocks[block][part] for block, part in keys], *before)
 
 
 def paired_shards(codes, row_scale, row_group, row_sub, centroids):
@@ -243,31 +234,45 @@
     to_x, to_y, to_sib = plane_pairs()
     own, sib, x_block, y_block = blocks = [{} for _ in range(4)]
 
-    def spread(part, arrived, sib_after=(), x_after=(), y_after=()):
-        unit = pl.pallas_call(
+    def unit_rows(*arrived):
+        return pl.pallas_call(
             functools.partial(unit_kernel, cap),
-            out_shape=chunks_shape(len(part)),
-            in_specs=vmem_specs(len(part) + 1),
+            out_shape=chunks_shape(len(arrived)),
+            in_specs=vmem_specs(len(arrived) + 1),
             out_specs=pl.BlockSpec(memory_space=pltpu.VMEM),
             compiler_params=params,
             cost_estimate=COST,
         )(*arrived, centroids)
+
+    def spread(part, unit, sib_after=(), x_after=(), y_after=()):
         own[part] = unit
         sib[part] = lax.ppermute(after(unit, *sib_after), "blk", to_sib)
         x_block[part] = lax.ppermute(after(unit, *x_after), "blk", to_x)
         y_block[part] = lax.ppermute(after(unit, *y_after), "blk", to_y)
 
+    def score(before, *jobs):
+        return score_call(cap, blocks, jobs, before)
+
     near, middle, far = (0,), (2, 1), (3,)
     at_two = lax.ppermute(packed[2], "group", hops[2])
     at_one = lax.ppermute(packed[1], "group", hops[1])
     at_three = lax.ppermute(after(packed[3], at_two), "group", hops[3])
-    spread(near, [packed[0]])
-    best = score_call(cap, (), (near,), blocks, [])
-    spread(middle, [at_two, at_one], [sib[near]], [x_block[near]], [y_block[near]])
-    spread(far, [after(at_three, *best)])
-    best = score_call(cap, (near,), (middle,), blocks, best)
-    best = score_call(cap, (near, middle), (far,), blocks, best, outer=False)
-    best, for_x, for_y = score_call(cap, (near, middle), (far,), blocks, best, inner=False)
+    spread(near, unit_rows(packed[0]))
+    landed = [sib[near], x_block[near], y_block[near]]
+    spread(
+        middle,
+        unit_rows(at_two, at_one),
+        landed,
+        [x_block[near]],
+        [y_block[near]],
+    )
+    best = score([], (FAR_PAIRS, (), (near,)), (OWN_PAIRS, (), (near, middle)))
+    spread(far, unit_rows(after(at_three, *best)), [sib[middle]], [sib[middle]], [sib[middle]])
+    best = score(
+        best, (FAR_PAIRS, (near,), (middle,)), (SIB_PAIRS, (), (near, middle))
+    )
+    best = score(best, (OWN_PAIRS, (near, middle), (far,)), (SIB_PAIRS, (near, middle), (far,)))
+    best, for_x, for_y = score(best, (FAR_PAIRS, (near, middle), (far,)))
     returned = pl.pallas_call(
         split_kernel,
         out_shape=[jax.ShapeDtypeStruct((1, cap), jnp.float32)] * groups,

time: 77.4 us -> 76.6 us (0.990)
  waiting for transfers between devices: 33.4 us -> 30 us
  starting transfers between devices: 26.4 us -> 29.1 us
    ppermute x3, starting transfers between devices: 3.97 us -> 6.09 us  [spread(): sib[part] = lax.ppermute(after(unit, *sib_after), 'blk', to_sib)]
    ppermute x1, waiting for transfers between devices: 2.66 us -> 1.47 us  [paired_shards(): lax.ppermute(for_x, 'blk', reverse(to_x))]
    ppermute x1, waiting for transfers between devices: 5.28 us -> 4.12 us  [paired_shards(): at_three = lax.ppermute(after(packed[3], at_two), 'group', hops[3])]
    ppermute x1, waiting for transfers between devices: 12.3 us -> 11.3 us  [paired_shards(): at_two = lax.ppermute(packed[2], 'group', hops[2])]
  transfers between devices with their start and end apart: 17 -> 17, of which waited for: 9 -> 10; matrix products, arithmetic and copies ran while one was open for 0% -> 0% of each run, Pallas kernels for 11% -> 11%
where the time goes in v4:
time: 76.6 us; the launch traced here: 76.3 us
  waiting for transfers between devices  30 us (39%)
  starting transfers between devices  29.1 us (38%)
  Pallas kernels  14.4 us (19%)
  local copies, waits for them, and re-layouts  1.93 us (3%)
    ppermute x1, waiting for transfers between devices, paired_shards(): at_two = lax.ppermute(packed[2], 'group', hops[2])  11.3 us
    pallas_call x4, Pallas kernels, score_call(): pl.pallas_call(functools.partial(score_kernel, cap, keys, jobs), out_shap...  10.8 us
    ppermute x3, waiting for transfers between devices, spread(): y_block[part] = lax.ppermute(after(unit, *y_after), 'blk', to_y)  8.95 us
    ppermute x3, starting transfers between devices, spread(): sib[part] = lax.ppermute(after(unit, *sib_after), 'blk', to_sib)  6.09 us
    ppermute x3, starting transfers between devices, spread(): x_block[part] = lax.ppermute(after(unit, *x_after), 'blk', to_x)  5.69 us
    ppermute x3, starting transfers between devices, paired_shards(): lax.ppermute(returned[s], 'group', hops[s])  4.45 us
    ppermute x1, waiting for transfers between devices, paired_shards(): at_three = lax.ppermute(after(packed[3], at_two), 'group', hops[3])  4.12 us
    ppermute x1, starting transfers between devices, paired_shards(): at_two = lax.ppermute(packed[2], 'group', hops[2])  4.11 us
  transfers between devices with their start and end apart: 17, of which 10 were waited for; matrix products, arithmetic and copies ran while one was open for 0% of the time, Pallas kernels for 11%

profile of v4, /device:TPU:0, one launch (start us, length us, event | category | flops | bytes accessed | tf_op | source)
XLA Modules:
  0.0 76.3 jit_solution(4536549581607526777)
XLA Ops:
  0.0 0.7 reshape.19
  0.7 0.7 copy-done.3
  1.4 1.2 %copy-done = bf16[512,1024]{1,0:T(8,128)(2,1)S(1)} copy-done((bf16[512,1024]{1,0:T(8,128)(2,1)S(1)}, bf16[512,1024]{1,0:T(8,128)(2,1)}, u32[]{:S(2)}) %copy-start) | copy-done | bytes 1048600
  2.6 1.5 %shard_map.55 = (bf16[200,1024]{1,0:T(8,128)(2,1)S(1)}, bf16[200,1024]{1,0:T(8,128)(2,1)S(1)}, bf16[200,1024]{1,0:T(8,128)(2,1)S(1)}, bf16[200,1024]{1,0:T(8,128)(2,1)S(1)}, s32[8,512]{1,0:T(8,128)S(1)}) custom-call(s32[1,512]{1,0:T(1,128)S(1)} %bitcast.5, s32[1,512]{1,0:T(1,128)S(1)} %bitcast.6, f32[1,512]{1,0:T(1,128)S(1)} %bitcast.4, ...), custom_call_target="tpu_custom_call" | custom-call | tf_op jit(solution)/shard_map/pallas_call | solution.py:221
  4.1 4.1 %collective-permute-start = (bf16[200,1024]{1,0:T(8,128)(2,1)S(1)}, bf16[200,1024]{1,0:T(8,128)(2,1)S(1)}, u32[]{:S(2)}, u32[]{:S(2)}) collective-permute-start(bf16[200,1024]{1,0:T(8,128)(2,1)S(1)} %get-tuple-element.34), channel_id=1, source_target_pairs={{0,2},{1,3},{2,0},{3,1},{4,6},{5,7},{6,4},{7,5},{8,10},{9,11},{10,... | collective-permute-start | bytes 1228808 | tf_op jit(solution)/shard_map/ppermute | solution.py:257
  8.2 1.6 %collective-permute-start.1 = (bf16[200,1024]{1,0:T(8,128)(2,1)S(1)}, bf16[200,1024]{1,0:T(8,128)(2,1)S(1)}, u32[]{:S(2)}, u32[]{:S(2)}) collective-permute-start(bf16[200,1024]{1,0:T(8,128)(2,1)S(1)} %get-tuple-element.35), channel_id=1, source_target_pairs={{0,1},{1,0},{2,3},{3,2},{4,5},{5,4},{6,7},{7,6},{8,9},{9,8},{10,11... | collective-permute-start | bytes 1228808 | tf_op jit(solution)/shard_map/ppermute | solution.py:258
  10.2 0.4 collective-permute-start.3
  10.6 1.2 %collective-permute-start.4 = (bf16[200,1024]{1,0:T(8,128)(2,1)S(1)}, bf16[200,1024]{1,0:T(8,128)(2,1)S(1)}, u32[]{:S(2)}, u32[]{:S(2)}) collective-permute-start(bf16[200,1024]{1,0:T(8,128)(2,1)S(1)} %shard_map.56.refs_0_), channel_id=1, source_target_pairs={{16,0},{20,4},{24,8},{28,12},{4,16},{0,20},{12,24},{8,28},{17,1},{... | collective-permute-start | bytes 1228808 | tf_op jit(solution)/shard_map/ppermute | solution.py:251
  11.8 3.4 %collective-permute-start.6 = (bf16[200,1024]{1,0:T(8,128)(2,1)S(1)}, bf16[200,1024]{1,0:T(8,128)(2,1)S(1)}, u32[]{:S(2)}, u32[]{:S(2)}) collective-permute-start(bf16[200,1024]{1,0:T(8,128)(2,1)S(1)} %shard_map.56.refs_0_), channel_id=1, source_target_pairs={{0,4},{8,12},{16,20},{24,28},{1,5},{9,13},{17,21},{25,29},{2,6},{1... | collective-permute-start | bytes 1228808 | tf_op jit(solution)/shard_map/ppermute | solution.py:249
  15.3 11.3 %collective-permute-done.refs_0_ = bf16[200,1024]{1,0:T(8,128)(2,1)S(1)} collective-permute-done((bf16[200,1024]{1,0:T(8,128)(2,1)S(1)}, bf16[200,1024]{1,0:T(8,128)(2,1)S(1)}, u32[]{:S(2)}, u32[]{:S(2)}) %collective-permute-start) | collective-permute-done | bytes 409632 | tf_op jit(solution)/shard_map/ppermute | solution.py:257
  26.7 0.6 shard_map.57.refs_3_.refs_1_
  27.4 1.3 %collective-permute-start.7 = (bf16[400,1024]{1,0:T(8,128)(2,1)S(1)}, bf16[400,1024]{1,0:T(8,128)(2,1)S(1)}, u32[]{:S(2)}, u32[]{:S(2)}) collective-permute-start(bf16[400,1024]{1,0:T(8,128)(2,1)S(1)} %shard_map.57.refs_3_.refs_1_), channel_id=1, source_target_pairs={{0,4},{8,12},{16,20},{24,28},{1,5},{9,13},{17,21},{25,29},{2,6},{1... | collective-permute-start | bytes 2457608 | tf_op jit(solution)/shard_map/ppermute | solution.py:249
  28.7 4.0 %collective-permute-start.2 = (bf16[200,1024]{1,0:T(8,128)(2,1)S(1)}, bf16[200,1024]{1,0:T(8,128)(2,1)S(1)}, u32[]{:S(2)}, u32[]{:S(2)}) collective-permute-start(bf16[200,1024]{1,0:T(8,128)(2,1)S(1)} %get-tuple-element.37), channel_id=1, source_target_pairs={{0,3},{1,2},{2,1},{3,0},{4,7},{5,6},{6,5},{7,4},{8,11},{9,10},{10,... | collective-permute-start | bytes 1228808 | tf_op jit(solution)/shard_map/ppermute | solution.py:259
  32.9 2.5 %collective-permute-start.5 = (bf16[400,1024]{1,0:T(8,128)(2,1)S(1)}, bf16[400,1024]{1,0:T(8,128)(2,1)S(1)}, u32[]{:S(2)}, u32[]{:S(2)}) collective-permute-start(bf16[400,1024]{1,0:T(8,128)(2,1)S(1)} %shard_map.57.refs_3_.refs_1_), channel_id=1, source_target_pairs={{8,0},{12,4},{4,8},{0,12},{28,16},{24,20},{16,24},{20,28},{9,1},{1... | collective-permute-start | bytes 2457608 | tf_op jit(solution)/shard_map/ppermute | solution.py:250
  35.4 2.2 %shard_map.58 = (f32[4,192]{1,0:T(4,128)S(1)}, f32[4,192]{1,0:T(4,128)S(1)}, f32[4,192]{1,0:T(4,128)S(1)}) custom-call(bf16[200,1024]{1,0:T(8,128)(2,1)S(1)} %shard_map.56.refs_0_, bf16[200,1024]{1,0:T(8,128)(2,1)S(1)} %collective-permute-done.3.refs_1_.refs_2_.refs_3_, bf16[200,1024]{1,0:T(8,128)(2,1)S(1)} %collective-permute-done.4.refs_2_.refs_4_.refs_6_, ...), custom_call_target="tpu_custom_call" | custom-call | flops 1 | bytes 1 | tf_op jit(solution)/shard_map/pallas_call | solution.py:202
  37.6 4.1 %collective-permute-done.2.refs_0_ = bf16[200,1024]{1,0:T(8,128)(2,1)S(1)} collective-permute-done((bf16[200,1024]{1,0:T(8,128)(2,1)S(1)}, bf16[200,1024]{1,0:T(8,128)(2,1)S(1)}, u32[]{:S(2)}, u32[]{:S(2)}) %collective-permute-start.2) | collective-permute-done | bytes 409632 | tf_op jit(solution)/shard_map/ppermute | solution.py:259
  42.1 1.3 %collective-permute-start.11 = (bf16[200,1024]{1,0:T(8,128)(2,1)S(1)}, bf16[200,1024]{1,0:T(8,128)(2,1)S(1)}, u32[]{:S(2)}, u32[]{:S(2)}) collective-permute-start(bf16[200,1024]{1,0:T(8,128)(2,1)S(1)} %shard_map.59.refs_2_), channel_id=1, source_target_pairs={{0,4},{8,12},{16,20},{24,28},{1,5},{9,13},{17,21},{25,29},{2,6},{1... | collective-permute-start | bytes 1228808 | tf_op jit(solution)/shard_map/ppermute | solution.py:249
  43.5 2.7 %collective-permute-start.8 = (bf16[200,1024]{1,0:T(8,128)(2,1)S(1)}, bf16[200,1024]{1,0:T(8,128)(2,1)S(1)}, u32[]{:S(2)}, u32[]{:S(2)}) collective-permute-start(bf16[200,1024]{1,0:T(8,128)(2,1)S(1)} %shard_map.59.refs_2_), channel_id=1, source_target_pairs={{8,0},{12,4},{4,8},{0,12},{28,16},{24,20},{16,24},{20,28},{9,1},{1... | collective-permute-start | bytes 1228808 | tf_op jit(solution)/shard_map/ppermute | solution.py:250
  46.2 7.6 %collective-permute-done.9.refs_5_.refs_7_ = bf16[400,1024]{1,0:T(8,128)(2,1)S(1)} collective-permute-done((bf16[400,1024]{1,0:T(8,128)(2,1)S(1)}, bf16[400,1024]{1,0:T(8,128)(2,1)S(1)}, u32[]{:S(2)}, u32[]{:S(2)}) %collective-permute-start.9) | collective-permute-done | bytes 819232 | tf_op jit(solution)/shard_map/ppermute | solution.py:251
  54.1 4.0 %shard_map.60 = (f32[4,192]{1,0:T(4,128)S(1)}, f32[4,192]{1,0:T(4,128)S(1)}, f32[4,192]{1,0:T(4,128)S(1)}) custom-call(bf16[200,1024]{1,0:T(8,128)(2,1)S(1)} %shard_map.56.refs_0_, bf16[400,1024]{1,0:T(8,128)(2,1)S(1)} %shard_map.57.refs_3_.refs_1_, bf16[200,1024]{1,0:T(8,128)(2,1)S(1)} %collective-permute-done.3.refs_1_.refs_2_.refs_3_, ...), custom_call_target="tpu_custom_call" | custom-call | flops 1 | bytes 1 | tf_op jit(solution)/shard_map/pallas_call | solution.py:202
  58.2 1.2 %shard_map.61 = (f32[4,192]{1,0:T(4,128)S(1)}, f32[4,192]{1,0:T(4,128)S(1)}, f32[4,192]{1,0:T(4,128)S(1)}) custom-call(bf16[200,1024]{1,0:T(8,128)(2,1)S(1)} %shard_map.56.refs_0_, bf16[400,1024]{1,0:T(8,128)(2,1)S(1)} %shard_map.57.refs_3_.refs_1_, bf16[200,1024]{1,0:T(8,128)(2,1)S(1)} %shard_map.59.refs_2_, ...), custom_call_target="tpu_custom_call" | custom-call | flops 1 | bytes 1 | tf_op jit(solution)/shard_map/pallas_call | solution.py:202
  59.4 1.3 %collective-permute-done.10.refs_8_ = bf16[200,1024]{1,0:T(8,128)(2,1)S(1)} collective-permute-done((bf16[200,1024]{1,0:T(8,128)(2,1)S(1)}, bf16[200,1024]{1,0:T(8,128)(2,1)S(1)}, u32[]{:S(2)}, u32[]{:S(2)}) %collective-permute-start.10) | collective-permute-done | bytes 409632 | tf_op jit(solution)/shard_map/ppermute | solution.py:251
  60.7 1.7 %collective-permute-done.8.refs_5_ = bf16[200,1024]{1,0:T(8,128)(2,1)S(1)} collective-permute-done((bf16[200,1024]{1,0:T(8,128)(2,1)S(1)}, bf16[200,1024]{1,0:T(8,128)(2,1)S(1)}, u32[]{:S(2)}, u32[]{:S(2)}) %collective-permute-start.8) | collective-permute-done | bytes 409632 | tf_op jit(solution)/shard_map/ppermute | solution.py:250
  62.4 3.4 %shard_map.62 = (f32[4,192]{1,0:T(4,128)S(1)}, f32[4,192]{1,0:T(4,128)S(1)}, f32[4,192]{1,0:T(4,128)S(1)}) custom-call(bf16[200,1024]{1,0:T(8,128)(2,1)S(1)} %shard_map.56.refs_0_, bf16[400,1024]{1,0:T(8,128)(2,1)S(1)} %shard_map.57.refs_3_.refs_1_, bf16[200,1024]{1,0:T(8,128)(2,1)S(1)} %shard_map.59.refs_2_, ...), custom_call_target="tpu_custom_call" | custom-call | flops 1 | bytes 1 | tf_op jit(solution)/shard_map/pallas_call | solution.py:202
  65.8 1.7 %collective-permute-start.13 = (f32[4,192]{1,0:T(4,128)S(1)}, f32[4,192]{1,0:T(4,128)S(1)}, u32[]{:S(2)}, u32[]{:S(2)}) collective-permute-start(f32[4,192]{1,0:T(4,128)S(1)} %get-tuple-element.54), channel_id=1, source_target_pairs={{0,16},{4,20},{8,24},{12,28},{16,4},{20,0},{24,12},{28,8},{1,17},{... | collective-permute-start | bytes 9224 | tf_op jit(solution)/shard_map/ppermute | solution.py:282
  67.5 1.5 %collective-permute-done.12.x_ref = f32[4,192]{1,0:T(4,128)S(1)} collective-permute-done((f32[4,192]{1,0:T(4,128)S(1)}, f32[4,192]{1,0:T(4,128)S(1)}, u32[]{:S(2)}, u32[]{:S(2)}) %collective-permute-start.12) | collective-permute-done | bytes 3104 | tf_op jit(solution)/shard_map/ppermute | solution.py:282
  69.0 0.7 collective-permute-start.14
  69.7 0.4 collective-permute-start.15
  70.1 3.4 %collective-permute-start.16 = (f32[1,192]{1,0:T(1,128)S(1)}, f32[1,192]{1,0:T(1,128)S(1)}, u32[]{:S(2)}, u32[]{:S(2)}) collective-permute-start(f32[1,192]{1,0:T(1,128)S(1)} %get-tuple-element.58), channel_id=1, source_target_pairs={{0,3},{1,2},{2,1},{3,0},{4,7},{5,6},{6,5},{7,4},{8,11},{9,10},{10,... | collective-permute-start | bytes 2312 | tf_op jit(solution)/shard_map/ppermute | solution.py:284
  73.5 0.7 collective-permute-done.15.refs_2_
  74.2 1.3 %collective-permute-done.16.refs_3_ = f32[1,192]{1,0:T(1,128)S(1)} collective-permute-done((f32[1,192]{1,0:T(1,128)S(1)}, f32[1,192]{1,0:T(1,128)S(1)}, u32[]{:S(2)}, u32[]{:S(2)}) %collective-permute-start.16) | collective-permute-done | bytes 800 | tf_op jit(solution)/shard_map/ppermute | solution.py:284
  75.5 0.8 %shard_map.64 = f32[1,512]{1,0:T(1,128)} custom-call(s32[8,512]{1,0:T(8,128)S(1)} %get-tuple-element.32.place_ref, f32[1,192]{1,0:T(1,128)S(1)} %get-tuple-element.55.refs_0_, f32[1,192]{1,0:T(1,128)S(1)} %collective-permute-done.14.refs_1_, f32[1,192]{1,0:T(1,128)S(1)} %collective-permute-done.15.refs_2_, f32[1,192]{1,0:T(1,128)S(1)} %collective-permute-done.16.refs_3_), custom_call_target="tpu_custom_call" | custom-call | tf_op jit(solution)/shard_map/pallas_call | solution.py:286
  (21 shorter events, 1.5 us)
Async XLA Ops:
  0.7 0.7 copy-start.3
  0.7 0.7 copy-start.2
  1.4 1.2 %copy-start = (bf16[512,1024]{1,0:T(8,128)(2,1)S(1)}, bf16[512,1024]{1,0:T(8,128)(2,1)}, u32[]{:S(2)}) copy-start(bf16[512,1024]{1,0:T(8,128)(2,1)} %codes_ref.1) | copy-start | bytes 3145732
  4.1 5.7 %copy-start.1 = (bf16[2,1024]{1,0:T(2,128)(2,1)S(1)}, bf16[2,1024]{1,0:T(2,128)(2,1)}, u32[]{:S(2)}) copy-start(bf16[2,1024]{1,0:T(2,128)(2,1)} %refs_1_.3) | copy-start | bytes 12292
  4.1 22.5 %collective-permute-start = (bf16[200,1024]{1,0:T(8,128)(2,1)S(1)}, bf16[200,1024]{1,0:T(8,128)(2,1)S(1)}, u32[]{:S(2)}, u32[]{:S(2)}) collective-permute-start(bf16[200,1024]{1,0:T(8,128)(2,1)S(1)} %get-tuple-element.34), channel_id=1, source_target_pairs={{0,2},{1,3},{2,0},{3,1},{4,6},{5,7},{6,4},{7,5},{8,10},{9,11},{10,... | collective-permute-start | bytes 1228808 | tf_op jit(solution)/shard_map/ppermute | solution.py:257
  8.2 18.5 %collective-permute-start.1 = (bf16[200,1024]{1,0:T(8,128)(2,1)S(1)}, bf16[200,1024]{1,0:T(8,128)(2,1)S(1)}, u32[]{:S(2)}, u32[]{:S(2)}) collective-permute-start(bf16[200,1024]{1,0:T(8,128)(2,1)S(1)} %get-tuple-element.35), channel_id=1, source_target_pairs={{0,1},{1,0},{2,3},{3,2},{4,5},{5,4},{6,7},{7,6},{8,9},{9,8},{10,11... | collective-permute-start | bytes 1228808 | tf_op jit(solution)/shard_map/ppermute | solution.py:258
  10.2 17.2 %collective-permute-start.3 = (bf16[200,1024]{1,0:T(8,128)(2,1)S(1)}, bf16[200,1024]{1,0:T(8,128)(2,1)S(1)}, u32[]{:S(2)}, u32[]{:S(2)}) collective-permute-start(bf16[200,1024]{1,0:T(8,128)(2,1)S(1)} %shard_map.56.refs_0_), channel_id=1, source_target_pairs={{8,0},{12,4},{4,8},{0,12},{28,16},{24,20},{16,24},{20,28},{9,1},{1... | collective-permute-start | bytes 1228808 | tf_op jit(solution)/shard_map/ppermute | solution.py:250
  10.6 16.8 %collective-permute-start.4 = (bf16[200,1024]{1,0:T(8,128)(2,1)S(1)}, bf16[200,1024]{1,0:T(8,128)(2,1)S(1)}, u32[]{:S(2)}, u32[]{:S(2)}) collective-permute-start(bf16[200,1024]{1,0:T(8,128)(2,1)S(1)} %shard_map.56.refs_0_), channel_id=1, source_target_pairs={{16,0},{20,4},{24,8},{28,12},{4,16},{0,20},{12,24},{8,28},{17,1},{... | collective-permute-start | bytes 1228808 | tf_op jit(solution)/shard_map/ppermute | solution.py:251
  11.8 15.6 %collective-permute-start.6 = (bf16[200,1024]{1,0:T(8,128)(2,1)S(1)}, bf16[200,1024]{1,0:T(8,128)(2,1)S(1)}, u32[]{:S(2)}, u32[]{:S(2)}) collective-permute-start(bf16[200,1024]{1,0:T(8,128)(2,1)S(1)} %shard_map.56.refs_0_), channel_id=1, source_target_pairs={{0,4},{8,12},{16,20},{24,28},{1,5},{9,13},{17,21},{25,29},{2,6},{1... | collective-permute-start | bytes 1228808 | tf_op jit(solution)/shard_map/ppermute | solution.py:249
  27.4 14.7 %collective-permute-start.7 = (bf16[400,1024]{1,0:T(8,128)(2,1)S(1)}, bf16[400,1024]{1,0:T(8,128)(2,1)S(1)}, u32[]{:S(2)}, u32[]{:S(2)}) collective-permute-start(bf16[400,1024]{1,0:T(8,128)(2,1)S(1)} %shard_map.57.refs_3_.refs_1_), channel_id=1, source_target_pairs={{0,4},{8,12},{16,20},{24,28},{1,5},{9,13},{17,21},{25,29},{2,6},{1... | collective-permute-start | bytes 2457608 | tf_op jit(solution)/shard_map/ppermute | solution.py:249
  28.7 13.0 %collective-permute-start.2 = (bf16[200,1024]{1,0:T(8,128)(2,1)S(1)}, bf16[200,1024]{1,0:T(8,128)(2,1)S(1)}, u32[]{:S(2)}, u32[]{:S(2)}) collective-permute-start(bf16[200,1024]{1,0:T(8,128)(2,1)S(1)} %get-tuple-element.37), channel_id=1, source_target_pairs={{0,3},{1,2},{2,1},{3,0},{4,7},{5,6},{6,5},{7,4},{8,11},{9,10},{10,... | collective-permute-start | bytes 1228808 | tf_op jit(solution)/shard_map/ppermute | solution.py:259
  32.7 21.2 %collective-permute-start.9 = (bf16[400,1024]{1,0:T(8,128)(2,1)S(1)}, bf16[400,1024]{1,0:T(8,128)(2,1)S(1)}, u32[]{:S(2)}, u32[]{:S(2)}) collective-permute-start(bf16[400,1024]{1,0:T(8,128)(2,1)S(1)} %shard_map.57.refs_3_.refs_1_), channel_id=1, source_target_pairs={{16,0},{20,4},{24,8},{28,12},{4,16},{0,20},{12,24},{8,28},{17,1},{... | collective-permute-start | bytes 2457608 | tf_op jit(solution)/shard_map/ppermute | solution.py:251
  32.9 21.2 %collective-permute-start.5 = (bf16[400,1024]{1,0:T(8,128)(2,1)S(1)}, bf16[400,1024]{1,0:T(8,128)(2,1)S(1)}, u32[]{:S(2)}, u32[]{:S(2)}) collective-permute-start(bf16[400,1024]{1,0:T(8,128)(2,1)S(1)} %shard_map.57.refs_3_.refs_1_), channel_id=1, source_target_pairs={{8,0},{12,4},{4,8},{0,12},{28,16},{24,20},{16,24},{20,28},{9,1},{1... | collective-permute-start | bytes 2457608 | tf_op jit(solution)/shard_map/ppermute | solution.py:250
  42.1 16.1 %collective-permute-start.11 = (bf16[200,1024]{1,0:T(8,128)(2,1)S(1)}, bf16[200,1024]{1,0:T(8,128)(2,1)S(1)}, u32[]{:S(2)}, u32[]{:S(2)}) collective-permute-start(bf16[200,1024]{1,0:T(8,128)(2,1)S(1)} %shard_map.59.refs_2_), channel_id=1, source_target_pairs={{0,4},{8,12},{16,20},{24,28},{1,5},{9,13},{17,21},{25,29},{2,6},{1... | collective-permute-start | bytes 1228808 | tf_op jit(solution)/shard_map/ppermute | solution.py:249
  43.5 17.2 %collective-permute-start.10 = (bf16[200,1024]{1,0:T(8,128)(2,1)S(1)}, bf16[200,1024]{1,0:T(8,128)(2,1)S(1)}, u32[]{:S(2)}, u32[]{:S(2)}) collective-permute-start(bf16[200,1024]{1,0:T(8,128)(2,1)S(1)} %shard_map.59.refs_2_), channel_id=1, source_target_pairs={{16,0},{20,4},{24,8},{28,12},{4,16},{0,20},{12,24},{8,28},{17,1},{... | collective-permute-start | bytes 1228808 | tf_op jit(solution)/shard_map/ppermute | solution.py:251
  43.5 18.8 %collective-permute-start.8 = (bf16[200,1024]{1,0:T(8,128)(2,1)S(1)}, bf16[200,1024]{1,0:T(8,128)(2,1)S(1)}, u32[]{:S(2)}, u32[]{:S(2)}) collective-permute-start(bf16[200,1024]{1,0:T(8,128)(2,1)S(1)} %shard_map.59.refs_2_), channel_id=1, source_target_pairs={{8,0},{12,4},{4,8},{0,12},{28,16},{24,20},{16,24},{20,28},{9,1},{1... | collective-permute-start | bytes 1228808 | tf_op jit(solution)/shard_map/ppermute | solution.py:250
  65.8 3.2 %collective-permute-start.12 = (f32[4,192]{1,0:T(4,128)S(1)}, f32[4,192]{1,0:T(4,128)S(1)}, u32[]{:S(2)}, u32[]{:S(2)}) collective-permute-start(f32[4,192]{1,0:T(4,128)S(1)} %get-tuple-element.53), channel_id=1, source_target_pairs={{0,8},{4,12},{8,4},{12,0},{16,28},{20,24},{24,16},{28,20},{1,9},{5... | collective-permute-start | bytes 9224 | tf_op jit(solution)/shard_map/ppermute | solution.py:282
  65.8 3.2 %collective-permute-start.13 = (f32[4,192]{1,0:T(4,128)S(1)}, f32[4,192]{1,0:T(4,128)S(1)}, u32[]{:S(2)}, u32[]{:S(2)}) collective-permute-start(f32[4,192]{1,0:T(4,128)S(1)} %get-tuple-element.54), channel_id=1, source_target_pairs={{0,16},{4,20},{8,24},{12,28},{16,4},{20,0},{24,12},{28,8},{1,17},{... | collective-permute-start | bytes 9224 | tf_op jit(solution)/shard_map/ppermute | solution.py:282
  69.0 4.5 %collective-permute-start.14 = (f32[1,192]{1,0:T(1,128)S(1)}, f32[1,192]{1,0:T(1,128)S(1)}, u32[]{:S(2)}, u32[]{:S(2)}) collective-permute-start(f32[1,192]{1,0:T(1,128)S(1)} %get-tuple-element.56), channel_id=1, source_target_pairs={{0,1},{1,0},{2,3},{3,2},{4,5},{5,4},{6,7},{7,6},{8,9},{9,8},{10,11... | collective-permute-start | bytes 2312 | tf_op jit(solution)/shard_map/ppermute | solution.py:284
  69.7 4.5 %collective-permute-start.15 = (f32[1,192]{1,0:T(1,128)S(1)}, f32[1,192]{1,0:T(1,128)S(1)}, u32[]{:S(2)}, u32[]{:S(2)}) collective-permute-start(f32[1,192]{1,0:T(1,128)S(1)} %get-tuple-element.57), channel_id=1, source_target_pairs={{0,2},{1,3},{2,0},{3,1},{4,6},{5,7},{6,4},{7,5},{8,10},{9,11},{10,... | collective-permute-start | bytes 2312 | tf_op jit(solution)/shard_map/ppermute | solution.py:284
  70.1 5.4 %collective-permute-start.16 = (f32[1,192]{1,0:T(1,128)S(1)}, f32[1,192]{1,0:T(1,128)S(1)}, u32[]{:S(2)}, u32[]{:S(2)}) collective-permute-start(f32[1,192]{1,0:T(1,128)S(1)} %get-tuple-element.58), channel_id=1, source_target_pairs={{0,3},{1,2},{2,1},{3,0},{4,7},{5,6},{6,5},{7,4},{8,11},{9,10},{10,... | collective-permute-start | bytes 2312 | tf_op jit(solution)/shard_map/ppermute | solution.py:284

commit v5 on v4

--- a/solution.py
+++ b/solution.py
@@ -117,14 +117,19 @@
             for chunk in chunks if late_chunk in fresh else fresh:
                 scores = dot_last(rows_of(early, chunk), rows_of(late, late_chunk))
                 first, both = sizes(early, chunk)
-                low = jnp.where(late_first, 0, first)
-                high = jnp.where(late_first, first, both)
                 if early == late:
+                    low = jnp.where(late_first, 0, first)
+                    high = jnp.where(late_first, first, both)
                     if chunk == late_chunk:
                         high = jnp.minimum(high, lane)
                     else:
                         high = jnp.where((group_pos ^ chunk) < (group_pos ^ late_chunk), high, 0)
-                kept = jnp.where((row >= low) & (row < high), scores, -1.0)
+                    allowed = (row >= low) & (row < high)
+                else:
+                    column = iota((cap, 1), 0)
+                    code = jnp.where(column < first, 0, jnp.where(column < both, 1, 2))
+                    allowed = code == jnp.where(late_first, 0, 1)
+                kept = jnp.where(allowed, scores, -1.0)
                 best = jnp.maximum(best, jnp.max(kept, axis=0, keepdims=True))
             best_refs[late][late_chunk : late_chunk + 1, :] = best
 

time: 76.6 us -> 75.8 us (0.990)
  Pallas kernels: 14.4 us -> 12.8 us
  waiting for transfers between devices: 30 us -> 30.9 us
    pallas_call x4, Pallas kernels: 10.8 us -> 9.15 us  [score_call(): pl.pallas_call(functools.partial(score_kernel, cap, keys, jobs), out_shap...]
    ppermute x3, waiting for transfers between devices: 8.95 us -> 9.84 us  [spread(): y_block[part] = lax.ppermute(after(unit, *y_after), 'blk', to_y)]
  transfers between devices with their start and end apart: 17 -> 17, of which waited for: 10 -> 11; matrix products, arithmetic and copies ran while one was open for 0% -> 0% of each run, Pallas kernels for 11% -> 10%
where the time goes in v5:
time: 75.8 us; the launch traced here: 75.6 us
  waiting for transfers between devices  30.9 us (41%)
  starting transfers between devices  29.1 us (38%)
  Pallas kernels  12.8 us (17%)
  local copies, waits for them, and re-layouts  1.93 us (3%)
    ppermute x1, waiting for transfers between devices, paired_shards(): at_two = lax.ppermute(packed[2], 'group', hops[2])  11.3 us
    ppermute x3, waiting for transfers between devices, spread(): y_block[part] = lax.ppermute(after(unit, *y_after), 'blk', to_y)  9.84 us
    pallas_call x4, Pallas kernels, score_call(): pl.pallas_call(functools.partial(score_kernel, cap, keys, jobs), out_shap...  9.15 us
    ppermute x3, starting transfers between devices, spread(): sib[part] = lax.ppermute(after(unit, *sib_after), 'blk', to_sib)  6.09 us
    ppermute x3, starting transfers between devices, spread(): x_block[part] = lax.ppermute(after(unit, *x_after), 'blk', to_x)  5.69 us
    ppermute x3, starting transfers between devices, paired_shards(): lax.ppermute(returned[s], 'group', hops[s])  4.44 us
    ppermute x1, waiting for transfers between devices, paired_shards(): at_three = lax.ppermute(after(packed[3], at_two), 'group', hops[3])  4.17 us
    ppermute x1, starting transfers between devices, paired_shards(): at_two = lax.ppermute(packed[2], 'group', hops[2])  4.11 us
  transfers between devices with their start and end apart: 17, of which 11 were waited for; matrix products, arithmetic and copies ran while one was open for 0% of the time, Pallas kernels for 10%

profile of v5, /device:TPU:0, one launch (start us, length us, event | category | flops | bytes accessed | tf_op | source)
XLA Modules:
  0.0 75.6 jit_solution(13935600323000605696)
XLA Ops:
  0.0 0.7 reshape.19
  0.7 0.7 copy-done.3
  1.4 1.2 %copy-done = bf16[512,1024]{1,0:T(8,128)(2,1)S(1)} copy-done((bf16[512,1024]{1,0:T(8,128)(2,1)S(1)}, bf16[512,1024]{1,0:T(8,128)(2,1)}, u32[]{:S(2)}) %copy-start) | copy-done | bytes 1048600
  2.6 1.5 %shard_map.55 = (bf16[200,1024]{1,0:T(8,128)(2,1)S(1)}, bf16[200,1024]{1,0:T(8,128)(2,1)S(1)}, bf16[200,1024]{1,0:T(8,128)(2,1)S(1)}, bf16[200,1024]{1,0:T(8,128)(2,1)S(1)}, s32[8,512]{1,0:T(8,128)S(1)}) custom-call(s32[1,512]{1,0:T(1,128)S(1)} %bitcast.5, s32[1,512]{1,0:T(1,128)S(1)} %bitcast.6, f32[1,512]{1,0:T(1,128)S(1)} %bitcast.4, ...), custom_call_target="tpu_custom_call" | custom-call | tf_op jit(solution)/shard_map/pallas_call | solution.py:226
  4.1 4.1 %collective-permute-start = (bf16[200,1024]{1,0:T(8,128)(2,1)S(1)}, bf16[200,1024]{1,0:T(8,128)(2,1)S(1)}, u32[]{:S(2)}, u32[]{:S(2)}) collective-permute-start(bf16[200,1024]{1,0:T(8,128)(2,1)S(1)} %get-tuple-element.34), channel_id=1, source_target_pairs={{0,2},{1,3},{2,0},{3,1},{4,6},{5,7},{6,4},{7,5},{8,10},{9,11},{10,... | collective-permute-start | bytes 1228808 | tf_op jit(solution)/shard_map/ppermute | solution.py:262
  8.2 1.6 %collective-permute-start.1 = (bf16[200,1024]{1,0:T(8,128)(2,1)S(1)}, bf16[200,1024]{1,0:T(8,128)(2,1)S(1)}, u32[]{:S(2)}, u32[]{:S(2)}) collective-permute-start(bf16[200,1024]{1,0:T(8,128)(2,1)S(1)} %get-tuple-element.35), channel_id=1, source_target_pairs={{0,1},{1,0},{2,3},{3,2},{4,5},{5,4},{6,7},{7,6},{8,9},{9,8},{10,11... | collective-permute-start | bytes 1228808 | tf_op jit(solution)/shard_map/ppermute | solution.py:263
  10.2 0.4 collective-permute-start.3
  10.6 1.2 %collective-permute-start.4 = (bf16[200,1024]{1,0:T(8,128)(2,1)S(1)}, bf16[200,1024]{1,0:T(8,128)(2,1)S(1)}, u32[]{:S(2)}, u32[]{:S(2)}) collective-permute-start(bf16[200,1024]{1,0:T(8,128)(2,1)S(1)} %shard_map.56.refs_0_), channel_id=1, source_target_pairs={{16,0},{20,4},{24,8},{28,12},{4,16},{0,20},{12,24},{8,28},{17,1},{... | collective-permute-start | bytes 1228808 | tf_op jit(solution)/shard_map/ppermute | solution.py:256
  11.8 3.4 %collective-permute-start.6 = (bf16[200,1024]{1,0:T(8,128)(2,1)S(1)}, bf16[200,1024]{1,0:T(8,128)(2,1)S(1)}, u32[]{:S(2)}, u32[]{:S(2)}) collective-permute-start(bf16[200,1024]{1,0:T(8,128)(2,1)S(1)} %shard_map.56.refs_0_), channel_id=1, source_target_pairs={{0,4},{8,12},{16,20},{24,28},{1,5},{9,13},{17,21},{25,29},{2,6},{1... | collective-permute-start | bytes 1228808 | tf_op jit(solution)/shard_map/ppermute | solution.py:254
  15.3 11.3 %collective-permute-done.refs_0_ = bf16[200,1024]{1,0:T(8,128)(2,1)S(1)} collective-permute-done((bf16[200,1024]{1,0:T(8,128)(2,1)S(1)}, bf16[200,1024]{1,0:T(8,128)(2,1)S(1)}, u32[]{:S(2)}, u32[]{:S(2)}) %collective-permute-start) | collective-permute-done | bytes 409632 | tf_op jit(solution)/shard_map/ppermute | solution.py:262
  26.7 0.6 shard_map.57.refs_3_.refs_1_
  27.4 1.3 %collective-permute-start.7 = (bf16[400,1024]{1,0:T(8,128)(2,1)S(1)}, bf16[400,1024]{1,0:T(8,128)(2,1)S(1)}, u32[]{:S(2)}, u32[]{:S(2)}) collective-permute-start(bf16[400,1024]{1,0:T(8,128)(2,1)S(1)} %shard_map.57.refs_3_.refs_1_), channel_id=1, source_target_pairs={{0,4},{8,12},{16,20},{24,28},{1,5},{9,13},{17,21},{25,29},{2,6},{1... | collective-permute-start | bytes 2457608 | tf_op jit(solution)/shard_map/ppermute | solution.py:254
  28.7 4.0 %collective-permute-start.2 = (bf16[200,1024]{1,0:T(8,128)(2,1)S(1)}, bf16[200,1024]{1,0:T(8,128)(2,1)S(1)}, u32[]{:S(2)}, u32[]{:S(2)}) collective-permute-start(bf16[200,1024]{1,0:T(8,128)(2,1)S(1)} %get-tuple-element.37), channel_id=1, source_target_pairs={{0,3},{1,2},{2,1},{3,0},{4,7},{5,6},{6,5},{7,4},{8,11},{9,10},{10,... | collective-permute-start | bytes 1228808 | tf_op jit(solution)/shard_map/ppermute | solution.py:264
  32.9 2.5 %collective-permute-start.5 = (bf16[400,1024]{1,0:T(8,128)(2,1)S(1)}, bf16[400,1024]{1,0:T(8,128)(2,1)S(1)}, u32[]{:S(2)}, u32[]{:S(2)}) collective-permute-start(bf16[400,1024]{1,0:T(8,128)(2,1)S(1)} %shard_map.57.refs_3_.refs_1_), channel_id=1, source_target_pairs={{8,0},{12,4},{4,8},{0,12},{28,16},{24,20},{16,24},{20,28},{9,1},{1... | collective-permute-start | bytes 2457608 | tf_op jit(solution)/shard_map/ppermute | solution.py:255
  35.4 2.2 %shard_map.58 = (f32[4,192]{1,0:T(4,128)S(1)}, f32[4,192]{1,0:T(4,128)S(1)}, f32[4,192]{1,0:T(4,128)S(1)}) custom-call(bf16[200,1024]{1,0:T(8,128)(2,1)S(1)} %shard_map.56.refs_0_, bf16[200,1024]{1,0:T(8,128)(2,1)S(1)} %collective-permute-done.3.refs_1_.refs_2_.refs_3_, bf16[200,1024]{1,0:T(8,128)(2,1)S(1)} %collective-permute-done.4.refs_2_.refs_4_.refs_6_, ...), custom_call_target="tpu_custom_call" | custom-call | flops 1 | bytes 1 | tf_op jit(solution)/shard_map/pallas_call | solution.py:207
  37.6 4.2 %collective-permute-done.2.refs_0_ = bf16[200,1024]{1,0:T(8,128)(2,1)S(1)} collective-permute-done((bf16[200,1024]{1,0:T(8,128)(2,1)S(1)}, bf16[200,1024]{1,0:T(8,128)(2,1)S(1)}, u32[]{:S(2)}, u32[]{:S(2)}) %collective-permute-start.2) | collective-permute-done | bytes 409632 | tf_op jit(solution)/shard_map/ppermute | solution.py:264
  42.1 1.3 %collective-permute-start.11 = (bf16[200,1024]{1,0:T(8,128)(2,1)S(1)}, bf16[200,1024]{1,0:T(8,128)(2,1)S(1)}, u32[]{:S(2)}, u32[]{:S(2)}) collective-permute-start(bf16[200,1024]{1,0:T(8,128)(2,1)S(1)} %shard_map.59.refs_2_), channel_id=1, source_target_pairs={{0,4},{8,12},{16,20},{24,28},{1,5},{9,13},{17,21},{25,29},{2,6},{1... | collective-permute-start | bytes 1228808 | tf_op jit(solution)/shard_map/ppermute | solution.py:254
  43.5 2.7 %collective-permute-start.8 = (bf16[200,1024]{1,0:T(8,128)(2,1)S(1)}, bf16[200,1024]{1,0:T(8,128)(2,1)S(1)}, u32[]{:S(2)}, u32[]{:S(2)}) collective-permute-start(bf16[200,1024]{1,0:T(8,128)(2,1)S(1)} %shard_map.59.refs_2_), channel_id=1, source_target_pairs={{8,0},{12,4},{4,8},{0,12},{28,16},{24,20},{16,24},{20,28},{9,1},{1... | collective-permute-start | bytes 1228808 | tf_op jit(solution)/shard_map/ppermute | solution.py:255
  46.2 7.6 %collective-permute-done.9.refs_5_.refs_7_ = bf16[400,1024]{1,0:T(8,128)(2,1)S(1)} collective-permute-done((bf16[400,1024]{1,0:T(8,128)(2,1)S(1)}, bf16[400,1024]{1,0:T(8,128)(2,1)S(1)}, u32[]{:S(2)}, u32[]{:S(2)}) %collective-permute-start.9) | collective-permute-done | bytes 819232 | tf_op jit(solution)/shard_map/ppermute | solution.py:256
  54.1 3.2 %shard_map.60 = (f32[4,192]{1,0:T(4,128)S(1)}, f32[4,192]{1,0:T(4,128)S(1)}, f32[4,192]{1,0:T(4,128)S(1)}) custom-call(bf16[200,1024]{1,0:T(8,128)(2,1)S(1)} %shard_map.56.refs_0_, bf16[400,1024]{1,0:T(8,128)(2,1)S(1)} %shard_map.57.refs_3_.refs_1_, bf16[200,1024]{1,0:T(8,128)(2,1)S(1)} %collective-permute-done.3.refs_1_.refs_2_.refs_3_, ...), custom_call_target="tpu_custom_call" | custom-call | flops 1 | bytes 1 | tf_op jit(solution)/shard_map/pallas_call | solution.py:207
  57.3 1.2 %shard_map.61 = (f32[4,192]{1,0:T(4,128)S(1)}, f32[4,192]{1,0:T(4,128)S(1)}, f32[4,192]{1,0:T(4,128)S(1)}) custom-call(bf16[200,1024]{1,0:T(8,128)(2,1)S(1)} %shard_map.56.refs_0_, bf16[400,1024]{1,0:T(8,128)(2,1)S(1)} %shard_map.57.refs_3_.refs_1_, bf16[200,1024]{1,0:T(8,128)(2,1)S(1)} %shard_map.59.refs_2_, ...), custom_call_target="tpu_custom_call" | custom-call | flops 1 | bytes 1 | tf_op jit(solution)/shard_map/pallas_call | solution.py:207
  58.5 2.2 %collective-permute-done.10.refs_8_ = bf16[200,1024]{1,0:T(8,128)(2,1)S(1)} collective-permute-done((bf16[200,1024]{1,0:T(8,128)(2,1)S(1)}, bf16[200,1024]{1,0:T(8,128)(2,1)S(1)}, u32[]{:S(2)}, u32[]{:S(2)}) %collective-permute-start.10) | collective-permute-done | bytes 409632 | tf_op jit(solution)/shard_map/ppermute | solution.py:256
  60.7 1.7 %collective-permute-done.8.refs_5_ = bf16[200,1024]{1,0:T(8,128)(2,1)S(1)} collective-permute-done((bf16[200,1024]{1,0:T(8,128)(2,1)S(1)}, bf16[200,1024]{1,0:T(8,128)(2,1)S(1)}, u32[]{:S(2)}, u32[]{:S(2)}) %collective-permute-start.8) | collective-permute-done | bytes 409632 | tf_op jit(solution)/shard_map/ppermute | solution.py:255
  62.4 2.7 %shard_map.62 = (f32[4,192]{1,0:T(4,128)S(1)}, f32[4,192]{1,0:T(4,128)S(1)}, f32[4,192]{1,0:T(4,128)S(1)}) custom-call(bf16[200,1024]{1,0:T(8,128)(2,1)S(1)} %shard_map.56.refs_0_, bf16[400,1024]{1,0:T(8,128)(2,1)S(1)} %shard_map.57.refs_3_.refs_1_, bf16[200,1024]{1,0:T(8,128)(2,1)S(1)} %shard_map.59.refs_2_, ...), custom_call_target="tpu_custom_call" | custom-call | flops 1 | bytes 1 | tf_op jit(solution)/shard_map/pallas_call | solution.py:207
  65.1 1.7 %collective-permute-start.13 = (f32[4,192]{1,0:T(4,128)S(1)}, f32[4,192]{1,0:T(4,128)S(1)}, u32[]{:S(2)}, u32[]{:S(2)}) collective-permute-start(f32[4,192]{1,0:T(4,128)S(1)} %get-tuple-element.54), channel_id=1, source_target_pairs={{0,16},{4,20},{8,24},{12,28},{16,4},{20,0},{24,12},{28,8},{1,17},{... | collective-permute-start | bytes 9224 | tf_op jit(solution)/shard_map/ppermute | solution.py:287
  66.8 1.3 %collective-permute-done.12.x_ref = f32[4,192]{1,0:T(4,128)S(1)} collective-permute-done((f32[4,192]{1,0:T(4,128)S(1)}, f32[4,192]{1,0:T(4,128)S(1)}, u32[]{:S(2)}, u32[]{:S(2)}) %collective-permute-start.12) | collective-permute-done | bytes 3104 | tf_op jit(solution)/shard_map/ppermute | solution.py:287
  68.2 0.8 %collective-permute-start.14 = (f32[1,192]{1,0:T(1,128)S(1)}, f32[1,192]{1,0:T(1,128)S(1)}, u32[]{:S(2)}, u32[]{:S(2)}) collective-permute-start(f32[1,192]{1,0:T(1,128)S(1)} %get-tuple-element.56), channel_id=1, source_target_pairs={{0,1},{1,0},{2,3},{3,2},{4,5},{5,4},{6,7},{7,6},{8,9},{9,8},{10,11... | collective-permute-start | bytes 2312 | tf_op jit(solution)/shard_map/ppermute | solution.py:289
  69.0 0.4 collective-permute-start.15
  69.4 3.3 %collective-permute-start.16 = (f32[1,192]{1,0:T(1,128)S(1)}, f32[1,192]{1,0:T(1,128)S(1)}, u32[]{:S(2)}, u32[]{:S(2)}) collective-permute-start(f32[1,192]{1,0:T(1,128)S(1)} %get-tuple-element.58), channel_id=1, source_target_pairs={{0,3},{1,2},{2,1},{3,0},{4,7},{5,6},{6,5},{7,4},{8,11},{9,10},{10,... | collective-permute-start | bytes 2312 | tf_op jit(solution)/shard_map/ppermute | solution.py:289
  72.7 0.8 %collective-permute-done.15.refs_2_ = f32[1,192]{1,0:T(1,128)S(1)} collective-permute-done((f32[1,192]{1,0:T(1,128)S(1)}, f32[1,192]{1,0:T(1,128)S(1)}, u32[]{:S(2)}, u32[]{:S(2)}) %collective-permute-start.15) | collective-permute-done | bytes 800 | tf_op jit(solution)/shard_map/ppermute | solution.py:289
  73.5 1.3 %collective-permute-done.16.refs_3_ = f32[1,192]{1,0:T(1,128)S(1)} collective-permute-done((f32[1,192]{1,0:T(1,128)S(1)}, f32[1,192]{1,0:T(1,128)S(1)}, u32[]{:S(2)}, u32[]{:S(2)}) %collective-permute-start.16) | collective-permute-done | bytes 800 | tf_op jit(solution)/shard_map/ppermute | solution.py:289
  74.7 0.8 %shard_map.64 = f32[1,512]{1,0:T(1,128)} custom-call(s32[8,512]{1,0:T(8,128)S(1)} %get-tuple-element.32.place_ref, f32[1,192]{1,0:T(1,128)S(1)} %get-tuple-element.55.refs_0_, f32[1,192]{1,0:T(1,128)S(1)} %collective-permute-done.14.refs_1_, f32[1,192]{1,0:T(1,128)S(1)} %collective-permute-done.15.refs_2_, f32[1,192]{1,0:T(1,128)S(1)} %collective-permute-done.16.refs_3_), custom_call_target="tpu_custom_call" | custom-call | tf_op jit(solution)/shard_map/pallas_call | solution.py:291
  (21 shorter events, 1.6 us)
Async XLA Ops:
  0.7 0.7 copy-start.3
  0.7 0.7 copy-start.2
  1.4 1.2 %copy-start = (bf16[512,1024]{1,0:T(8,128)(2,1)S(1)}, bf16[512,1024]{1,0:T(8,128)(2,1)}, u32[]{:S(2)}) copy-start(bf16[512,1024]{1,0:T(8,128)(2,1)} %codes_ref.1) | copy-start | bytes 3145732
  4.1 5.7 %copy-start.1 = (bf16[2,1024]{1,0:T(2,128)(2,1)S(1)}, bf16[2,1024]{1,0:T(2,128)(2,1)}, u32[]{:S(2)}) copy-start(bf16[2,1024]{1,0:T(2,128)(2,1)} %refs_1_.3) | copy-start | bytes 12292
  4.1 22.5 %collective-permute-start = (bf16[200,1024]{1,0:T(8,128)(2,1)S(1)}, bf16[200,1024]{1,0:T(8,128)(2,1)S(1)}, u32[]{:S(2)}, u32[]{:S(2)}) collective-permute-start(bf16[200,1024]{1,0:T(8,128)(2,1)S(1)} %get-tuple-element.34), channel_id=1, source_target_pairs={{0,2},{1,3},{2,0},{3,1},{4,6},{5,7},{6,4},{7,5},{8,10},{9,11},{10,... | collective-permute-start | bytes 1228808 | tf_op jit(solution)/shard_map/ppermute | solution.py:262
  8.2 18.5 %collective-permute-start.1 = (bf16[200,1024]{1,0:T(8,128)(2,1)S(1)}, bf16[200,1024]{1,0:T(8,128)(2,1)S(1)}, u32[]{:S(2)}, u32[]{:S(2)}) collective-permute-start(bf16[200,1024]{1,0:T(8,128)(2,1)S(1)} %get-tuple-element.35), channel_id=1, source_target_pairs={{0,1},{1,0},{2,3},{3,2},{4,5},{5,4},{6,7},{7,6},{8,9},{9,8},{10,11... | collective-permute-start | bytes 1228808 | tf_op jit(solution)/shard_map/ppermute | solution.py:263
  10.2 17.2 %collective-permute-start.3 = (bf16[200,1024]{1,0:T(8,128)(2,1)S(1)}, bf16[200,1024]{1,0:T(8,128)(2,1)S(1)}, u32[]{:S(2)}, u32[]{:S(2)}) collective-permute-start(bf16[200,1024]{1,0:T(8,128)(2,1)S(1)} %shard_map.56.refs_0_), channel_id=1, source_target_pairs={{8,0},{12,4},{4,8},{0,12},{28,16},{24,20},{16,24},{20,28},{9,1},{1... | collective-permute-start | bytes 1228808 | tf_op jit(solution)/shard_map/ppermute | solution.py:255
  10.6 16.8 %collective-permute-start.4 = (bf16[200,1024]{1,0:T(8,128)(2,1)S(1)}, bf16[200,1024]{1,0:T(8,128)(2,1)S(1)}, u32[]{:S(2)}, u32[]{:S(2)}) collective-permute-start(bf16[200,1024]{1,0:T(8,128)(2,1)S(1)} %shard_map.56.refs_0_), channel_id=1, source_target_pairs={{16,0},{20,4},{24,8},{28,12},{4,16},{0,20},{12,24},{8,28},{17,1},{... | collective-permute-start | bytes 1228808 | tf_op jit(solution)/shard_map/ppermute | solution.py:256
  11.8 15.6 %collective-permute-start.6 = (bf16[200,1024]{1,0:T(8,128)(2,1)S(1)}, bf16[200,1024]{1,0:T(8,128)(2,1)S(1)}, u32[]{:S(2)}, u32[]{:S(2)}) collective-permute-start(bf16[200,1024]{1,0:T(8,128)(2,1)S(1)} %shard_map.56.refs_0_), channel_id=1, source_target_pairs={{0,4},{8,12},{16,20},{24,28},{1,5},{9,13},{17,21},{25,29},{2,6},{1... | collective-permute-start | bytes 1228808 | tf_op jit(solution)/shard_map/ppermute | solution.py:254
  27.4 14.7 %collective-permute-start.7 = (bf16[400,1024]{1,0:T(8,128)(2,1)S(1)}, bf16[400,1024]{1,0:T(8,128)(2,1)S(1)}, u32[]{:S(2)}, u32[]{:S(2)}) collective-permute-start(bf16[400,1024]{1,0:T(8,128)(2,1)S(1)} %shard_map.57.refs_3_.refs_1_), channel_id=1, source_target_pairs={{0,4},{8,12},{16,20},{24,28},{1,5},{9,13},{17,21},{25,29},{2,6},{1... | collective-permute-start | bytes 2457608 | tf_op jit(solution)/shard_map/ppermute | solution.py:254
  28.7 13.0 %collective-permute-start.2 = (bf16[200,1024]{1,0:T(8,128)(2,1)S(1)}, bf16[200,1024]{1,0:T(8,128)(2,1)S(1)}, u32[]{:S(2)}, u32[]{:S(2)}) collective-permute-start(bf16[200,1024]{1,0:T(8,128)(2,1)S(1)} %get-tuple-element.37), channel_id=1, source_target_pairs={{0,3},{1,2},{2,1},{3,0},{4,7},{5,6},{6,5},{7,4},{8,11},{9,10},{10,... | collective-permute-start | bytes 1228808 | tf_op jit(solution)/shard_map/ppermute | solution.py:264
  32.7 21.2 %collective-permute-start.9 = (bf16[400,1024]{1,0:T(8,128)(2,1)S(1)}, bf16[400,1024]{1,0:T(8,128)(2,1)S(1)}, u32[]{:S(2)}, u32[]{:S(2)}) collective-permute-start(bf16[400,1024]{1,0:T(8,128)(2,1)S(1)} %shard_map.57.refs_3_.refs_1_), channel_id=1, source_target_pairs={{16,0},{20,4},{24,8},{28,12},{4,16},{0,20},{12,24},{8,28},{17,1},{... | collective-permute-start | bytes 2457608 | tf_op jit(solution)/shard_map/ppermute | solution.py:256
  32.9 21.2 %collective-permute-start.5 = (bf16[400,1024]{1,0:T(8,128)(2,1)S(1)}, bf16[400,1024]{1,0:T(8,128)(2,1)S(1)}, u32[]{:S(2)}, u32[]{:S(2)}) collective-permute-start(bf16[400,1024]{1,0:T(8,128)(2,1)S(1)} %shard_map.57.refs_3_.refs_1_), channel_id=1, source_target_pairs={{8,0},{12,4},{4,8},{0,12},{28,16},{24,20},{16,24},{20,28},{9,1},{1... | collective-permute-start | bytes 2457608 | tf_op jit(solution)/shard_map/ppermute | solution.py:255
  42.1 15.2 %collective-permute-start.11 = (bf16[200,1024]{1,0:T(8,128)(2,1)S(1)}, bf16[200,1024]{1,0:T(8,128)(2,1)S(1)}, u32[]{:S(2)}, u32[]{:S(2)}) collective-permute-start(bf16[200,1024]{1,0:T(8,128)(2,1)S(1)} %shard_map.59.refs_2_), channel_id=1, source_target_pairs={{0,4},{8,12},{16,20},{24,28},{1,5},{9,13},{17,21},{25,29},{2,6},{1... | collective-permute-start | bytes 1228808 | tf_op jit(solution)/shard_map/ppermute | solution.py:254
  43.5 17.2 %collective-permute-start.10 = (bf16[200,1024]{1,0:T(8,128)(2,1)S(1)}, bf16[200,1024]{1,0:T(8,128)(2,1)S(1)}, u32[]{:S(2)}, u32[]{:S(2)}) collective-permute-start(bf16[200,1024]{1,0:T(8,128)(2,1)S(1)} %shard_map.59.refs_2_), channel_id=1, source_target_pairs={{16,0},{20,4},{24,8},{28,12},{4,16},{0,20},{12,24},{8,28},{17,1},{... | collective-permute-start | bytes 1228808 | tf_op jit(solution)/shard_map/ppermute | solution.py:256
  43.5 18.8 %collective-permute-start.8 = (bf16[200,1024]{1,0:T(8,128)(2,1)S(1)}, bf16[200,1024]{1,0:T(8,128)(2,1)S(1)}, u32[]{:S(2)}, u32[]{:S(2)}) collective-permute-start(bf16[200,1024]{1,0:T(8,128)(2,1)S(1)} %shard_map.59.refs_2_), channel_id=1, source_target_pairs={{8,0},{12,4},{4,8},{0,12},{28,16},{24,20},{16,24},{20,28},{9,1},{1... | collective-permute-start | bytes 1228808 | tf_op jit(solution)/shard_map/ppermute | solution.py:255
  65.0 3.1 %collective-permute-start.12 = (f32[4,192]{1,0:T(4,128)S(1)}, f32[4,192]{1,0:T(4,128)S(1)}, u32[]{:S(2)}, u32[]{:S(2)}) collective-permute-start(f32[4,192]{1,0:T(4,128)S(1)} %get-tuple-element.53), channel_id=1, source_target_pairs={{0,8},{4,12},{8,4},{12,0},{16,28},{20,24},{24,16},{28,20},{1,9},{5... | collective-permute-start | bytes 9224 | tf_op jit(solution)/shard_map/ppermute | solution.py:287
  65.1 3.1 %collective-permute-start.13 = (f32[4,192]{1,0:T(4,128)S(1)}, f32[4,192]{1,0:T(4,128)S(1)}, u32[]{:S(2)}, u32[]{:S(2)}) collective-permute-start(f32[4,192]{1,0:T(4,128)S(1)} %get-tuple-element.54), channel_id=1, source_target_pairs={{0,16},{4,20},{8,24},{12,28},{16,4},{20,0},{24,12},{28,8},{1,17},{... | collective-permute-start | bytes 9224 | tf_op jit(solution)/shard_map/ppermute | solution.py:287
  68.2 4.4 %collective-permute-start.14 = (f32[1,192]{1,0:T(1,128)S(1)}, f32[1,192]{1,0:T(1,128)S(1)}, u32[]{:S(2)}, u32[]{:S(2)}) collective-permute-start(f32[1,192]{1,0:T(1,128)S(1)} %get-tuple-element.56), channel_id=1, source_target_pairs={{0,1},{1,0},{2,3},{3,2},{4,5},{5,4},{6,7},{7,6},{8,9},{9,8},{10,11... | collective-permute-start | bytes 2312 | tf_op jit(solution)/shard_map/ppermute | solution.py:289
  69.0 4.5 %collective-permute-start.15 = (f32[1,192]{1,0:T(1,128)S(1)}, f32[1,192]{1,0:T(1,128)S(1)}, u32[]{:S(2)}, u32[]{:S(2)}) collective-permute-start(f32[1,192]{1,0:T(1,128)S(1)} %get-tuple-element.57), channel_id=1, source_target_pairs={{0,2},{1,3},{2,0},{3,1},{4,6},{5,7},{6,4},{7,5},{8,10},{9,11},{10,... | collective-permute-start | bytes 2312 | tf_op jit(solution)/shard_map/ppermute | solution.py:289
  69.4 5.4 %collective-permute-start.16 = (f32[1,192]{1,0:T(1,128)S(1)}, f32[1,192]{1,0:T(1,128)S(1)}, u32[]{:S(2)}, u32[]{:S(2)}) collective-permute-start(f32[1,192]{1,0:T(1,128)S(1)} %get-tuple-element.58), channel_id=1, source_target_pairs={{0,3},{1,2},{2,1},{3,0},{4,7},{5,6},{6,5},{7,4},{8,11},{9,10},{10,... | collective-permute-start | bytes 2312 | tf_op jit(solution)/shard_map/ppermute | solution.py:289

commit v6 on v5

--- a/solution.py
+++ b/solution.py
@@ -117,13 +117,14 @@
             for chunk in chunks if late_chunk in fresh else fresh:
                 scores = dot_last(rows_of(early, chunk), rows_of(late, late_chunk))
                 first, both = sizes(early, chunk)
+                low = jnp.where(late_first, 0, first)
+                high = jnp.where(late_first, first, both)
                 if early == late:
-                    low = jnp.where(late_first, 0, first)
-                    high = jnp.where(late_first, first, both)
                     if chunk == late_chunk:
                         high = jnp.minimum(high, lane)
                     else:
                         high = jnp.where((group_pos ^ chunk) < (group_pos ^ late_chunk), high, 0)
+                if early == late:
                     allowed = (row >= low) & (row < high)
                 else:
                     column = iota((cap, 1), 0)
@@ -153,11 +154,16 @@
         ref[...] = best[s : s + 1, :]
 
 
-def restore_kernel(cap, groups, place_ref, *refs):
+def picks_kernel(cap, groups, place_ref, out_ref):
+    hop, rank = place_ref[0:1, :], place_ref[1:2, :]
+    for s in range(groups):
+        pick = iota((cap, hop.shape[1]), 0) == jnp.where(hop == s, rank, -1)
+        out_ref[s * cap : (s + 1) * cap, :] = pick.astype(jnp.bfloat16)
+
+
+def restore_kernel(cap, groups, picks_ref, *refs):
     parts, out_ref = refs[:groups], refs[groups]
-    rows = place_ref.shape[1]
-    hop, rank = place_ref[0:1, :], place_ref[1:2, :]
-    total = jnp.zeros((16, rows), jnp.float32)
+    total = jnp.zeros((16, picks_ref.shape[1]), jnp.float32)
     for s in range(groups):
         value = parts[s][...]
         high = value.astype(jnp.bfloat16)
@@ -169,7 +175,7 @@
             + [jnp.zeros((13, cap), jnp.float32)],
             axis=0,
         ).astype(jnp.bfloat16)
-        pick = (iota((cap, rows), 0) == jnp.where(hop == s, rank, -1)).astype(jnp.bfloat16)
+        pick = picks_ref[s * cap : (s + 1) * cap, :]
         total = total + jnp.dot(stacked, pick, preferred_element_type=jnp.float32)
     out_ref[...] = total[0:1, :] + (total[1:2, :] + total[2:3, :])
 
@@ -271,6 +277,15 @@
         [x_block[near]],
         [y_block[near]],
     )
+    picks = pl.pallas_call(
+        functools.partial(picks_kernel, cap, groups),
+        out_shape=jax.ShapeDtypeStruct((groups * cap, row_count), jnp.bfloat16),
+        in_specs=vmem_specs(1),
+        out_specs=pl.BlockSpec(memory_space=pltpu.VMEM),
+        compiler_params=params,
+        cost_estimate=COST,
+    )(place)
+    own[near] = after(own[near], picks)
     best = score([], (FAR_PAIRS, (), (near,)), (OWN_PAIRS, (), (near, middle)))
     spread(far, unit_rows(after(at_three, *best)), [sib[middle]], [sib[middle]], [sib[middle]])
     best = score(
@@ -294,7 +309,7 @@
         in_specs=vmem_specs(groups + 1),
         out_specs=pl.BlockSpec(memory_space=pltpu.VMEM),
         compiler_params=params,
-    )(place, *returned)
+    )(picks, *returned)
     return out.reshape(row_count)
 
 

time: 75.8 us -> 75.8 us (level)
  transfers between devices with their start and end apart: 17 -> 17, of which waited for: 11 -> 11; matrix products, arithmetic and copies ran while one was open for 0% -> 0% of each run, Pallas kernels for 10% -> 11%
where the time goes in v6:
time: 75.8 us; the launch traced here: 75.5 us
  waiting for transfers between devices  30.7 us (41%)
  starting transfers between devices  29.1 us (38%)
  Pallas kernels  12.9 us (17%)
  local copies, waits for them, and re-layouts  1.93 us (3%)
    ppermute x1, waiting for transfers between devices, paired_shards(): at_two = lax.ppermute(packed[2], 'group', hops[2])  11.3 us
    ppermute x3, waiting for transfers between devices, spread(): y_block[part] = lax.ppermute(after(unit, *y_after), 'blk', to_y)  9.83 us
    pallas_call x4, Pallas kernels, score_call(): pl.pallas_call(functools.partial(score_kernel, cap, keys, jobs), out_shap...  9.15 us
    ppermute x3, starting transfers between devices, spread(): sib[part] = lax.ppermute(after(unit, *sib_after), 'blk', to_sib)  6.09 us
    ppermute x3, starting transfers between devices, spread(): x_block[part] = lax.ppermute(after(unit, *x_after), 'blk', to_x)  5.69 us
    ppermute x3, starting transfers between devices, paired_shards(): lax.ppermute(returned[s], 'group', hops[s])  4.44 us
    ppermute x1, starting transfers between devices, paired_shards(): at_two = lax.ppermute(packed[2], 'group', hops[2])  4.11 us
    ppermute x1, waiting for transfers between devices, paired_shards(): at_three = lax.ppermute(after(packed[3], at_two), 'group', hops[3])  4.01 us
  transfers between devices with their start and end apart: 17, of which 11 were waited for; matrix products, arithmetic and copies ran while one was open for 0% of the time, Pallas kernels for 11%

profile of v6, /device:TPU:0, one launch (start us, length us, event | category | flops | bytes accessed | tf_op | source)
XLA Modules:
  0.0 75.5 jit_solution(5711052018884403172)
XLA Ops:
  0.0 0.7 reshape.19
  0.7 0.7 copy-done.3
  1.4 1.2 %copy-done = bf16[512,1024]{1,0:T(8,128)(2,1)S(1)} copy-done((bf16[512,1024]{1,0:T(8,128)(2,1)S(1)}, bf16[512,1024]{1,0:T(8,128)(2,1)}, u32[]{:S(2)}) %copy-start) | copy-done | bytes 1048600
  2.6 1.5 %shard_map.55 = (bf16[200,1024]{1,0:T(8,128)(2,1)S(1)}, bf16[200,1024]{1,0:T(8,128)(2,1)S(1)}, bf16[200,1024]{1,0:T(8,128)(2,1)S(1)}, bf16[200,1024]{1,0:T(8,128)(2,1)S(1)}, s32[8,512]{1,0:T(8,128)S(1)}) custom-call(s32[1,512]{1,0:T(1,128)S(1)} %bitcast.5, s32[1,512]{1,0:T(1,128)S(1)} %bitcast.6, f32[1,512]{1,0:T(1,128)S(1)} %bitcast.4, ...), custom_call_target="tpu_custom_call" | custom-call | tf_op jit(solution)/shard_map/pallas_call | solution.py:232
  4.1 4.1 %collective-permute-start = (bf16[200,1024]{1,0:T(8,128)(2,1)S(1)}, bf16[200,1024]{1,0:T(8,128)(2,1)S(1)}, u32[]{:S(2)}, u32[]{:S(2)}) collective-permute-start(bf16[200,1024]{1,0:T(8,128)(2,1)S(1)} %get-tuple-element.36), channel_id=1, source_target_pairs={{0,2},{1,3},{2,0},{3,1},{4,6},{5,7},{6,4},{7,5},{8,10},{9,11},{10,... | collective-permute-start | bytes 1228808 | tf_op jit(solution)/shard_map/ppermute | solution.py:268
  8.2 1.6 %collective-permute-start.1 = (bf16[200,1024]{1,0:T(8,128)(2,1)S(1)}, bf16[200,1024]{1,0:T(8,128)(2,1)S(1)}, u32[]{:S(2)}, u32[]{:S(2)}) collective-permute-start(bf16[200,1024]{1,0:T(8,128)(2,1)S(1)} %get-tuple-element.37), channel_id=1, source_target_pairs={{0,1},{1,0},{2,3},{3,2},{4,5},{5,4},{6,7},{7,6},{8,9},{9,8},{10,11... | collective-permute-start | bytes 1228808 | tf_op jit(solution)/shard_map/ppermute | solution.py:269
  9.8 0.3 shard_map.57.refs_0_
  10.2 0.4 collective-permute-start.3
  10.6 1.2 %collective-permute-start.4 = (bf16[200,1024]{1,0:T(8,128)(2,1)S(1)}, bf16[200,1024]{1,0:T(8,128)(2,1)S(1)}, u32[]{:S(2)}, u32[]{:S(2)}) collective-permute-start(bf16[200,1024]{1,0:T(8,128)(2,1)S(1)} %shard_map.57.refs_0_), channel_id=1, source_target_pairs={{16,0},{20,4},{24,8},{28,12},{4,16},{0,20},{12,24},{8,28},{17,1},{... | collective-permute-start | bytes 1228808 | tf_op jit(solution)/shard_map/ppermute | solution.py:262
  11.8 3.4 %collective-permute-start.6 = (bf16[200,1024]{1,0:T(8,128)(2,1)S(1)}, bf16[200,1024]{1,0:T(8,128)(2,1)S(1)}, u32[]{:S(2)}, u32[]{:S(2)}) collective-permute-start(bf16[200,1024]{1,0:T(8,128)(2,1)S(1)} %shard_map.57.refs_0_), channel_id=1, source_target_pairs={{0,4},{8,12},{16,20},{24,28},{1,5},{9,13},{17,21},{25,29},{2,6},{1... | collective-permute-start | bytes 1228808 | tf_op jit(solution)/shard_map/ppermute | solution.py:260
  15.3 11.3 %collective-permute-done.refs_0_ = bf16[200,1024]{1,0:T(8,128)(2,1)S(1)} collective-permute-done((bf16[200,1024]{1,0:T(8,128)(2,1)S(1)}, bf16[200,1024]{1,0:T(8,128)(2,1)S(1)}, u32[]{:S(2)}, u32[]{:S(2)}) %collective-permute-start) | collective-permute-done | bytes 409632 | tf_op jit(solution)/shard_map/ppermute | solution.py:268
  26.7 0.6 shard_map.58.refs_3_.refs_1_
  27.4 1.3 %collective-permute-start.7 = (bf16[400,1024]{1,0:T(8,128)(2,1)S(1)}, bf16[400,1024]{1,0:T(8,128)(2,1)S(1)}, u32[]{:S(2)}, u32[]{:S(2)}) collective-permute-start(bf16[400,1024]{1,0:T(8,128)(2,1)S(1)} %shard_map.58.refs_3_.refs_1_), channel_id=1, source_target_pairs={{0,4},{8,12},{16,20},{24,28},{1,5},{9,13},{17,21},{25,29},{2,6},{1... | collective-permute-start | bytes 2457608 | tf_op jit(solution)/shard_map/ppermute | solution.py:260
  28.7 4.0 %collective-permute-start.2 = (bf16[200,1024]{1,0:T(8,128)(2,1)S(1)}, bf16[200,1024]{1,0:T(8,128)(2,1)S(1)}, u32[]{:S(2)}, u32[]{:S(2)}) collective-permute-start(bf16[200,1024]{1,0:T(8,128)(2,1)S(1)} %get-tuple-element.39), channel_id=1, source_target_pairs={{0,3},{1,2},{2,1},{3,0},{4,7},{5,6},{6,5},{7,4},{8,11},{9,10},{10,... | collective-permute-start | bytes 1228808 | tf_op jit(solution)/shard_map/ppermute | solution.py:270
  32.9 2.5 %collective-permute-start.5 = (bf16[400,1024]{1,0:T(8,128)(2,1)S(1)}, bf16[400,1024]{1,0:T(8,128)(2,1)S(1)}, u32[]{:S(2)}, u32[]{:S(2)}) collective-permute-start(bf16[400,1024]{1,0:T(8,128)(2,1)S(1)} %shard_map.58.refs_3_.refs_1_), channel_id=1, source_target_pairs={{8,0},{12,4},{4,8},{0,12},{28,16},{24,20},{16,24},{20,28},{9,1},{1... | collective-permute-start | bytes 2457608 | tf_op jit(solution)/shard_map/ppermute | solution.py:261
  35.6 2.2 %shard_map.59 = (f32[4,192]{1,0:T(4,128)S(1)}, f32[4,192]{1,0:T(4,128)S(1)}, f32[4,192]{1,0:T(4,128)S(1)}) custom-call(bf16[200,1024]{1,0:T(8,128)(2,1)S(1)} %shard_map.57.refs_0_, bf16[200,1024]{1,0:T(8,128)(2,1)S(1)} %collective-permute-done.3.refs_1_.refs_2_.refs_3_, bf16[200,1024]{1,0:T(8,128)(2,1)S(1)} %collective-permute-done.4.refs_2_.refs_4_.refs_6_, ...), custom_call_target="tpu_custom_call" | custom-call | flops 1 | bytes 1 | tf_op jit(solution)/shard_map/pallas_call | solution.py:213
  37.8 4.0 %collective-permute-done.2.refs_0_ = bf16[200,1024]{1,0:T(8,128)(2,1)S(1)} collective-permute-done((bf16[200,1024]{1,0:T(8,128)(2,1)S(1)}, bf16[200,1024]{1,0:T(8,128)(2,1)S(1)}, u32[]{:S(2)}, u32[]{:S(2)}) %collective-permute-start.2) | collective-permute-done | bytes 409632 | tf_op jit(solution)/shard_map/ppermute | solution.py:270
  42.1 1.3 %collective-permute-start.11 = (bf16[200,1024]{1,0:T(8,128)(2,1)S(1)}, bf16[200,1024]{1,0:T(8,128)(2,1)S(1)}, u32[]{:S(2)}, u32[]{:S(2)}) collective-permute-start(bf16[200,1024]{1,0:T(8,128)(2,1)S(1)} %shard_map.60.refs_2_), channel_id=1, source_target_pairs={{0,4},{8,12},{16,20},{24,28},{1,5},{9,13},{17,21},{25,29},{2,6},{1... | collective-permute-start | bytes 1228808 | tf_op jit(solution)/shard_map/ppermute | solution.py:260
  43.5 2.7 %collective-permute-start.8 = (bf16[200,1024]{1,0:T(8,128)(2,1)S(1)}, bf16[200,1024]{1,0:T(8,128)(2,1)S(1)}, u32[]{:S(2)}, u32[]{:S(2)}) collective-permute-start(bf16[200,1024]{1,0:T(8,128)(2,1)S(1)} %shard_map.60.refs_2_), channel_id=1, source_target_pairs={{8,0},{12,4},{4,8},{0,12},{28,16},{24,20},{16,24},{20,28},{9,1},{1... | collective-permute-start | bytes 1228808 | tf_op jit(solution)/shard_map/ppermute | solution.py:261
  46.2 7.6 %collective-permute-done.9.refs_5_.refs_7_ = bf16[400,1024]{1,0:T(8,128)(2,1)S(1)} collective-permute-done((bf16[400,1024]{1,0:T(8,128)(2,1)S(1)}, bf16[400,1024]{1,0:T(8,128)(2,1)S(1)}, u32[]{:S(2)}, u32[]{:S(2)}) %collective-permute-start.9) | collective-permute-done | bytes 819232 | tf_op jit(solution)/shard_map/ppermute | solution.py:262
  54.1 3.2 %shard_map.61 = (f32[4,192]{1,0:T(4,128)S(1)}, f32[4,192]{1,0:T(4,128)S(1)}, f32[4,192]{1,0:T(4,128)S(1)}) custom-call(bf16[200,1024]{1,0:T(8,128)(2,1)S(1)} %shard_map.57.refs_0_, bf16[400,1024]{1,0:T(8,128)(2,1)S(1)} %shard_map.58.refs_3_.refs_1_, bf16[200,1024]{1,0:T(8,128)(2,1)S(1)} %collective-permute-done.3.refs_1_.refs_2_.refs_3_, ...), custom_call_target="tpu_custom_call" | custom-call | flops 1 | bytes 1 | tf_op jit(solution)/shard_map/pallas_call | solution.py:213
  57.3 1.2 %shard_map.62 = (f32[4,192]{1,0:T(4,128)S(1)}, f32[4,192]{1,0:T(4,128)S(1)}, f32[4,192]{1,0:T(4,128)S(1)}) custom-call(bf16[200,1024]{1,0:T(8,128)(2,1)S(1)} %shard_map.57.refs_0_, bf16[400,1024]{1,0:T(8,128)(2,1)S(1)} %shard_map.58.refs_3_.refs_1_, bf16[200,1024]{1,0:T(8,128)(2,1)S(1)} %shard_map.60.refs_2_, ...), custom_call_target="tpu_custom_call" | custom-call | flops 1 | bytes 1 | tf_op jit(solution)/shard_map/pallas_call | solution.py:213
  58.5 2.2 %collective-permute-done.10.refs_8_ = bf16[200,1024]{1,0:T(8,128)(2,1)S(1)} collective-permute-done((bf16[200,1024]{1,0:T(8,128)(2,1)S(1)}, bf16[200,1024]{1,0:T(8,128)(2,1)S(1)}, u32[]{:S(2)}, u32[]{:S(2)}) %collective-permute-start.10) | collective-permute-done | bytes 409632 | tf_op jit(solution)/shard_map/ppermute | solution.py:262
  60.7 1.7 %collective-permute-done.8.refs_5_ = bf16[200,1024]{1,0:T(8,128)(2,1)S(1)} collective-permute-done((bf16[200,1024]{1,0:T(8,128)(2,1)S(1)}, bf16[200,1024]{1,0:T(8,128)(2,1)S(1)}, u32[]{:S(2)}, u32[]{:S(2)}) %collective-permute-start.8) | collective-permute-done | bytes 409632 | tf_op jit(solution)/shard_map/ppermute | solution.py:261
  62.4 2.6 %shard_map.63 = (f32[4,192]{1,0:T(4,128)S(1)}, f32[4,192]{1,0:T(4,128)S(1)}, f32[4,192]{1,0:T(4,128)S(1)}) custom-call(bf16[200,1024]{1,0:T(8,128)(2,1)S(1)} %shard_map.57.refs_0_, bf16[400,1024]{1,0:T(8,128)(2,1)S(1)} %shard_map.58.refs_3_.refs_1_, bf16[200,1024]{1,0:T(8,128)(2,1)S(1)} %shard_map.60.refs_2_, ...), custom_call_target="tpu_custom_call" | custom-call | flops 1 | bytes 1 | tf_op jit(solution)/shard_map/pallas_call | solution.py:213
  65.1 1.7 %collective-permute-start.13 = (f32[4,192]{1,0:T(4,128)S(1)}, f32[4,192]{1,0:T(4,128)S(1)}, u32[]{:S(2)}, u32[]{:S(2)}) collective-permute-start(f32[4,192]{1,0:T(4,128)S(1)} %get-tuple-element.56), channel_id=1, source_target_pairs={{0,16},{4,20},{8,24},{12,28},{16,4},{20,0},{24,12},{28,8},{1,17},{... | collective-permute-start | bytes 9224 | tf_op jit(solution)/shard_map/ppermute | solution.py:302
  66.8 1.3 %collective-permute-done.12.x_ref = f32[4,192]{1,0:T(4,128)S(1)} collective-permute-done((f32[4,192]{1,0:T(4,128)S(1)}, f32[4,192]{1,0:T(4,128)S(1)}, u32[]{:S(2)}, u32[]{:S(2)}) %collective-permute-start.12) | collective-permute-done | bytes 3104 | tf_op jit(solution)/shard_map/ppermute | solution.py:302
  68.2 0.8 %collective-permute-start.14 = (f32[1,192]{1,0:T(1,128)S(1)}, f32[1,192]{1,0:T(1,128)S(1)}, u32[]{:S(2)}, u32[]{:S(2)}) collective-permute-start(f32[1,192]{1,0:T(1,128)S(1)} %get-tuple-element.58), channel_id=1, source_target_pairs={{0,1},{1,0},{2,3},{3,2},{4,5},{5,4},{6,7},{7,6},{8,9},{9,8},{10,11... | collective-permute-start | bytes 2312 | tf_op jit(solution)/shard_map/ppermute | solution.py:304
  69.4 3.3 %collective-permute-start.16 = (f32[1,192]{1,0:T(1,128)S(1)}, f32[1,192]{1,0:T(1,128)S(1)}, u32[]{:S(2)}, u32[]{:S(2)}) collective-permute-start(f32[1,192]{1,0:T(1,128)S(1)} %get-tuple-element.60), channel_id=1, source_target_pairs={{0,3},{1,2},{2,1},{3,0},{4,7},{5,6},{6,5},{7,4},{8,11},{9,10},{10,... | collective-permute-start | bytes 2312 | tf_op jit(solution)/shard_map/ppermute | solution.py:304
  72.6 0.8 %collective-permute-done.15.refs_2_ = f32[1,192]{1,0:T(1,128)S(1)} collective-permute-done((f32[1,192]{1,0:T(1,128)S(1)}, f32[1,192]{1,0:T(1,128)S(1)}, u32[]{:S(2)}, u32[]{:S(2)}) %collective-permute-start.15) | collective-permute-done | bytes 800 | tf_op jit(solution)/shard_map/ppermute | solution.py:304
  73.5 1.2 %collective-permute-done.16.refs_3_ = f32[1,192]{1,0:T(1,128)S(1)} collective-permute-done((f32[1,192]{1,0:T(1,128)S(1)}, f32[1,192]{1,0:T(1,128)S(1)}, u32[]{:S(2)}, u32[]{:S(2)}) %collective-permute-start.16) | collective-permute-done | bytes 800 | tf_op jit(solution)/shard_map/ppermute | solution.py:304
  74.7 0.8 %shard_map.65 = f32[1,512]{1,0:T(1,128)} custom-call(bf16[768,512]{1,0:T(8,128)(2,1)S(1)} %shard_map.56.picks_ref, f32[1,192]{1,0:T(1,128)S(1)} %get-tuple-element.57.refs_0_, f32[1,192]{1,0:T(1,128)S(1)} %collective-permute-done.14.refs_1_, f32[1,192]{1,0:T(1,128)S(1)} %collective-permute-done.15.refs_2_, f32[1,192]{1,0:T(1,128)S(1)} %collective-permute-done.16.refs_3_), custom_call_target="tpu_custom_call" | custom-call | tf_op jit(solution)/shard_map/pallas_call | solution.py:306
  (22 shorter events, 1.7 us)
Async XLA Ops:
  0.7 0.7 copy-start.3
  0.7 0.7 copy-start.2
  1.4 1.2 %copy-start = (bf16[512,1024]{1,0:T(8,128)(2,1)S(1)}, bf16[512,1024]{1,0:T(8,128)(2,1)}, u32[]{:S(2)}) copy-start(bf16[512,1024]{1,0:T(8,128)(2,1)} %codes_ref.1) | copy-start | bytes 3145732
  4.1 5.7 %copy-start.1 = (bf16[2,1024]{1,0:T(2,128)(2,1)S(1)}, bf16[2,1024]{1,0:T(2,128)(2,1)}, u32[]{:S(2)}) copy-start(bf16[2,1024]{1,0:T(2,128)(2,1)} %refs_1_.3) | copy-start | bytes 12292
  4.1 22.5 %collective-permute-start = (bf16[200,1024]{1,0:T(8,128)(2,1)S(1)}, bf16[200,1024]{1,0:T(8,128)(2,1)S(1)}, u32[]{:S(2)}, u32[]{:S(2)}) collective-permute-start(bf16[200,1024]{1,0:T(8,128)(2,1)S(1)} %get-tuple-element.36), channel_id=1, source_target_pairs={{0,2},{1,3},{2,0},{3,1},{4,6},{5,7},{6,4},{7,5},{8,10},{9,11},{10,... | collective-permute-start | bytes 1228808 | tf_op jit(solution)/shard_map/ppermute | solution.py:268
  8.2 18.5 %collective-permute-start.1 = (bf16[200,1024]{1,0:T(8,128)(2,1)S(1)}, bf16[200,1024]{1,0:T(8,128)(2,1)S(1)}, u32[]{:S(2)}, u32[]{:S(2)}) collective-permute-start(bf16[200,1024]{1,0:T(8,128)(2,1)S(1)} %get-tuple-element.37), channel_id=1, source_target_pairs={{0,1},{1,0},{2,3},{3,2},{4,5},{5,4},{6,7},{7,6},{8,9},{9,8},{10,11... | collective-permute-start | bytes 1228808 | tf_op jit(solution)/shard_map/ppermute | solution.py:269
  10.2 17.2 %collective-permute-start.3 = (bf16[200,1024]{1,0:T(8,128)(2,1)S(1)}, bf16[200,1024]{1,0:T(8,128)(2,1)S(1)}, u32[]{:S(2)}, u32[]{:S(2)}) collective-permute-start(bf16[200,1024]{1,0:T(8,128)(2,1)S(1)} %shard_map.57.refs_0_), channel_id=1, source_target_pairs={{8,0},{12,4},{4,8},{0,12},{28,16},{24,20},{16,24},{20,28},{9,1},{1... | collective-permute-start | bytes 1228808 | tf_op jit(solution)/shard_map/ppermute | solution.py:261
  10.6 16.8 %collective-permute-start.4 = (bf16[200,1024]{1,0:T(8,128)(2,1)S(1)}, bf16[200,1024]{1,0:T(8,128)(2,1)S(1)}, u32[]{:S(2)}, u32[]{:S(2)}) collective-permute-start(bf16[200,1024]{1,0:T(8,128)(2,1)S(1)} %shard_map.57.refs_0_), channel_id=1, source_target_pairs={{16,0},{20,4},{24,8},{28,12},{4,16},{0,20},{12,24},{8,28},{17,1},{... | collective-permute-start | bytes 1228808 | tf_op jit(solution)/shard_map/ppermute | solution.py:262
  11.8 15.6 %collective-permute-start.6 = (bf16[200,1024]{1,0:T(8,128)(2,1)S(1)}, bf16[200,1024]{1,0:T(8,128)(2,1)S(1)}, u32[]{:S(2)}, u32[]{:S(2)}) collective-permute-start(bf16[200,1024]{1,0:T(8,128)(2,1)S(1)} %shard_map.57.refs_0_), channel_id=1, source_target_pairs={{0,4},{8,12},{16,20},{24,28},{1,5},{9,13},{17,21},{25,29},{2,6},{1... | collective-permute-start | bytes 1228808 | tf_op jit(solution)/shard_map/ppermute | solution.py:260
  27.4 14.7 %collective-permute-start.7 = (bf16[400,1024]{1,0:T(8,128)(2,1)S(1)}, bf16[400,1024]{1,0:T(8,128)(2,1)S(1)}, u32[]{:S(2)}, u32[]{:S(2)}) collective-permute-start(bf16[400,1024]{1,0:T(8,128)(2,1)S(1)} %shard_map.58.refs_3_.refs_1_), channel_id=1, source_target_pairs={{0,4},{8,12},{16,20},{24,28},{1,5},{9,13},{17,21},{25,29},{2,6},{1... | collective-permute-start | bytes 2457608 | tf_op jit(solution)/shard_map/ppermute | solution.py:260
  28.7 13.0 %collective-permute-start.2 = (bf16[200,1024]{1,0:T(8,128)(2,1)S(1)}, bf16[200,1024]{1,0:T(8,128)(2,1)S(1)}, u32[]{:S(2)}, u32[]{:S(2)}) collective-permute-start(bf16[200,1024]{1,0:T(8,128)(2,1)S(1)} %get-tuple-element.39), channel_id=1, source_target_pairs={{0,3},{1,2},{2,1},{3,0},{4,7},{5,6},{6,5},{7,4},{8,11},{9,10},{10,... | collective-permute-start | bytes 1228808 | tf_op jit(solution)/shard_map/ppermute | solution.py:270
  32.7 21.2 %collective-permute-start.9 = (bf16[400,1024]{1,0:T(8,128)(2,1)S(1)}, bf16[400,1024]{1,0:T(8,128)(2,1)S(1)}, u32[]{:S(2)}, u32[]{:S(2)}) collective-permute-start(bf16[400,1024]{1,0:T(8,128)(2,1)S(1)} %shard_map.58.refs_3_.refs_1_), channel_id=1, source_target_pairs={{16,0},{20,4},{24,8},{28,12},{4,16},{0,20},{12,24},{8,28},{17,1},{... | collective-permute-start | bytes 2457608 | tf_op jit(solution)/shard_map/ppermute | solution.py:262
  32.9 21.2 %collective-permute-start.5 = (bf16[400,1024]{1,0:T(8,128)(2,1)S(1)}, bf16[400,1024]{1,0:T(8,128)(2,1)S(1)}, u32[]{:S(2)}, u32[]{:S(2)}) collective-permute-start(bf16[400,1024]{1,0:T(8,128)(2,1)S(1)} %shard_map.58.refs_3_.refs_1_), channel_id=1, source_target_pairs={{8,0},{12,4},{4,8},{0,12},{28,16},{24,20},{16,24},{20,28},{9,1},{1... | collective-permute-start | bytes 2457608 | tf_op jit(solution)/shard_map/ppermute | solution.py:261
  42.1 15.2 %collective-permute-start.11 = (bf16[200,1024]{1,0:T(8,128)(2,1)S(1)}, bf16[200,1024]{1,0:T(8,128)(2,1)S(1)}, u32[]{:S(2)}, u32[]{:S(2)}) collective-permute-start(bf16[200,1024]{1,0:T(8,128)(2,1)S(1)} %shard_map.60.refs_2_), channel_id=1, source_target_pairs={{0,4},{8,12},{16,20},{24,28},{1,5},{9,13},{17,21},{25,29},{2,6},{1... | collective-permute-start | bytes 1228808 | tf_op jit(solution)/shard_map/ppermute | solution.py:260
  43.5 17.2 %collective-permute-start.10 = (bf16[200,1024]{1,0:T(8,128)(2,1)S(1)}, bf16[200,1024]{1,0:T(8,128)(2,1)S(1)}, u32[]{:S(2)}, u32[]{:S(2)}) collective-permute-start(bf16[200,1024]{1,0:T(8,128)(2,1)S(1)} %shard_map.60.refs_2_), channel_id=1, source_target_pairs={{16,0},{20,4},{24,8},{28,12},{4,16},{0,20},{12,24},{8,28},{17,1},{... | collective-permute-start | bytes 1228808 | tf_op jit(solution)/shard_map/ppermute | solution.py:262
  43.5 18.8 %collective-permute-start.8 = (bf16[200,1024]{1,0:T(8,128)(2,1)S(1)}, bf16[200,1024]{1,0:T(8,128)(2,1)S(1)}, u32[]{:S(2)}, u32[]{:S(2)}) collective-permute-start(bf16[200,1024]{1,0:T(8,128)(2,1)S(1)} %shard_map.60.refs_2_), channel_id=1, source_target_pairs={{8,0},{12,4},{4,8},{0,12},{28,16},{24,20},{16,24},{20,28},{9,1},{1... | collective-permute-start | bytes 1228808 | tf_op jit(solution)/shard_map/ppermute | solution.py:261
  65.0 3.1 %collective-permute-start.12 = (f32[4,192]{1,0:T(4,128)S(1)}, f32[4,192]{1,0:T(4,128)S(1)}, u32[]{:S(2)}, u32[]{:S(2)}) collective-permute-start(f32[4,192]{1,0:T(4,128)S(1)} %get-tuple-element.55), channel_id=1, source_target_pairs={{0,8},{4,12},{8,4},{12,0},{16,28},{20,24},{24,16},{28,20},{1,9},{5... | collective-permute-start | bytes 9224 | tf_op jit(solution)/shard_map/ppermute | solution.py:302
  65.1 3.1 %collective-permute-start.13 = (f32[4,192]{1,0:T(4,128)S(1)}, f32[4,192]{1,0:T(4,128)S(1)}, u32[]{:S(2)}, u32[]{:S(2)}) collective-permute-start(f32[4,192]{1,0:T(4,128)S(1)} %get-tuple-element.56), channel_id=1, source_target_pairs={{0,16},{4,20},{8,24},{12,28},{16,4},{20,0},{24,12},{28,8},{1,17},{... | collective-permute-start | bytes 9224 | tf_op jit(solution)/shard_map/ppermute | solution.py:302
  68.2 4.4 %collective-permute-start.14 = (f32[1,192]{1,0:T(1,128)S(1)}, f32[1,192]{1,0:T(1,128)S(1)}, u32[]{:S(2)}, u32[]{:S(2)}) collective-permute-start(f32[1,192]{1,0:T(1,128)S(1)} %get-tuple-element.58), channel_id=1, source_target_pairs={{0,1},{1,0},{2,3},{3,2},{4,5},{5,4},{6,7},{7,6},{8,9},{9,8},{10,11... | collective-permute-start | bytes 2312 | tf_op jit(solution)/shard_map/ppermute | solution.py:304
  69.0 4.5 %collective-permute-start.15 = (f32[1,192]{1,0:T(1,128)S(1)}, f32[1,192]{1,0:T(1,128)S(1)}, u32[]{:S(2)}, u32[]{:S(2)}) collective-permute-start(f32[1,192]{1,0:T(1,128)S(1)} %get-tuple-element.59), channel_id=1, source_target_pairs={{0,2},{1,3},{2,0},{3,1},{4,6},{5,7},{6,4},{7,5},{8,10},{9,11},{10,... | collective-permute-start | bytes 2312 | tf_op jit(solution)/shard_map/ppermute | solution.py:304
  69.4 5.4 %collective-permute-start.16 = (f32[1,192]{1,0:T(1,128)S(1)}, f32[1,192]{1,0:T(1,128)S(1)}, u32[]{:S(2)}, u32[]{:S(2)}) collective-permute-start(f32[1,192]{1,0:T(1,128)S(1)} %get-tuple-element.60), channel_id=1, source_target_pairs={{0,3},{1,2},{2,1},{3,0},{4,7},{5,6},{6,5},{7,4},{8,11},{9,10},{10,... | collective-permute-start | bytes 2312 | tf_op jit(solution)/shard_map/ppermute | solution.py:304
